TPU v7x, 32 devices: a whole 2x2x4 slice. The times are simulated.
32 devices in a mesh: frame: 8 (over z, x), head: 4 (over y, core).
Axes of the slice: x: 2, y: 2, z: 4, core: 2. Of those that a mesh axis runs over, the one named last changes fastest.
Arguments:
- queries: bfloat16 [2048, 5120], P('frame', 'head'), may hold values from -20 to 20
- key_vectors: bfloat16 [2048, 5120], P('frame', 'head'), may hold values from -20 to 20
- value_vectors: bfloat16 [2048, 5120], P('frame', 'head'), may hold values from -6 to 6
- live_blocks: int32 [32, 32], P('frame'), may hold values from 0 to 1, as said below
- out_weight: bfloat16 [5120, 5120], P('head'), may hold values from -0.078125 to 0.078125
Outputs:
- mixed: bfloat16 [2048, 5120], P('frame', 'head')
Inputs may be any that keep to these rules, and one draw needn't show every extreme that they name: live_blocks is 1 wherever the distance |i - j| between the frames i, j of the query block and the key block is 0 or 1, and 0 wherever that distance is not 0, 1 or a power of two up to 4.
All inputs are finite; a program needn't handle non-finite values.
Results may differ from a plain program's by a relative error of at most 0.015.
Values may be sent and summed in bfloat16 or wider, within the bound.
No kernel may reach another device: no remote copies, remote signals or barrier semaphores. Data moves between devices by JAX's collectives and lax.ppermute only.
A program may use at most 192 MiB of HBM per device.

v0:
```python
import jax
import jax.numpy as jnp
from jax import lax
from jax.sharding import PartitionSpec as P

HDIM = 128
BLK = 64


def offsets_for(frames):
    result = [0]
    step = 1
    while step <= frames // 2:
        result.append(step)
        result.append(-step)
        step = step * 2
    return result


def on_device(queries, key_vectors, value_vectors, live_blocks, out_weight):
    frames = lax.axis_size("frame")
    own_index = lax.axis_index("frame")
    offsets = offsets_for(frames)
    frame_rows = queries.shape[0]
    blocks = frame_rows // BLK
    local_heads = queries.shape[1] // HDIM
    scale = 1.0 / HDIM**0.5
    pieces = []
    every_key, every_value = (
        lax.all_gather(key_vectors, "frame", axis=0, tiled=True),
        lax.all_gather(value_vectors, "frame", axis=0, tiled=True),
    )
    for offset in offsets:
        other = jnp.clip(own_index + offset, 0, frames - 1)
        pieces.append(
            (
                lax.dynamic_slice_in_dim(every_key, other * frame_rows, frame_rows, 0),
                lax.dynamic_slice_in_dim(every_value, other * frame_rows, frame_rows, 0),
            )
        )
    mask_list = []
    for offset in offsets:
        target = own_index + offset
        inside = (target >= 0) & (target < frames)
        other = jnp.clip(target, 0, frames - 1)
        square = lax.dynamic_slice_in_dim(live_blocks, other * blocks, blocks, 1)
        square = jnp.where(inside, square, 0)
        mask_list.append(jnp.repeat(jnp.repeat(square, BLK, 0), BLK, 1))
    mask_all = jnp.concatenate(mask_list, 1)
    key_all = jnp.concatenate([piece[0] for piece in pieces], 0).reshape(-1, local_heads, HDIM)
    value_all = jnp.concatenate([piece[1] for piece in pieces], 0).reshape(-1, local_heads, HDIM)
    query_now = queries.reshape(frame_rows, local_heads, HDIM)
    scores = (
        jnp.einsum("qhd,khd->hqk", query_now, key_all, preferred_element_type=jnp.float32) * scale
    )
    scores = jnp.where(mask_all[None] > 0, scores, -jnp.inf)
    peak = jnp.max(scores, axis=2, keepdims=True)
    expo = jnp.exp(scores - peak)
    total = jnp.sum(expo, axis=2, keepdims=True)
    weights = (expo / total).astype(jnp.bfloat16)
    attended = jnp.einsum("hqk,khd->qhd", weights, value_all, preferred_element_type=jnp.float32)
    attended = attended.astype(jnp.bfloat16).reshape(frame_rows, local_heads * HDIM)
    partial_value = jnp.dot(attended, out_weight, preferred_element_type=jnp.float32)
    return lax.psum_scatter(
        partial_value.astype(jnp.bfloat16), "head", scatter_dimension=1, tiled=True
    )


def solution(mesh):
    placed = (
        P("frame", "head"),
        P("frame", "head"),
        P("frame", "head"),
        P("frame", None),
        P("head", None),
    )
    return jax.shard_map(
        on_device, mesh=mesh, in_specs=placed, out_specs=P("frame", "head"), check_vma=False
    )
```

profile of v0, /device:TPU:10, one launch (start us, length us, event | category | flops | bytes accessed | tf_op | source)
XLA Modules:
  0.0 268.7 jit_solution(15751202515975635530)
XLA Ops:
  7.3 2.2 copy.24
  9.6 1.0 fusion.13
  12.4 1.3 copy.25
  14.3 80.7 %all-gather.3.cloned.1.call-done = bf16[2048,1280]{1,0:T(8,128)(2,1)} async-done(((bf16[256,1280]{1,0:T(8,128)(2,1)}), bf16[2048,1280]{1,0:T(8,128)(2,1)}) %all-gather.3.cloned.1.call-update) | async-done | bytes 5242896 | tf_op jit(solution)/shard_map/all_gather | solution.py:31
  95.0 2.0 dynamic-slice_dynamic-update-slice_fusion.13
  97.0 2.0 dynamic-slice_dynamic-update-slice_fusion.12
  98.9 2.0 dynamic-slice_dynamic-update-slice_fusion.11
  100.9 2.0 dynamic-slice_dynamic-update-slice_fusion.10
  102.9 2.0 dynamic-slice_dynamic-update-slice_fusion.9
  104.9 2.1 dynamic-slice_dynamic-update-slice_fusion.8
  107.0 2.0 dynamic-slice_dynamic-update-slice_fusion.7
  109.0 7.2 %copy.16 = bf16[1792,1280]{0,1:T(8,128)(2,1)} copy(bf16[1792,1280]{1,0:T(8,128)(2,1)} %dynamic-slice_dynamic-update-slice_fusion.7) | data formatting | bytes 9175040 | tf_op jit(solution)/shard_map/concatenate | solution.py:51
  116.2 65.4 %all-gather.5.cloned.1.call-done = bf16[2048,1280]{0,1:T(8,128)(2,1)} async-done(((bf16[256,1280]{0,1:T(8,128)(2,1)}), bf16[2048,1280]{0,1:T(8,128)(2,1)}) %all-gather.5.cloned.1.call-update) | async-done | bytes 5242896 | tf_op jit(solution)/shard_map/all_gather | solution.py:30
  181.6 2.0 dynamic-slice_dynamic-update-slice_fusion.6
  183.6 2.0 dynamic-slice_dynamic-update-slice_fusion.5
  185.6 2.1 dynamic-slice_dynamic-update-slice_fusion.4
  187.7 2.1 dynamic-slice_dynamic-update-slice_fusion.3
  189.8 2.0 dynamic-slice_dynamic-update-slice_fusion.2
  191.8 2.0 dynamic-slice_dynamic-update-slice_fusion.1
  193.8 2.1 dynamic-slice_dynamic-update-slice_fusion
  195.9 11.6 %fusion.18 = (f32[10,256]{1,0:T(8,128)S(1)}, f32[10,256,1792]{1,2,0:T(8,128)}) fusion(pred[256,1792]{0,1:T(8,128)(4,1)S(1)} %broadcast_compare_fusion, bf16[1792,10,128]{0,2,1:T(8,128)(2,1)} %bitcast.8, bf16[256,10,128]{0,2,1:T(8,128)(2,1)S(1)} %bitcast.54), kind=kOutput, calls=%fused_computation.50 | convolution fusion | flops 1192756992 | bytes 24061952 | tf_op jit(solution)/shard_map/sub | solution.py:58
  207.5 9.1 %fusion.6 = bf16[10,128,256]{2,1,0:T(8,128)(2,1)S(1)} fusion(bf16[1792,10,128]{0,2,1:T(8,128)(2,1)} %bitcast.45, f32[10,256,1792]{1,2,0:T(8,128)} %get-tuple-element.13, f32[10,256]{1,0:T(8,128)S(1)} %get-tuple-element.12), kind=kOutput, calls=%fused_computation.10 | convolution fusion | flops 1183907840 | bytes 23603200 | tf_op jit(solution)/shard_map/hqk,khd->qhd/dot_general | solution.py:61
  216.6 9.7 %convolution_convert_fusion = bf16[256,5120]{1,0:T(8,128)(2,1)} fusion(bf16[256,1280]{0,1:T(8,128)(2,1)S(1)} %bitcast.53, bf16[1280,5120]{1,0:T(8,128)(2,1)} %param.9), kind=kOutput, calls=%fused_computation.9 | convolution fusion | flops 3356753920 | bytes 16384000 | tf_op jit(solution)/shard_map/dot_general | solution.py:63
  226.3 35.9 %reduce-scatter.2.cloned.1.call-done = bf16[256,1280]{1,0:T(8,128)(2,1)} async-done(((bf16[256,5120]{1,0:T(8,128)(2,1)}), bf16[256,1280]{1,0:T(8,128)(2,1)}) %reduce-scatter.2.cloned.1.call-update) | async-done | bytes 655376 | tf_op jit(solution)/shard_map/reduce_scatter | solution.py:64
  (42 shorter events, 3.1 us)
Async XLA Ops:
  6.5 88.5 %all-gather.3.cloned.1.call-start = ((), (), s32[]{:S(2)}) async-start(), calls=%async_computation.1 | async-start | bytes 5898240 | tf_op jit(solution)/shard_map/all_gather | solution.py:31
  7.3 174.4 %all-gather.5.cloned.1.call-start = ((), (), s32[]{:S(2)}) async-start(), calls=%async_computation.2 | async-start | bytes 5898240 | tf_op jit(solution)/shard_map/all_gather | solution.py:30
  9.5 252.7 %reduce-scatter.2.cloned.1.call-start = ((), (), s32[]{:S(2)}) async-start(), calls=%async_computation.3 | async-start | bytes 3276800 | tf_op jit(solution)/shard_map/reduce_scatter | solution.py:64
Sparse Core Ops, SparseCore 0:
  9.5 85.4 all-gather.2
  97.0 84.5 all-gather.4
  226.4 35.7 reduce-scatter.1
where the time goes:
time: 271 us; the launch traced here: 269 us
  waiting for transfers between devices  183 us (68%)
  local copies, waits for them, and re-layouts  41 us (15%)
  matrix products  30.4 us (11%)
  between operations  13.3 us (5%)
    all_gather x1, waiting for transfers between devices, on_device(): lax.all_gather(value_vectors, 'frame', axis=0, tiled=True)  80.7 us
    all_gather x1, waiting for transfers between devices, on_device(): lax.all_gather(key_vectors, 'frame', axis=0, tiled=True)  65.4 us
    reduce_scatter x1, waiting for transfers between devices, on_device(): lax.psum_scatter(partial_value.astype(jnp.bfloat16), 'head', scatter_dime...  35.9 us
    unnamed x20, local copies, waits for them, and re-layouts  27.8 us
    sub x1, matrix products, on_device(): expo = jnp.exp(scores - peak)  11.6 us
    dot_general x1, matrix products, on_device(): jnp.dot(attended, out_weight, preferred_element_type=jnp.float32)  9.72 us
    concatenate x2, local copies, waits for them, and re-layouts, on_device(): jnp.concatenate([piece[1] for piece in pieces], 0)  9.21 us
    dot_general x1, matrix products, on_device(): jnp.einsum('hqk,khd->qhd', weights, value_all, preferred_element_type=jnp...  9.09 us
  transfers between devices with their start and end apart: 3, of which 3 were waited for; matrix products, arithmetic and copies ran while one was open for 10% of the time, Pallas kernels for 0%

commit v1 on v0

v1 whole, which is shorter than its diff:
```python
import functools
import math

import jax
import jax.numpy as jnp
from jax import lax
from jax.experimental import pallas as pl
from jax.experimental.pallas import tpu as pltpu
from jax.sharding import PartitionSpec as P

HDIM = 128
BLK = 64
EXP_SCALE = math.log2(math.e) / math.sqrt(HDIM)
DEAD = -1e30
CHUNKS = (4, 3, 3)
F32 = jnp.float32
BF16 = jnp.bfloat16


def offsets_for(frames):
    result = [0]
    step = 1
    while step <= frames // 2:
        result.append(step)
        result.append(-step)
        step = step * 2
    return result


def shift(frames, by, keep=None):
    return [
        (i, i + by)
        for i in range(frames)
        if 0 <= i + by < frames and (keep is None or keep(i))
    ]


def params(megabytes=48):
    return pltpu.CompilerParams(vmem_limit_bytes=megabytes << 20)


def pack_kernel(starts, widths, k_ref, v_ref, *rest):
    outs, sem = rest[:-1], rest[-1]
    rows = k_ref.shape[0]
    copies = []
    for n, out in enumerate(outs):
        columns = pl.ds(starts[n], widths[n])
        for half, ref in enumerate((k_ref, v_ref)):
            copies.append(
                pltpu.make_async_copy(
                    ref.at[:, columns], out.at[pl.ds(half * rows, rows), :], sem.at[2 * n + half]
                )
            )
    for copy in copies:
        copy.start()
    for copy in copies:
        copy.wait()


def pack(keys, values, starts, widths):
    rows = keys.shape[0]
    moved = 4 * rows * sum(widths) * 2
    return pl.pallas_call(
        functools.partial(pack_kernel, starts, widths),
        out_shape=[jax.ShapeDtypeStruct((2 * rows, w), BF16) for w in widths],
        in_specs=[pl.BlockSpec(memory_space=pl.ANY)] * 2,
        out_specs=[pl.BlockSpec(memory_space=pl.ANY)] * len(widths),
        scratch_shapes=[pltpu.SemaphoreType.DMA((2 * len(widths),))],
        cost_estimate=pl.CostEstimate(flops=0, bytes_accessed=moved, transcendentals=0),
        name="pack",
    )(keys, values)


def attend_kernel(groups, flag_ref, q_ref, k_ref, v_ref, bias_ref, *rest):
    slots, o_ref = rest[:-1], rest[-1]
    rows = q_ref.shape[0]
    q = q_ref[...]
    scores = []
    values = []
    for n in range(len(groups) + 1):
        if n == 0:
            key, value = k_ref[...], v_ref[...]
        elif len(groups[n - 1]) == 1:
            ref = slots[groups[n - 1][0]]
            key, value = ref[:rows, :], ref[rows:, :]
        else:
            one, two = (slots[g] for g in groups[n - 1])
            first = flag_ref[n] > 0
            both = jnp.where(first, one[...], two[...])
            key, value = both[:rows, :], both[rows:, :]
        s = lax.dot_general(q, key, (((1,), (1,)), ((), ())), preferred_element_type=F32)
        bias = jnp.concatenate(
            [
                jnp.broadcast_to(bias_ref[b : b + 1, n * rows : (n + 1) * rows], (BLK, rows))
                for b in range(rows // BLK)
            ],
            0,
        )
        scores.append(s + bias)
        values.append(value)
    peak = functools.reduce(jnp.maximum, scores)
    peak = jnp.max(peak, axis=1, keepdims=True)
    acc = None
    total = None
    for s, value in zip(scores, values):
        e = jnp.exp2((s - peak) * EXP_SCALE)
        total = e if total is None else total + e
        part = jnp.dot(e.astype(BF16), value, preferred_element_type=F32)
        acc = part if acc is None else acc + part
    total = jnp.sum(total, axis=1, keepdims=True)
    o_ref[...] = (acc / total).astype(o_ref.dtype)


def attend(queries, keys, values, bias, flags, slots, groups, first, heads):
    rows = queries.shape[0]
    wide = lambda h, f: (0, first + h)
    near = lambda h, f: (0, h)
    keys_seen = rows * (len(groups) + 1)
    return pl.pallas_call(
        functools.partial(attend_kernel, groups),
        out_shape=jax.ShapeDtypeStruct((rows, heads * HDIM), BF16),
        grid_spec=pltpu.PrefetchScalarGridSpec(
            num_scalar_prefetch=1,
            grid=(heads,),
            in_specs=[pl.BlockSpec((rows, HDIM), wide)] * 3
            + [pl.BlockSpec(bias.shape, lambda h, f: (0, 0))]
            + [pl.BlockSpec((2 * rows, HDIM), near)] * len(slots),
            out_specs=pl.BlockSpec((rows, HDIM), near),
        ),
        compiler_params=params(),
        cost_estimate=pl.CostEstimate(
            flops=4 * heads * rows * keys_seen * HDIM,
            bytes_accessed=4 * heads * keys_seen * HDIM,
            transcendentals=heads * rows * keys_seen,
        ),
        name="attend",
    )(flags, queries, keys, values, bias, *slots)


def project_kernel(count, pick_ref, *refs):
    weight, outs = refs[count], refs[count + 1]
    acc = None
    at = 0
    for ref in refs[:count]:
        a = ref[...]
        part = jnp.dot(a, weight[at : at + a.shape[1], :], preferred_element_type=F32)
        at += a.shape[1]
        acc = part if acc is None else acc + part
    outs[...] = acc.astype(outs.dtype)


def project(pieces, weight, picks, rows_used, tile):
    rows = pieces[0].shape[0]
    columns = weight.shape[1] // lax.axis_size("head")
    steps = columns // tile
    groups = picks.shape[0]
    return pl.pallas_call(
        functools.partial(project_kernel, len(pieces)),
        out_shape=jax.ShapeDtypeStruct((groups * rows, columns), BF16),
        grid_spec=pltpu.PrefetchScalarGridSpec(
            num_scalar_prefetch=1,
            grid=(groups, steps),
            in_specs=[pl.BlockSpec(p.shape, lambda g, t, k: (0, 0)) for p in pieces]
            + [pl.BlockSpec((rows_used, tile), lambda g, t, k: (0, k[g] * steps + t))],
            out_specs=pl.BlockSpec((rows, tile), lambda g, t, k: (g, t)),
        ),
        compiler_params=params(),
        cost_estimate=pl.CostEstimate(
            flops=2 * rows * rows_used * columns * groups,
            bytes_accessed=2 * rows_used * columns * groups,
            transcendentals=0,
        ),
        name="project",
    )(picks, *pieces, weight)


def finish_kernel(count, *refs):
    out = refs[-1]
    acc = None
    for a, w in zip(refs[:count], refs[count : 2 * count]):
        part = jnp.dot(a[...], w[...], preferred_element_type=F32)
        acc = part if acc is None else acc + part
    for ref in refs[2 * count : -1]:
        acc = acc + ref[...].astype(F32)
    out[...] = acc.astype(out.dtype)


def finish(pieces, weights, sums, tile):
    rows = pieces[0].shape[0]
    columns = weights[0].shape[1]
    depth = weights[0].shape[0]
    return pl.pallas_call(
        functools.partial(finish_kernel, len(pieces)),
        out_shape=jax.ShapeDtypeStruct((rows, columns), BF16),
        grid=(columns // tile,),
        in_specs=[pl.BlockSpec(p.shape, lambda t: (0, 0)) for p in pieces]
        + [pl.BlockSpec((depth, tile), lambda t: (0, t))] * len(weights)
        + [pl.BlockSpec((rows, tile), lambda t: (0, t))] * len(sums),
        out_specs=pl.BlockSpec((rows, tile), lambda t: (0, t)),
        compiler_params=params(),
        cost_estimate=pl.CostEstimate(
            flops=2 * rows * depth * columns * len(pieces),
            bytes_accessed=2 * depth * columns * len(pieces),
            transcendentals=0,
        ),
        name="finish",
    )(*pieces, *weights, *sums)


def send(x, axis, pairs):
    return lax.ppermute(x, axis, pairs)


def first_hops(kv, frames):
    if frames != 8:
        return [send(kv, "frame", shift(frames, -o)) for o in offsets_for(frames)[1:]]
    return [
        send(kv, "frame", [(i, i ^ 1) for i in range(frames)]),
        send(kv, "frame", shift(frames, 2)),
        send(kv, "frame", shift(frames, -2)),
    ]


def second_hops(hops, frames):
    if frames != 8:
        return hops
    pair, low, high = hops
    inner = lambda i: 2 <= i <= 5
    return hops + [
        send(low, "frame", shift(frames, -1, lambda i: i % 2 == 1 and i >= 2)),
        send(high, "frame", shift(frames, 1, lambda i: i % 2 == 0 and i <= 5)),
        send(low, "frame", shift(frames, 2, inner)),
        send(high, "frame", shift(frames, -2, inner)),
    ]


def plan(frames, own):
    if frames != 8:
        offsets = offsets_for(frames)
        groups = tuple((n,) for n in range(len(offsets) - 1))
        return groups, [own + o for o in offsets], [jnp.int32(1)] * len(offsets)
    even = own % 2 == 0
    upper = own >= 4
    groups = ((0,), (1,), (2,), (3, 4), (5, 6))
    one = jnp.int32(1)
    held = [
        own,
        jnp.where(even, own + 1, own - 1),
        own - 2,
        own + 2,
        jnp.where(even, own - 1, own + 1),
        jnp.where(upper, own - 4, own + 4),
    ]
    return groups, held, [one, one, one, one, even.astype(jnp.int32), upper.astype(jnp.int32)]


def on_device(queries, key_vectors, value_vectors, live_blocks, out_weight):
    frames = lax.axis_size("frame")
    own = lax.axis_index("frame")
    group = lax.axis_index("head")
    rows = queries.shape[0]
    blocks = rows // BLK
    columns = out_weight.shape[1] // lax.axis_size("head")

    widths = [c * HDIM for c in CHUNKS]
    starts = [sum(widths[:n]) for n in range(len(widths))]
    packed = pack(key_vectors, value_vectors, starts[:1], widths[:1]) + pack(
        key_vectors, value_vectors, starts[1:], widths[1:]
    )
    hops = [first_hops(kv, frames) for kv in packed]

    groups, held, flags = plan(frames, own)
    flags = jnp.stack(flags)
    lives = []
    for frame in held:
        inside = (frame >= 0) & (frame < frames)
        square = lax.dynamic_slice_in_dim(
            live_blocks, jnp.clip(frame, 0, frames - 1) * blocks, blocks, 1
        )
        lives.append(jnp.where(inside, square, 0))
    live = jnp.repeat(jnp.concatenate(lives, 1), BLK, 1)
    bias = jnp.where(live > 0, 0.0, DEAD).astype(F32)

    last = starts[-1]

    def weight_part(other):
        return lax.dynamic_slice(
            out_weight, (jnp.int32(last), other * columns), (widths[-1], columns)
        )

    swap = lambda x, bit: send(x, "head", [(g, g ^ bit) for g in range(4)])
    late_weights = [weight_part(group)] + [
        swap(weight_part(group ^ bit), bit) for bit in (1, 2, 3)
    ]

    attended = []
    for n, width in enumerate(widths):
        slots = second_hops(hops[n], frames)
        attended.append(
            attend(
                queries, key_vectors, value_vectors, bias, flags, slots, groups,
                starts[n] // HDIM, width // HDIM,
            )
        )

    early = attended[:-1]
    away = project(early, out_weight, jnp.stack([group ^ 3, group ^ 2]), last, columns // 2)
    near = project(early, out_weight, jnp.stack([group ^ 1, group]), last, columns // 2)
    crossed = (away[rows:].astype(F32) + swap(away[:rows], 1).astype(F32)).astype(BF16)
    from_far = swap(crossed, 2)
    from_near = swap(near[:rows], 1)

    late = attended[-1]
    pieces = [late] + [swap(late, bit) for bit in (1, 2, 3)]
    return finish(pieces, late_weights, [near[rows:], from_near, from_far], columns // 2)


def solution(mesh):
    placed = (
        P("frame", "head"),
        P("frame", "head"),
        P("frame", "head"),
        P("frame", None),
        P("head", None),
    )
    return jax.shard_map(
        on_device, mesh=mesh, in_specs=placed, out_specs=P("frame", "head"), check_vma=False
    )
```

time: 271 us -> 217 us (0.80)
  waiting for transfers between devices: 183 us -> 66 us
  Pallas kernels: 0 us -> 71.1 us
  starting transfers between devices: 0.08 us -> 64.2 us
  matrix products: 30.4 us -> 0 us
  local copies, waits for them, and re-layouts: 41 us -> 13.9 us
  between operations: 13.3 us -> 0.48 us
    all_gather x2 -> x0, waiting for transfers between devices: 146 us -> none  [the longest x1 80.7 us: on_device(): lax.all_gather(value_vectors, 'frame', axis=0, tiled=True)]
    pallas_call x0 -> x8, Pallas kernels: none -> 71.1 us  [the longest x2 42 us: pack(): pl.pallas_call(functools.partial(pack_kernel, starts, widths), out_shape=...]
    ppermute x0 -> x30, waiting for transfers between devices: none -> 66 us  [send(): return lax.ppermute(x, axis, pairs)]
    ppermute x0 -> x30, starting transfers between devices: none -> 64.2 us  [send(): return lax.ppermute(x, axis, pairs)]
    reduce_scatter x1 -> x0, waiting for transfers between devices: 35.9 us -> none  [on_device(): lax.psum_scatter(partial_value.astype(jnp.bfloat16), 'head', scatter_dime...]
    dot_general x2 -> x0, matrix products: 18.8 us -> none  [the longest x1 9.72 us: on_device(): jnp.dot(attended, out_weight, preferred_element_type=jnp.float32)]
    unnamed x20 -> x42, local copies, waits for them, and re-layouts: 27.8 us -> 9.58 us
    sub x1 -> x0, matrix products: 11.6 us -> none  [on_device(): expo = jnp.exp(scores - peak)]
  transfers between devices with their start and end apart: 3 -> 30, of which waited for: 3 -> 8; matrix products, arithmetic and copies ran while one was open for 10% -> 2% of each run, Pallas kernels for 0% -> 20%
where the time goes in v1:
time: 217 us; the launch traced here: 216 us
  Pallas kernels  71.1 us (33%)
  waiting for transfers between devices  66 us (30%)
  starting transfers between devices  64.2 us (30%)
  local copies, waits for them, and re-layouts  13.9 us (6%)
    ppermute x30, waiting for transfers between devices, send(): return lax.ppermute(x, axis, pairs)  66 us
    ppermute x30, starting transfers between devices, send(): return lax.ppermute(x, axis, pairs)  64.2 us
    pallas_call x2, Pallas kernels, pack(): pl.pallas_call(functools.partial(pack_kernel, starts, widths), out_shape=...  42 us
    pallas_call x3, Pallas kernels, attend(): pl.pallas_call(functools.partial(attend_kernel, groups), out_shape=jax.Sh...  15.4 us
    pallas_call x2, Pallas kernels, project(): pl.pallas_call(functools.partial(project_kernel, len(pieces)), out_shape=...  9.95 us
    unnamed x42, local copies, waits for them, and re-layouts  9.58 us
  transfers between devices with their start and end apart: 30, of which 8 were waited for; matrix products, arithmetic and copies ran while one was open for 2% of the time, Pallas kernels for 20%

profile of v1, /device:TPU:10, one launch (start us, length us, event | category | flops | bytes accessed | tf_op | source)
XLA Modules:
  0.0 216.1 jit_solution(8585524683078572277)
XLA Ops:
  0.0 25.0 %pack.2 = (bf16[512,384]{1,0:T(8,128)(2,1)}, bf16[512,384]{1,0:T(8,128)(2,1)}) custom-call(bf16[256,1280]{1,0:T(8,128)(2,1)} %k_ref.9, bf16[256,1280]{1,0:T(8,128)(2,1)} %v_ref.9), custom_call_target="tpu_custom_call" | custom-call | bytes 1572864 | tf_op jit(solution)/shard_map/pack/pallas_call | solution.py:63
  25.0 2.5 %collective-permute-start.2 = (bf16[512,384]{1,0:T(8,128)(2,1)}, bf16[512,384]{1,0:T(8,128)(2,1)}, u32[]{:S(2)}, u32[]{:S(2)}) collective-permute-start(bf16[512,384]{1,0:T(8,128)(2,1)} %get-tuple-element.7), channel_id=1, source_target_pairs={{8,0},{12,4},{16,8},{20,12},{24,16},{28,20},{9,1},{13,5},{17,9},{2... | collective-permute-start | bytes 1179656 | tf_op jit(solution)/shard_map/ppermute | solution.py:211
  27.5 3.5 %collective-permute-start.1 = (bf16[512,384]{1,0:T(8,128)(2,1)}, bf16[512,384]{1,0:T(8,128)(2,1)}, u32[]{:S(2)}, u32[]{:S(2)}) collective-permute-start(bf16[512,384]{1,0:T(8,128)(2,1)} %get-tuple-element.7), channel_id=1, source_target_pairs={{0,8},{4,12},{8,16},{12,20},{16,24},{20,28},{1,9},{5,13},{9,17},{1... | collective-permute-start | bytes 1179656 | tf_op jit(solution)/shard_map/ppermute | solution.py:211
  31.0 3.1 %collective-permute-start.22 = (bf16[512,384]{1,0:T(8,128)(2,1)}, bf16[512,384]{1,0:T(8,128)(2,1)S(1)}, u32[]{:S(2)}, u32[]{:S(2)}) collective-permute-start(bf16[512,384]{1,0:T(8,128)(2,1)} %get-tuple-element.8), channel_id=1, source_target_pairs={{8,0},{12,4},{16,8},{20,12},{24,16},{28,20},{9,1},{13,5},{17,9},{2... | collective-permute-start | bytes 1179656 | tf_op jit(solution)/shard_map/ppermute | solution.py:211
  34.1 17.0 %pack.3 = bf16[512,512]{1,0:T(8,128)(2,1)} custom-call(bf16[256,1280]{1,0:T(8,128)(2,1)} %k_ref.9, bf16[256,1280]{1,0:T(8,128)(2,1)} %v_ref.9), custom_call_target="tpu_custom_call" | custom-call | bytes 1048576 | tf_op jit(solution)/shard_map/pack/pallas_call | solution.py:63
  53.0 3.9 %collective-permute-start.21 = (bf16[512,384]{1,0:T(8,128)(2,1)S(1)}, bf16[512,384]{1,0:T(8,128)(2,1)}, u32[]{:S(2)}, u32[]{:S(2)}) collective-permute-start(bf16[512,384]{1,0:T(8,128)(2,1)S(1)} %copy-done.20), channel_id=1, source_target_pairs={{0,8},{4,12},{8,16},{12,20},{16,24},{20,28},{1,9},{5,13},{9,17},{1... | collective-permute-start | bytes 1179656 | tf_op jit(solution)/shard_map/ppermute | solution.py:211
  57.1 3.5 %collective-permute-start.14 = (bf16[512,512]{1,0:T(8,128)(2,1)}, bf16[512,512]{1,0:T(8,128)(2,1)}, u32[]{:S(2)}, u32[]{:S(2)}) collective-permute-start(bf16[512,512]{1,0:T(8,128)(2,1)} %pack.3), channel_id=1, source_target_pairs={{0,8},{4,12},{8,16},{12,20},{16,24},{20,28},{1,9},{5,13},{9,17},{1... | collective-permute-start | bytes 1572872 | tf_op jit(solution)/shard_map/ppermute | solution.py:211
  62.2 4.9 %collective-permute-done.21.rest_1_ = bf16[512,384]{1,0:T(8,128)(2,1)} collective-permute-done((bf16[512,384]{1,0:T(8,128)(2,1)S(1)}, bf16[512,384]{1,0:T(8,128)(2,1)}, u32[]{:S(2)}, u32[]{:S(2)}) %collective-permute-start.21) | collective-permute-done | bytes 393248 | tf_op jit(solution)/shard_map/ppermute | solution.py:211
  71.9 3.9 %collective-permute-start.25 = (bf16[512,384]{1,0:T(8,128)(2,1)}, bf16[512,384]{1,0:T(8,128)(2,1)S(1)}, u32[]{:S(2)}, u32[]{:S(2)}) collective-permute-start(bf16[512,384]{1,0:T(8,128)(2,1)} %collective-permute-done.21.rest_1_), channel_id=1, source_target_pairs={{8,16},{12,20},{16,24},{20,28},{9,17},{13,21},{17,25},{21,29},{10,... | collective-permute-start | bytes 1179656 | tf_op jit(solution)/shard_map/ppermute | solution.py:211
  77.9 3.6 %collective-permute-start.23 = (bf16[512,384]{1,0:T(8,128)(2,1)}, bf16[512,384]{1,0:T(8,128)(2,1)}, u32[]{:S(2)}, u32[]{:S(2)}) collective-permute-start(bf16[512,384]{1,0:T(8,128)(2,1)} %collective-permute-done.21.rest_1_), channel_id=1, source_target_pairs={{12,8},{20,16},{28,24},{13,9},{21,17},{29,25},{14,10},{22,18},{30,... | collective-permute-start | bytes 1179656 | tf_op jit(solution)/shard_map/ppermute | solution.py:211
  87.6 4.9 %collective-permute-start.18 = (bf16[512,512]{1,0:T(8,128)(2,1)}, bf16[512,512]{1,0:T(8,128)(2,1)}, u32[]{:S(2)}, u32[]{:S(2)}) collective-permute-start(bf16[512,512]{1,0:T(8,128)(2,1)} %collective-permute-done.14.rest_1_), channel_id=1, source_target_pairs={{8,16},{12,20},{16,24},{20,28},{9,17},{13,21},{17,25},{21,29},{10,... | collective-permute-start | bytes 1572872 | tf_op jit(solution)/shard_map/ppermute | solution.py:211
  93.2 6.1 %collective-permute-start.16 = (bf16[512,512]{1,0:T(8,128)(2,1)}, bf16[512,512]{1,0:T(8,128)(2,1)}, u32[]{:S(2)}, u32[]{:S(2)}) collective-permute-start(bf16[512,512]{1,0:T(8,128)(2,1)} %collective-permute-done.14.rest_1_), channel_id=1, source_target_pairs={{12,8},{20,16},{28,24},{13,9},{21,17},{29,25},{14,10},{22,18},{30,... | collective-permute-start | bytes 1572872 | tf_op jit(solution)/shard_map/ppermute | solution.py:211
  99.4 3.9 %constant_dynamic-slice_fusion = (bf16[384,1280]{1,0:T(8,128)(2,1)}, bf16[384,1280]{1,0:T(8,128)(2,1)}, bf16[384,1280]{1,0:T(8,128)(2,1)}, bf16[384,1280]{1,0:T(8,128)(2,1)S(1)}) fusion(bf16[1280,5120]{1,0:T(8,128)(2,1)} %refs_2_.3, s32[]{:T(128)S(6)} %select_n.117, s32[]{:T(128)S(6)} %select_n.116, s32[]{:T(128)S(6)} %select_n.115, s32[]{:T(128)S(6)} %select_n.114), kind=kLoop, calls=%fused_computation.8 | loop fusion | bytes 7864336 | tf_op jit(solution)/shard_map/dynamic_slice | solution.py:287
  106.5 5.4 %collective-permute-start.5 = (bf16[512,384]{1,0:T(8,128)(2,1)}, bf16[512,384]{1,0:T(8,128)(2,1)}, u32[]{:S(2)}, u32[]{:S(2)}) collective-permute-start(bf16[512,384]{1,0:T(8,128)(2,1)} %collective-permute-done.1.rest_1_), channel_id=1, source_target_pairs={{8,16},{12,20},{16,24},{20,28},{9,17},{13,21},{17,25},{21,29},{10,... | collective-permute-start | bytes 1179656 | tf_op jit(solution)/shard_map/ppermute | solution.py:211
  112.0 6.0 %collective-permute-start.3 = (bf16[512,384]{1,0:T(8,128)(2,1)}, bf16[512,384]{1,0:T(8,128)(2,1)}, u32[]{:S(2)}, u32[]{:S(2)}) collective-permute-start(bf16[512,384]{1,0:T(8,128)(2,1)} %collective-permute-done.1.rest_1_), channel_id=1, source_target_pairs={{12,8},{20,16},{28,24},{13,9},{21,17},{29,25},{14,10},{22,18},{30,... | collective-permute-start | bytes 1179656 | tf_op jit(solution)/shard_map/ppermute | solution.py:211
  123.3 4.5 %attend.5.refs_1_ = bf16[256,384]{1,0:T(8,128)(2,1)S(1)} custom-call(s32[6]{0:T(128)S(1)} %pad_add_fusion.flag_ref, bf16[256,1280]{1,0:T(8,128)(2,1)S(1)} %copy-done.2, bf16[256,1280]{1,0:T(8,128)(2,1)S(1)} %copy-done, bf16[256,1280]{1,0:T(8,128)(2,1)S(1)} %copy-done.1, f32[4,1536]{1,0:T(4,128)S(1)} %select_n.113.bias_ref, bf16[512,384]{1,0:T(8,128)(2,1)S(1)} %copy-done.8, ...), custom_call_target="tpu_custom_call" | custom-call | flops 603979776 | bytes 2359296 | tf_op jit(solution)/shard_map/attend/pallas_call | solution.py:119
  127.9 5.9 %attend.4.refs_0_ = bf16[256,512]{1,0:T(8,128)(2,1)S(1)} custom-call(s32[6]{0:T(128)S(1)} %pad_add_fusion.flag_ref, bf16[256,1280]{1,0:T(8,128)(2,1)S(1)} %copy-done.2, bf16[256,1280]{1,0:T(8,128)(2,1)S(1)} %copy-done, bf16[256,1280]{1,0:T(8,128)(2,1)S(1)} %copy-done.1, f32[4,1536]{1,0:T(4,128)S(1)} %select_n.113.bias_ref, bf16[512,512]{1,0:T(8,128)(2,1)S(1)} %copy-done.4, ...), custom_call_target="tpu_custom_call" | custom-call | flops 805306368 | bytes 3145728 | tf_op jit(solution)/shard_map/attend/pallas_call | solution.py:119
  133.8 5.0 %project.3 = bf16[512,1280]{1,0:T(8,128)(2,1)S(1)} custom-call(s32[2]{0:T(128)S(1)} %get-tuple-element.22.pick_ref, bf16[256,512]{1,0:T(8,128)(2,1)S(1)} %attend.4.refs_0_, bf16[256,384]{1,0:T(8,128)(2,1)S(1)} %attend.5.refs_1_, bf16[1280,5120]{1,0:T(8,128)(2,1)} %refs_2_.3), custom_call_target="tpu_custom_call" | custom-call | flops 1174405120 | bytes 4587520 | tf_op jit(solution)/shard_map/project/pallas_call | solution.py:157
  141.1 5.0 %attend.3.refs_0_ = bf16[256,384]{1,0:T(8,128)(2,1)S(1)} custom-call(s32[6]{0:T(128)S(1)} %pad_add_fusion.flag_ref, bf16[256,1280]{1,0:T(8,128)(2,1)S(1)} %copy-done.2, bf16[256,1280]{1,0:T(8,128)(2,1)S(1)} %copy-done, bf16[256,1280]{1,0:T(8,128)(2,1)S(1)} %copy-done.1, f32[4,1536]{1,0:T(4,128)S(1)} %select_n.113.bias_ref, ...), custom_call_target="tpu_custom_call" | custom-call | flops 603979776 | bytes 2359296 | tf_op jit(solution)/shard_map/attend/pallas_call | solution.py:119
  147.6 5.0 %project.2 = bf16[512,1280]{1,0:T(8,128)(2,1)S(1)} custom-call(s32[2]{0:T(128)S(1)} %get-tuple-element.21.pick_ref, bf16[256,512]{1,0:T(8,128)(2,1)S(1)} %attend.4.refs_0_, bf16[256,384]{1,0:T(8,128)(2,1)S(1)} %attend.5.refs_1_, bf16[1280,5120]{1,0:T(8,128)(2,1)} %refs_2_.3), custom_call_target="tpu_custom_call" | custom-call | flops 1174405120 | bytes 4587520 | tf_op jit(solution)/shard_map/project/pallas_call | solution.py:157
  152.6 35.6 %collective-permute-done.9.refs_3_ = bf16[256,384]{1,0:T(8,128)(2,1)S(1)} collective-permute-done((bf16[256,384]{1,0:T(8,128)(2,1)S(1)}, bf16[256,384]{1,0:T(8,128)(2,1)S(1)}, u32[]{:S(2)}, u32[]{:S(2)}) %collective-permute-start.9) | collective-permute-done | bytes 196640 | tf_op jit(solution)/shard_map/ppermute | solution.py:211
  189.1 6.1 %collective-permute-done.8.refs_2_ = bf16[256,384]{1,0:T(8,128)(2,1)S(1)} collective-permute-done((bf16[256,384]{1,0:T(8,128)(2,1)S(1)}, bf16[256,384]{1,0:T(8,128)(2,1)S(1)}, u32[]{:S(2)}, u32[]{:S(2)}) %collective-permute-start.8) | collective-permute-done | bytes 196640 | tf_op jit(solution)/shard_map/ppermute | solution.py:211
  197.3 15.1 %collective-permute-done.29.refs_10_ = bf16[256,1280]{1,0:T(8,128)(2,1)S(1)} collective-permute-done((bf16[256,1280]{1,0:T(8,128)(2,1)S(1)}, bf16[256,1280]{1,0:T(8,128)(2,1)S(1)}, u32[]{:S(2)}, u32[]{:S(2)}) %collective-permute-start.29) | collective-permute-done | bytes 655392 | tf_op jit(solution)/shard_map/ppermute | solution.py:211
  212.3 3.8 %finish.1 = bf16[256,1280]{1,0:T(8,128)(2,1)} custom-call(bf16[256,384]{1,0:T(8,128)(2,1)S(1)} %attend.3.refs_0_, bf16[256,384]{1,0:T(8,128)(2,1)S(1)} %collective-permute-done.7.refs_1_, bf16[256,384]{1,0:T(8,128)(2,1)S(1)} %collective-permute-done.8.refs_2_, bf16[256,384]{1,0:T(8,128)(2,1)S(1)} %collective-permute-done.9.refs_3_, ...), custom_call_target="tpu_custom_call" | custom-call | flops 1006632960 | bytes 3932160 | tf_op jit(solution)/shard_map/finish/pallas_call | solution.py:192
  (98 shorter events, 32.6 us)
Async XLA Ops:
  25.0 32.0 %collective-permute-start.2 = (bf16[512,384]{1,0:T(8,128)(2,1)}, bf16[512,384]{1,0:T(8,128)(2,1)}, u32[]{:S(2)}, u32[]{:S(2)}) collective-permute-start(bf16[512,384]{1,0:T(8,128)(2,1)} %get-tuple-element.7), channel_id=1, source_target_pairs={{8,0},{12,4},{16,8},{20,12},{24,16},{28,20},{9,1},{13,5},{17,9},{2... | collective-permute-start | bytes 1179656 | tf_op jit(solution)/shard_map/ppermute | solution.py:211
  27.5 29.7 %collective-permute-start.1 = (bf16[512,384]{1,0:T(8,128)(2,1)}, bf16[512,384]{1,0:T(8,128)(2,1)}, u32[]{:S(2)}, u32[]{:S(2)}) collective-permute-start(bf16[512,384]{1,0:T(8,128)(2,1)} %get-tuple-element.7), channel_id=1, source_target_pairs={{0,8},{4,12},{8,16},{12,20},{16,24},{20,28},{1,9},{5,13},{9,17},{1... | collective-permute-start | bytes 1179656 | tf_op jit(solution)/shard_map/ppermute | solution.py:211
  31.0 29.7 %collective-permute-start.22 = (bf16[512,384]{1,0:T(8,128)(2,1)}, bf16[512,384]{1,0:T(8,128)(2,1)S(1)}, u32[]{:S(2)}, u32[]{:S(2)}) collective-permute-start(bf16[512,384]{1,0:T(8,128)(2,1)} %get-tuple-element.8), channel_id=1, source_target_pairs={{8,0},{12,4},{16,8},{20,12},{24,16},{28,20},{9,1},{13,5},{17,9},{2... | collective-permute-start | bytes 1179656 | tf_op jit(solution)/shard_map/ppermute | solution.py:211
  51.1 20.8 %collective-permute-start.15 = (bf16[512,512]{1,0:T(8,128)(2,1)}, bf16[512,512]{1,0:T(8,128)(2,1)S(1)}, u32[]{:S(2)}, u32[]{:S(2)}) collective-permute-start(bf16[512,512]{1,0:T(8,128)(2,1)} %pack.3), channel_id=1, source_target_pairs={{8,0},{12,4},{16,8},{20,12},{24,16},{28,20},{9,1},{13,5},{17,9},{2... | collective-permute-start | bytes 1572872 | tf_op jit(solution)/shard_map/ppermute | solution.py:211
  57.1 20.7 %collective-permute-start.14 = (bf16[512,512]{1,0:T(8,128)(2,1)}, bf16[512,512]{1,0:T(8,128)(2,1)}, u32[]{:S(2)}, u32[]{:S(2)}) collective-permute-start(bf16[512,512]{1,0:T(8,128)(2,1)} %pack.3), channel_id=1, source_target_pairs={{0,8},{4,12},{8,16},{12,20},{16,24},{20,28},{1,9},{5,13},{9,17},{1... | collective-permute-start | bytes 1572872 | tf_op jit(solution)/shard_map/ppermute | solution.py:211
  60.7 20.8 %collective-permute-start.13 = (bf16[512,512]{1,0:T(8,128)(2,1)}, bf16[512,512]{1,0:T(8,128)(2,1)S(1)}, u32[]{:S(2)}, u32[]{:S(2)}) collective-permute-start(bf16[512,512]{1,0:T(8,128)(2,1)} %pack.3), channel_id=1, source_target_pairs={{0,4},{4,0},{8,12},{12,8},{16,20},{20,16},{24,28},{28,24},{1,5},{5... | collective-permute-start | bytes 1572872 | tf_op jit(solution)/shard_map/ppermute | solution.py:211
  67.1 17.1 %collective-permute-start.26 = (bf16[512,384]{1,0:T(8,128)(2,1)S(1)}, bf16[512,384]{1,0:T(8,128)(2,1)S(1)}, u32[]{:S(2)}, u32[]{:S(2)}) collective-permute-start(bf16[512,384]{1,0:T(8,128)(2,1)S(1)} %collective-permute-done.22.rest_2_), channel_id=1, source_target_pairs={{8,0},{12,4},{16,8},{20,12},{9,1},{13,5},{17,9},{21,13},{10,2},{14... | collective-permute-start | bytes 1179656 | tf_op jit(solution)/shard_map/ppermute | solution.py:211
  71.9 20.6 %collective-permute-start.25 = (bf16[512,384]{1,0:T(8,128)(2,1)}, bf16[512,384]{1,0:T(8,128)(2,1)S(1)}, u32[]{:S(2)}, u32[]{:S(2)}) collective-permute-start(bf16[512,384]{1,0:T(8,128)(2,1)} %collective-permute-done.21.rest_1_), channel_id=1, source_target_pairs={{8,16},{12,20},{16,24},{20,28},{9,17},{13,21},{17,25},{21,29},{10,... | collective-permute-start | bytes 1179656 | tf_op jit(solution)/shard_map/ppermute | solution.py:211
  77.9 25.4 %collective-permute-start.23 = (bf16[512,384]{1,0:T(8,128)(2,1)}, bf16[512,384]{1,0:T(8,128)(2,1)}, u32[]{:S(2)}, u32[]{:S(2)}) collective-permute-start(bf16[512,384]{1,0:T(8,128)(2,1)} %collective-permute-done.21.rest_1_), channel_id=1, source_target_pairs={{12,8},{20,16},{28,24},{13,9},{21,17},{29,25},{14,10},{22,18},{30,... | collective-permute-start | bytes 1179656 | tf_op jit(solution)/shard_map/ppermute | solution.py:211
  82.2 21.0 %collective-permute-start.19 = (bf16[512,512]{1,0:T(8,128)(2,1)S(1)}, bf16[512,512]{1,0:T(8,128)(2,1)}, u32[]{:S(2)}, u32[]{:S(2)}) collective-permute-start(bf16[512,512]{1,0:T(8,128)(2,1)S(1)} %collective-permute-done.15.rest_2_), channel_id=1, source_target_pairs={{8,0},{12,4},{16,8},{20,12},{9,1},{13,5},{17,9},{21,13},{10,2},{14... | collective-permute-start | bytes 1572872 | tf_op jit(solution)/shard_map/ppermute | solution.py:211
  84.9 20.3 %collective-permute-start.17 = (bf16[512,512]{1,0:T(8,128)(2,1)S(1)}, bf16[512,512]{1,0:T(8,128)(2,1)}, u32[]{:S(2)}, u32[]{:S(2)}) collective-permute-start(bf16[512,512]{1,0:T(8,128)(2,1)S(1)} %collective-permute-done.15.rest_2_), channel_id=1, source_target_pairs={{0,4},{8,12},{16,20},{1,5},{9,13},{17,21},{2,6},{10,14},{18,22},{3... | collective-permute-start | bytes 1572872 | tf_op jit(solution)/shard_map/ppermute | solution.py:211
  87.6 18.9 %collective-permute-start.18 = (bf16[512,512]{1,0:T(8,128)(2,1)}, bf16[512,512]{1,0:T(8,128)(2,1)}, u32[]{:S(2)}, u32[]{:S(2)}) collective-permute-start(bf16[512,512]{1,0:T(8,128)(2,1)} %collective-permute-done.14.rest_1_), channel_id=1, source_target_pairs={{8,16},{12,20},{16,24},{20,28},{9,17},{13,21},{17,25},{21,29},{10,... | collective-permute-start | bytes 1572872 | tf_op jit(solution)/shard_map/ppermute | solution.py:211
  93.2 18.7 %collective-permute-start.16 = (bf16[512,512]{1,0:T(8,128)(2,1)}, bf16[512,512]{1,0:T(8,128)(2,1)}, u32[]{:S(2)}, u32[]{:S(2)}) collective-permute-start(bf16[512,512]{1,0:T(8,128)(2,1)} %collective-permute-done.14.rest_1_), channel_id=1, source_target_pairs={{12,8},{20,16},{28,24},{13,9},{21,17},{29,25},{14,10},{22,18},{30,... | collective-permute-start | bytes 1572872 | tf_op jit(solution)/shard_map/ppermute | solution.py:211
  103.3 35.6 %collective-permute-start = (bf16[512,384]{1,0:T(8,128)(2,1)}, bf16[512,384]{1,0:T(8,128)(2,1)}, u32[]{:S(2)}, u32[]{:S(2)}) collective-permute-start(bf16[512,384]{1,0:T(8,128)(2,1)} %get-tuple-element.7), channel_id=1, source_target_pairs={{0,4},{4,0},{8,12},{12,8},{16,20},{20,16},{24,28},{28,24},{1,5},{5... | collective-permute-start | bytes 1179656 | tf_op jit(solution)/shard_map/ppermute | solution.py:211
  103.3 35.7 %collective-permute-start.6 = (bf16[512,384]{1,0:T(8,128)(2,1)}, bf16[512,384]{1,0:T(8,128)(2,1)}, u32[]{:S(2)}, u32[]{:S(2)}) collective-permute-start(bf16[512,384]{1,0:T(8,128)(2,1)} %collective-permute-done.2.rest_2_), channel_id=1, source_target_pairs={{8,0},{12,4},{16,8},{20,12},{9,1},{13,5},{17,9},{21,13},{10,2},{14... | collective-permute-start | bytes 1179656 | tf_op jit(solution)/shard_map/ppermute | solution.py:211
  105.2 35.4 %collective-permute-start.4 = (bf16[512,384]{1,0:T(8,128)(2,1)}, bf16[512,384]{1,0:T(8,128)(2,1)}, u32[]{:S(2)}, u32[]{:S(2)}) collective-permute-start(bf16[512,384]{1,0:T(8,128)(2,1)} %collective-permute-done.2.rest_2_), channel_id=1, source_target_pairs={{0,4},{8,12},{16,20},{1,5},{9,13},{17,21},{2,6},{10,14},{18,22},{3... | collective-permute-start | bytes 1179656 | tf_op jit(solution)/shard_map/ppermute | solution.py:211
  106.5 34.3 %collective-permute-start.5 = (bf16[512,384]{1,0:T(8,128)(2,1)}, bf16[512,384]{1,0:T(8,128)(2,1)}, u32[]{:S(2)}, u32[]{:S(2)}) collective-permute-start(bf16[512,384]{1,0:T(8,128)(2,1)} %collective-permute-done.1.rest_1_), channel_id=1, source_target_pairs={{8,16},{12,20},{16,24},{20,28},{9,17},{13,21},{17,25},{21,29},{10,... | collective-permute-start | bytes 1179656 | tf_op jit(solution)/shard_map/ppermute | solution.py:211
  112.0 29.2 %collective-permute-start.3 = (bf16[512,384]{1,0:T(8,128)(2,1)}, bf16[512,384]{1,0:T(8,128)(2,1)}, u32[]{:S(2)}, u32[]{:S(2)}) collective-permute-start(bf16[512,384]{1,0:T(8,128)(2,1)} %collective-permute-done.1.rest_1_), channel_id=1, source_target_pairs={{12,8},{20,16},{28,24},{13,9},{21,17},{29,25},{14,10},{22,18},{30,... | collective-permute-start | bytes 1179656 | tf_op jit(solution)/shard_map/ppermute | solution.py:211
  138.9 56.5 %collective-permute-start.12 = (bf16[384,1280]{1,0:T(8,128)(2,1)S(1)}, bf16[384,1280]{1,0:T(8,128)(2,1)S(1)}, u32[]{:S(2)}, u32[]{:S(2)}) collective-permute-start(bf16[384,1280]{1,0:T(8,128)(2,1)S(1)} %copy-done.18), channel_id=1, source_target_pairs={{0,3},{1,2},{2,1},{3,0},{4,7},{5,6},{6,5},{7,4},{8,11},{9,10},{10,... | collective-permute-start | bytes 2949128 | tf_op jit(solution)/shard_map/ppermute | solution.py:211
  139.0 56.4 %collective-permute-start.11 = (bf16[384,1280]{1,0:T(8,128)(2,1)S(1)}, bf16[384,1280]{1,0:T(8,128)(2,1)S(1)}, u32[]{:S(2)}, u32[]{:S(2)}) collective-permute-start(bf16[384,1280]{1,0:T(8,128)(2,1)S(1)} %copy-done.17), channel_id=1, source_target_pairs={{0,2},{1,3},{2,0},{3,1},{4,6},{5,7},{6,4},{7,5},{8,10},{9,11},{10,... | collective-permute-start | bytes 2949128 | tf_op jit(solution)/shard_map/ppermute | solution.py:211
  140.6 54.9 %collective-permute-start.10 = (bf16[384,1280]{1,0:T(8,128)(2,1)S(1)}, bf16[384,1280]{1,0:T(8,128)(2,1)S(1)}, u32[]{:S(2)}, u32[]{:S(2)}) collective-permute-start(bf16[384,1280]{1,0:T(8,128)(2,1)S(1)} %copy-done.16), channel_id=1, source_target_pairs={{0,1},{1,0},{2,3},{3,2},{4,5},{5,4},{6,7},{7,6},{8,9},{9,8},{10,11... | collective-permute-start | bytes 2949128 | tf_op jit(solution)/shard_map/ppermute | solution.py:211
  140.9 48.0 %collective-permute-start.28 = (bf16[256,1280]{1,0:T(8,128)(2,1)S(1)}, bf16[256,1280]{1,0:T(8,128)(2,1)S(1)}, u32[]{:S(2)}, u32[]{:S(2)}) collective-permute-start(bf16[256,1280]{1,0:T(8,128)(2,1)S(1)} %slice.19), channel_id=1, source_target_pairs={{0,1},{1,0},{2,3},{3,2},{4,5},{5,4},{6,7},{7,6},{8,9},{9,8},{10,11... | collective-permute-start | bytes 1966088 | tf_op jit(solution)/shard_map/ppermute | solution.py:211
  146.1 42.1 %collective-permute-start.9 = (bf16[256,384]{1,0:T(8,128)(2,1)S(1)}, bf16[256,384]{1,0:T(8,128)(2,1)S(1)}, u32[]{:S(2)}, u32[]{:S(2)}) collective-permute-start(bf16[256,384]{1,0:T(8,128)(2,1)S(1)} %attend.3.refs_0_), channel_id=1, source_target_pairs={{0,3},{1,2},{2,1},{3,0},{4,7},{5,6},{6,5},{7,4},{8,11},{9,10},{10,... | collective-permute-start | bytes 589832 | tf_op jit(solution)/shard_map/ppermute | solution.py:211
  195.2 17.1 %collective-permute-start.29 = (bf16[256,1280]{1,0:T(8,128)(2,1)S(1)}, bf16[256,1280]{1,0:T(8,128)(2,1)S(1)}, u32[]{:S(2)}, u32[]{:S(2)}) collective-permute-start(bf16[256,1280]{1,0:T(8,128)(2,1)S(1)} %add_convert_fusion), channel_id=1, source_target_pairs={{0,2},{1,3},{2,0},{3,1},{4,6},{5,7},{6,4},{7,5},{8,10},{9,11},{10,... | collective-permute-start | bytes 1966088 | tf_op jit(solution)/shard_map/ppermute | solution.py:211
  (27 other events, 237.4 us)

commit v2 on v0

v2 whole, which is shorter than its diff:
```python
import functools
import math

import jax
import jax.numpy as jnp
from jax import lax
from jax.experimental import pallas as pl
from jax.experimental.pallas import tpu as pltpu
from jax.sharding import PartitionSpec as P

HDIM = 128
BLK = 64
EXP_SCALE = math.log2(math.e) / math.sqrt(HDIM)
DEAD = -1e30
F32 = jnp.float32
BF16 = jnp.bfloat16


def offsets_for(frames):
    result = [0]
    step = 1
    while step <= frames // 2:
        result.append(step)
        result.append(-step)
        step = step * 2
    return result


def params(megabytes=56):
    return pltpu.CompilerParams(vmem_limit_bytes=megabytes << 20)


def send(x, axis, pairs):
    return lax.ppermute(x, axis, pairs)


def from_offset(x, frames, offset):
    return send(
        x, "frame", [(i + offset, i) for i in range(frames) if 0 <= i + offset < frames]
    )


def early_hops(x, frames):
    if frames != 8:
        return [from_offset(x, frames, o) for o in offsets_for(frames)[1:-2]]
    return [
        send(x, "frame", [(i, i ^ 2) for i in range(frames)]),
        send(x, "frame", [(i, i ^ 6) for i in (2, 3, 4, 5)]),
        send(x, "frame", [(i, i ^ 1) for i in range(frames)]),
    ]


def late_hops(x, hops, own, frames):
    if frames != 8:
        return [from_offset(x, frames, o) for o in offsets_for(frames)[-2:]]
    outer, inner, _ = hops
    across = jnp.where((own == 2) | (own == 5), inner, outer)
    return [
        send(outer, "frame", [(i, i ^ 6) for i in (2, 3, 4, 5)]),
        send(inner, "frame", [(i, i ^ 2) for i in (2, 3, 4, 5)]),
        send(across, "frame", [(i, i ^ 1) for i in (0, 2, 3, 4, 5, 7)]),
    ]


def plan(own, frames):
    if frames != 8:
        held = [own + o for o in offsets_for(frames)]
        return held[:-2], held[-2:], ((0,), (1,)), jnp.int32(0)
    middle = (own >= 2) & (own <= 5)
    even = own % 2 == 0
    early = [own, own ^ 2, jnp.where(middle, own ^ 6, -1), own ^ 1]
    late = [own ^ 4, jnp.where(even, own - 1, own + 1)]
    return early, late, ((0, 1), (2,)), middle.astype(jnp.int32)


def bias_of(held, live_blocks, frames, rows):
    blocks = rows // BLK
    lives = []
    for frame in held:
        inside = (frame >= 0) & (frame < frames)
        square = lax.dynamic_slice_in_dim(
            live_blocks, jnp.clip(frame, 0, frames - 1) * blocks, blocks, 1
        )
        lives.append(jnp.where(inside, square, 0))
    live = jnp.repeat(jnp.concatenate(lives, 1), BLK, 1)
    return jnp.where(live > 0, 0.0, DEAD).astype(F32)


def scores_of(q, key, bias_ref, n):
    rows = q.shape[0]
    s = lax.dot_general(q, key, (((1,), (1,)), ((), ())), preferred_element_type=F32)
    bias = [
        jnp.broadcast_to(bias_ref[b : b + 1, n * rows : (n + 1) * rows], (BLK, rows))
        for b in range(rows // BLK)
    ]
    return s + jnp.concatenate(bias, 0)


def early_kernel(count, q_ref, k_ref, v_ref, bias_ref, *rest):
    keys, values = rest[:count], rest[count : 2 * count]
    sum_ref, peak_ref, total_ref = rest[2 * count :]
    q = q_ref[...]
    scores = [lax.dot_general(q, k_ref[...], (((1,), (1,)), ((), ())), preferred_element_type=F32)]
    for n, ref in enumerate(keys):
        scores.append(scores_of(q, ref[...], bias_ref, n))
    peak = jnp.max(functools.reduce(jnp.maximum, scores), axis=1, keepdims=True)
    acc = None
    total = None
    for s, ref in zip(scores, [v_ref, *values]):
        e = jnp.exp2((s - peak) * EXP_SCALE)
        total = e if total is None else total + e
        part = jnp.dot(e.astype(BF16), ref[...], preferred_element_type=F32)
        acc = part if acc is None else acc + part
    total = jnp.sum(total, axis=1, keepdims=True)
    sum_ref[...] = acc
    peak_ref[...] = jnp.broadcast_to(peak, peak_ref.shape)
    total_ref[...] = jnp.broadcast_to(total, total_ref.shape)


def early_attention(queries, keys, values, bias, early_keys, early_values):
    rows, width = queries.shape
    head = pl.BlockSpec((rows, HDIM), lambda h: (0, h))
    count = len(early_keys)
    seen = rows * (count + 1)
    heads = width // HDIM
    return pl.pallas_call(
        functools.partial(early_kernel, count),
        out_shape=[jax.ShapeDtypeStruct((rows, width), F32)] * 3,
        grid=(heads,),
        in_specs=[head] * 3
        + [pl.BlockSpec(bias.shape, lambda h: (0, 0))]
        + [head] * (2 * count),
        out_specs=[head] * 3,
        compiler_params=params(),
        cost_estimate=pl.CostEstimate(
            flops=4 * heads * rows * seen * HDIM,
            bytes_accessed=4 * heads * seen * HDIM,
            transcendentals=heads * rows * seen,
        ),
        name="early_attention",
    )(queries, keys, values, bias, *early_keys, *early_values)


def pick(refs, group, flag_ref):
    if len(group) == 1:
        return refs[group[0]][...]
    one, two = (refs[g][...] for g in group)
    return jnp.where(flag_ref[0] > 0, one, two)


def late_kernel(groups, flag_ref, q_ref, bias_ref, sum_ref, peak_ref, total_ref, *rest):
    keys, weight_ref, scaled_ref = rest[:-2], rest[-2], rest[-1]
    q = q_ref[...]
    rows = q.shape[0]
    scores = [
        scores_of(q, pick(keys, group, flag_ref), bias_ref, n) for n, group in enumerate(groups)
    ]
    before = peak_ref[...]
    peak = jnp.max(functools.reduce(jnp.maximum, scores), axis=1, keepdims=True)
    peak = jnp.maximum(before[:, :1], peak)
    expos = [jnp.exp2((s - peak) * EXP_SCALE) for s in scores]
    total = jnp.sum(functools.reduce(jnp.add, expos), axis=1, keepdims=True)
    shrink = jnp.exp2((before[:, :1] - peak) * EXP_SCALE)
    total = total_ref[...][:, :1] * shrink + total
    over = 1.0 / total
    for n, e in enumerate(expos):
        weight_ref[:, n * rows : (n + 1) * rows] = (e * over).astype(BF16)
    scaled_ref[...] = sum_ref[...] * (shrink * over)


def late_weights(queries, bias, sums, peaks, totals, late_keys, groups, flag):
    rows, width = queries.shape
    head = pl.BlockSpec((rows, HDIM), lambda h, f: (0, h))
    heads = width // HDIM
    seen = rows * len(groups)
    return pl.pallas_call(
        functools.partial(late_kernel, groups),
        out_shape=[
            jax.ShapeDtypeStruct((rows, heads * seen), BF16),
            jax.ShapeDtypeStruct((rows, width), F32),
        ],
        grid_spec=pltpu.PrefetchScalarGridSpec(
            num_scalar_prefetch=1,
            grid=(heads,),
            in_specs=[head]
            + [pl.BlockSpec(bias.shape, lambda h, f: (0, 0))]
            + [head] * (3 + len(late_keys)),
            out_specs=[pl.BlockSpec((rows, seen), lambda h, f: (0, h)), head],
        ),
        compiler_params=params(),
        cost_estimate=pl.CostEstimate(
            flops=2 * heads * rows * seen * HDIM,
            bytes_accessed=4 * heads * seen * HDIM,
            transcendentals=heads * rows * seen,
        ),
        name="late_weights",
    )(flag, queries, bias, sums, peaks, totals, *late_keys)


def first_project_kernel(groups, count, flag_ref, pick_ref, scaled_ref, weights_ref, *rest):
    values = rest[:count]
    w_ref, out_ref, att_ref = rest[count:]
    rows, width = scaled_ref.shape
    seen = rows * len(groups)

    @pl.when((pl.program_id(0) == 0) & (pl.program_id(1) == 0))
    def _():
        for h in range(width // HDIM):
            columns = slice(h * HDIM, (h + 1) * HDIM)
            acc = scaled_ref[:, columns]
            for n, group in enumerate(groups):
                value = pick([ref.at[:, columns] for ref in values], group, flag_ref)
                weight = weights_ref[:, h * seen + n * rows : h * seen + (n + 1) * rows]
                acc += jnp.dot(weight, value, preferred_element_type=F32)
            att_ref[:, columns] = acc.astype(BF16)

    out_ref[...] = jnp.dot(att_ref[...], w_ref[...], preferred_element_type=F32).astype(BF16)


def first_project(scaled, weights, late_values, groups, flag, weight, picks, tile):
    rows, width = scaled.shape
    columns = weight.shape[1] // lax.axis_size("head")
    steps = columns // tile
    whole = lambda x: pl.BlockSpec(x.shape, lambda g, t, f, k: (0, 0))
    return pl.pallas_call(
        functools.partial(first_project_kernel, groups, len(late_values)),
        out_shape=[
            jax.ShapeDtypeStruct((picks.shape[0] * rows, columns), BF16),
            jax.ShapeDtypeStruct((rows, width), BF16),
        ],
        grid_spec=pltpu.PrefetchScalarGridSpec(
            num_scalar_prefetch=2,
            grid=(picks.shape[0], steps),
            in_specs=[whole(scaled), whole(weights)]
            + [whole(v) for v in late_values]
            + [pl.BlockSpec((width, tile), lambda g, t, f, k: (0, k[g] * steps + t))],
            out_specs=[
                pl.BlockSpec((rows, tile), lambda g, t, f, k: (g, t)),
                pl.BlockSpec((rows, width), lambda g, t, f, k: (0, 0)),
            ],
        ),
        compiler_params=params(),
        cost_estimate=pl.CostEstimate(
            flops=2 * rows * width * columns * picks.shape[0],
            bytes_accessed=2 * width * columns * picks.shape[0],
            transcendentals=0,
        ),
        name="first_project",
    )(flag, picks, scaled, weights, *late_values, weight)


def project_kernel(pick_ref, a_ref, w_ref, out_ref):
    out_ref[...] = jnp.dot(a_ref[...], w_ref[...], preferred_element_type=F32).astype(BF16)


def project(attended, weight, picks, tile):
    rows, width = attended.shape
    columns = weight.shape[1] // lax.axis_size("head")
    steps = columns // tile
    return pl.pallas_call(
        project_kernel,
        out_shape=jax.ShapeDtypeStruct((picks.shape[0] * rows, columns), BF16),
        grid_spec=pltpu.PrefetchScalarGridSpec(
            num_scalar_prefetch=1,
            grid=(picks.shape[0], steps),
            in_specs=[
                pl.BlockSpec((rows, width), lambda g, t, k: (0, 0)),
                pl.BlockSpec((width, tile), lambda g, t, k: (0, k[g] * steps + t)),
            ],
            out_specs=pl.BlockSpec((rows, tile), lambda g, t, k: (g, t)),
        ),
        compiler_params=params(),
        cost_estimate=pl.CostEstimate(
            flops=2 * rows * width * columns * picks.shape[0],
            bytes_accessed=2 * width * columns * picks.shape[0],
            transcendentals=0,
        ),
        name="project",
    )(picks, attended, weight)


def on_device(queries, key_vectors, value_vectors, live_blocks, out_weight):
    frames = lax.axis_size("frame")
    own = lax.axis_index("frame")
    group = lax.axis_index("head")
    rows = queries.shape[0]

    early, late, groups, flag = plan(own, frames)
    flag = flag[None]
    early_bias = bias_of(early[1:], live_blocks, frames, rows)
    late_bias = bias_of(late, live_blocks, frames, rows)

    early_keys = early_hops(key_vectors, frames)
    early_values = early_hops(value_vectors, frames)
    late_keys = late_hops(key_vectors, early_keys, own, frames)
    late_values = late_hops(value_vectors, early_values, own, frames)

    sums, peaks, totals = early_attention(
        queries, key_vectors, value_vectors, early_bias, early_keys, early_values
    )
    weights, scaled = late_weights(
        queries, late_bias, sums, peaks, totals, late_keys, groups, flag
    )

    swap = lambda x, bit: send(x, "head", [(g, g ^ bit) for g in range(4)])
    tile = out_weight.shape[1] // 8
    away, attended = first_project(
        scaled, weights, late_values, groups, flag, out_weight,
        jnp.stack([group ^ 3, group ^ 2]), tile,
    )
    near = project(attended, out_weight, jnp.stack([group ^ 1, group]), tile)
    crossed = (away[rows:].astype(F32) + swap(away[:rows], 1).astype(F32)).astype(BF16)
    from_far = swap(crossed, 2)
    from_near = swap(near[:rows], 1)
    total = near[rows:].astype(F32) + from_near.astype(F32) + from_far.astype(F32)
    return total.astype(BF16)


def solution(mesh):
    placed = (
        P("frame", "head"),
        P("frame", "head"),
        P("frame", "head"),
        P("frame", None),
        P("head", None),
    )
    return jax.shard_map(
        on_device, mesh=mesh, in_specs=placed, out_specs=P("frame", "head"), check_vma=False
    )
```

time: 271 us -> 121 us (0.45)
  waiting for transfers between devices: 183 us -> 45.6 us
  Pallas kernels: 0 us -> 36.9 us
  local copies, waits for them, and re-layouts: 41 us -> 5.55 us
  matrix products: 30.4 us -> 0 us
  starting transfers between devices: 0.08 us -> 27.8 us
  between operations: 13.3 us -> 0.29 us
    all_gather x2 -> x0, waiting for transfers between devices: 146 us -> none  [the longest x1 80.7 us: on_device(): lax.all_gather(value_vectors, 'frame', axis=0, tiled=True)]
    ppermute x0 -> x15, waiting for transfers between devices: none -> 45.6 us  [send(): return lax.ppermute(x, axis, pairs)]
    pallas_call x0 -> x4, Pallas kernels: none -> 36.9 us  [the longest x1 10.5 us: early_attention(): pl.pallas_call(functools.partial(early_kernel, count), out_shape=[jax.Sha...]
    reduce_scatter x1 -> x0, waiting for transfers between devices: 35.9 us -> none  [on_device(): lax.psum_scatter(partial_value.astype(jnp.bfloat16), 'head', scatter_dime...]
    ppermute x0 -> x15, starting transfers between devices: none -> 27.8 us  [send(): return lax.ppermute(x, axis, pairs)]
    unnamed x20, local copies, waits for them, and re-layouts: 27.8 us -> 1.68 us
    dot_general x2 -> x0, matrix products: 18.8 us -> none  [the longest x1 9.72 us: on_device(): jnp.dot(attended, out_weight, preferred_element_type=jnp.float32)]
    sub x1 -> x0, matrix products: 11.6 us -> none  [on_device(): expo = jnp.exp(scores - peak)]
  transfers between devices with their start and end apart: 3 -> 15, of which waited for: 3 -> 5; matrix products, arithmetic and copies ran while one was open for 10% -> 4% of each run, Pallas kernels for 0% -> 23%
where the time goes in v2:
time: 121 us; the launch traced here: 120 us
  waiting for transfers between devices  45.6 us (38%)
  Pallas kernels  36.9 us (30%)
  starting transfers between devices  27.8 us (23%)
  local copies, waits for them, and re-layouts  5.55 us (5%)
  other arithmetic  3.7 us (3%)
    ppermute x15, waiting for transfers between devices, send(): return lax.ppermute(x, axis, pairs)  45.6 us
    ppermute x15, starting transfers between devices, send(): return lax.ppermute(x, axis, pairs)  27.8 us
    pallas_call x1, Pallas kernels, early_attention(): pl.pallas_call(functools.partial(early_kernel, count), out_shape=[jax.Sha...  10.5 us
    pallas_call x1, Pallas kernels, late_weights(): pl.pallas_call(functools.partial(late_kernel, groups), out_shape=[jax.Sha...  10.4 us
    pallas_call x1, Pallas kernels, first_project(): pl.pallas_call(functools.partial(first_project_kernel, groups, len(late_v...  9.22 us
    pallas_call x1, Pallas kernels, project(): pl.pallas_call(project_kernel, out_shape=jax.ShapeDtypeStruct((picks.shap...  6.83 us
  transfers between devices with their start and end apart: 15, of which 5 were waited for; matrix products, arithmetic and copies ran while one was open for 4% of the time, Pallas kernels for 23%

profile of v2, /device:TPU:10, one launch (start us, length us, event | category | flops | bytes accessed | tf_op | source)
XLA Modules:
  0.0 119.9 jit_solution(1327799164974151294)
XLA Ops:
  0.5 4.6 %collective-permute-start.1 = (bf16[256,1280]{1,0:T(8,128)(2,1)}, bf16[256,1280]{1,0:T(8,128)(2,1)S(1)}, u32[]{:S(2)}, u32[]{:S(2)}) collective-permute-start(bf16[256,1280]{1,0:T(8,128)(2,1)} %k_ref.1), channel_id=1, source_target_pairs={{8,16},{12,20},{16,8},{20,12},{9,17},{13,21},{17,9},{21,13},{10,18... | collective-permute-start | bytes 1966088 | tf_op jit(solution)/shard_map/ppermute | solution.py:34
  5.1 1.9 %collective-permute-start.4 = (bf16[256,1280]{1,0:T(8,128)(2,1)}, bf16[256,1280]{1,0:T(8,128)(2,1)S(1)}, u32[]{:S(2)}, u32[]{:S(2)}) collective-permute-start(bf16[256,1280]{1,0:T(8,128)(2,1)} %v_ref.1), channel_id=1, source_target_pairs={{8,16},{12,20},{16,8},{20,12},{9,17},{13,21},{17,9},{21,13},{10,18... | collective-permute-start | bytes 1966088 | tf_op jit(solution)/shard_map/ppermute | solution.py:34
  7.7 10.2 %collective-permute-done.rest_0_ = bf16[256,1280]{1,0:T(8,128)(2,1)S(1)} collective-permute-done((bf16[256,1280]{1,0:T(8,128)(2,1)}, bf16[256,1280]{1,0:T(8,128)(2,1)S(1)}, u32[]{:S(2)}, u32[]{:S(2)}) %collective-permute-start) | collective-permute-done | bytes 655392 | tf_op jit(solution)/shard_map/ppermute | solution.py:34
  18.4 2.5 %collective-permute-done.1.rest_1_ = bf16[256,1280]{1,0:T(8,128)(2,1)S(1)} collective-permute-done((bf16[256,1280]{1,0:T(8,128)(2,1)}, bf16[256,1280]{1,0:T(8,128)(2,1)S(1)}, u32[]{:S(2)}, u32[]{:S(2)}) %collective-permute-start.1) | collective-permute-done | bytes 655392 | tf_op jit(solution)/shard_map/ppermute | solution.py:34
  20.9 2.6 %collective-permute-start.8 = (bf16[256,1280]{1,0:T(8,128)(2,1)S(1)}, bf16[256,1280]{1,0:T(8,128)(2,1)S(1)}, u32[]{:S(2)}, u32[]{:S(2)}) collective-permute-start(bf16[256,1280]{1,0:T(8,128)(2,1)S(1)} %broadcast_select_fusion.1), channel_id=1, source_target_pairs={{0,4},{8,12},{12,8},{16,20},{20,16},{28,24},{1,5},{9,13},{13,9},{1... | collective-permute-start | bytes 1966088 | tf_op jit(solution)/shard_map/ppermute | solution.py:34
  23.5 7.2 %collective-permute-done.3.rest_3_ = bf16[256,1280]{1,0:T(8,128)(2,1)S(1)} collective-permute-done((bf16[256,1280]{1,0:T(8,128)(2,1)}, bf16[256,1280]{1,0:T(8,128)(2,1)S(1)}, u32[]{:S(2)}, u32[]{:S(2)}) %collective-permute-start.3) | collective-permute-done | bytes 655392 | tf_op jit(solution)/shard_map/ppermute | solution.py:34
  30.7 3.5 %collective-permute-start.6 = (bf16[256,1280]{1,0:T(8,128)(2,1)S(1)}, bf16[256,1280]{1,0:T(8,128)(2,1)}, u32[]{:S(2)}, u32[]{:S(2)}) collective-permute-start(bf16[256,1280]{1,0:T(8,128)(2,1)S(1)} %collective-permute-done.rest_0_), channel_id=1, source_target_pairs={{8,16},{12,20},{16,8},{20,12},{9,17},{13,21},{17,9},{21,13},{10,18... | collective-permute-start | bytes 1966088 | tf_op jit(solution)/shard_map/ppermute | solution.py:34
  34.2 2.1 %collective-permute-start.7 = (bf16[256,1280]{1,0:T(8,128)(2,1)S(1)}, bf16[256,1280]{1,0:T(8,128)(2,1)}, u32[]{:S(2)}, u32[]{:S(2)}) collective-permute-start(bf16[256,1280]{1,0:T(8,128)(2,1)S(1)} %collective-permute-done.1.rest_1_), channel_id=1, source_target_pairs={{8,0},{12,4},{16,24},{20,28},{9,1},{13,5},{17,25},{21,29},{10,2},{... | collective-permute-start | bytes 1966088 | tf_op jit(solution)/shard_map/ppermute | solution.py:34
  36.4 0.9 broadcast_select_fusion
  37.3 2.4 %collective-permute-start.11 = (bf16[256,1280]{1,0:T(8,128)(2,1)}, bf16[256,1280]{1,0:T(8,128)(2,1)S(1)}, u32[]{:S(2)}, u32[]{:S(2)}) collective-permute-start(bf16[256,1280]{1,0:T(8,128)(2,1)} %broadcast_select_fusion), channel_id=1, source_target_pairs={{0,4},{8,12},{12,8},{16,20},{20,16},{28,24},{1,5},{9,13},{13,9},{1... | collective-permute-start | bytes 1966088 | tf_op jit(solution)/shard_map/ppermute | solution.py:34
  39.8 2.9 %collective-permute-start.10 = (bf16[256,1280]{1,0:T(8,128)(2,1)S(1)}, bf16[256,1280]{1,0:T(8,128)(2,1)}, u32[]{:S(2)}, u32[]{:S(2)}) collective-permute-start(bf16[256,1280]{1,0:T(8,128)(2,1)S(1)} %collective-permute-done.4.rest_4_), channel_id=1, source_target_pairs={{8,0},{12,4},{16,24},{20,28},{9,1},{13,5},{17,25},{21,29},{10,2},{... | collective-permute-start | bytes 1966088 | tf_op jit(solution)/shard_map/ppermute | solution.py:34
  42.6 10.5 %collective-permute-done.8.rest_2_ = bf16[256,1280]{1,0:T(8,128)(2,1)S(1)} collective-permute-done((bf16[256,1280]{1,0:T(8,128)(2,1)S(1)}, bf16[256,1280]{1,0:T(8,128)(2,1)S(1)}, u32[]{:S(2)}, u32[]{:S(2)}) %collective-permute-start.8) | collective-permute-done | bytes 655392 | tf_op jit(solution)/shard_map/ppermute | solution.py:34
  53.1 0.8 copy-done.8
  53.9 3.9 %collective-permute-start.9 = (bf16[256,1280]{1,0:T(8,128)(2,1)S(1)}, bf16[256,1280]{1,0:T(8,128)(2,1)}, u32[]{:S(2)}, u32[]{:S(2)}) collective-permute-start(bf16[256,1280]{1,0:T(8,128)(2,1)S(1)} %collective-permute-done.3.rest_3_), channel_id=1, source_target_pairs={{8,16},{12,20},{16,8},{20,12},{9,17},{13,21},{17,9},{21,13},{10,18... | collective-permute-start | bytes 1966088 | tf_op jit(solution)/shard_map/ppermute | solution.py:34
  60.4 10.5 %early_attention.1 = (f32[256,1280]{1,0:T(8,128)}, f32[256,1280]{1,0:T(8,128)}, f32[256,1280]{1,0:T(8,128)}) custom-call(bf16[256,1280]{1,0:T(8,128)(2,1)} %q_ref.3, bf16[256,1280]{1,0:T(8,128)(2,1)} %k_ref.1, bf16[256,1280]{1,0:T(8,128)(2,1)} %v_ref.1, f32[4,768]{1,0:T(4,128)} %select_n.106.bias_ref, bf16[256,1280]{1,0:T(8,128)(2,1)} %copy-done.3, ...), custom_call_target="tpu_custom_call" | custom-call | flops 1342177280 | bytes 5242880 | tf_op jit(solution)/shard_map/early_attention/pallas_call | solution.py:126
  70.8 10.4 %late_weights.1 = (bf16[256,5120]{1,0:T(8,128)(2,1)}, f32[256,1280]{1,0:T(8,128)}) custom-call(s32[1]{0:T(128)} %bitcast.2.flag_ref, bf16[256,1280]{1,0:T(8,128)(2,1)} %q_ref.3, f32[4,512]{1,0:T(4,128)} %select_n.94.bias_ref, f32[256,1280]{1,0:T(8,128)} %get-tuple-element.12.sum_ref, f32[256,1280]{1,0:T(8,128)} %get-tuple-element.13.peak_ref, ...), custom_call_target="tpu_custom_call" | custom-call | flops 335544320 | bytes 2621440 | tf_op jit(solution)/shard_map/late_weights/pallas_call | solution.py:176
  81.3 0.8 copy-done.6
  82.1 9.2 %first_project.1 = (bf16[512,1280]{1,0:T(8,128)(2,1)}, bf16[256,1280]{1,0:T(8,128)(2,1)}) custom-call(s32[1]{0:T(128)} %bitcast.2.flag_ref, s32[2]{0:T(128)} %pad_add_fusion.1.pick_ref, f32[256,1280]{1,0:T(8,128)} %get-tuple-element.15.scaled_ref, bf16[256,5120]{1,0:T(8,128)(2,1)} %get-tuple-element.16.weights_ref, ...), custom_call_target="tpu_custom_call" | custom-call | flops 1677721600 | bytes 6553600 | tf_op jit(solution)/shard_map/first_project/pallas_call | solution.py:225
  91.3 1.1 slice.15
  93.1 6.8 %project.1 = bf16[512,1280]{1,0:T(8,128)(2,1)} custom-call(s32[2]{0:T(128)} %pad_add_fusion.pick_ref, bf16[256,1280]{1,0:T(8,128)(2,1)} %get-tuple-element.17.a_ref, bf16[1280,5120]{1,0:T(8,128)(2,1)} %w_ref.1), custom_call_target="tpu_custom_call" | custom-call | flops 1677721600 | bytes 6553600 | tf_op jit(solution)/shard_map/project/pallas_call | solution.py:260
  100.0 1.2 %slice.17 = bf16[256,1280]{1,0:T(8,128)(2,1)S(1)} slice(bf16[512,1280]{1,0:T(8,128)(2,1)} %project.1), slice={[0:256], [0:1280]} | slice | bytes 1310720 | tf_op jit(solution)/shard_map/slice | solution.py:314
  101.9 1.6 %collective-permute-start.14 = (bf16[256,1280]{1,0:T(8,128)(2,1)S(1)}, bf16[256,1280]{1,0:T(8,128)(2,1)S(1)}, u32[]{:S(2)}, u32[]{:S(2)}) collective-permute-start(bf16[256,1280]{1,0:T(8,128)(2,1)S(1)} %add_convert_fusion.1), channel_id=1, source_target_pairs={{0,2},{1,3},{2,0},{3,1},{4,6},{5,7},{6,4},{7,5},{8,10},{9,11},{10,... | collective-permute-start | bytes 1966088 | tf_op jit(solution)/shard_map/ppermute | solution.py:34
  103.5 15.3 %collective-permute-done.14 = bf16[256,1280]{1,0:T(8,128)(2,1)S(1)} collective-permute-done((bf16[256,1280]{1,0:T(8,128)(2,1)S(1)}, bf16[256,1280]{1,0:T(8,128)(2,1)S(1)}, u32[]{:S(2)}, u32[]{:S(2)}) %collective-permute-start.14) | collective-permute-done | bytes 655392 | tf_op jit(solution)/shard_map/ppermute | solution.py:34
  118.8 1.1 add_convert_fusion
  (45 shorter events, 5.6 us)
Async XLA Ops:
  0.0 17.8 %collective-permute-start = (bf16[256,1280]{1,0:T(8,128)(2,1)}, bf16[256,1280]{1,0:T(8,128)(2,1)S(1)}, u32[]{:S(2)}, u32[]{:S(2)}) collective-permute-start(bf16[256,1280]{1,0:T(8,128)(2,1)} %k_ref.1), channel_id=1, source_target_pairs={{0,8},{4,12},{8,0},{12,4},{16,24},{20,28},{24,16},{28,20},{1,9},{5... | collective-permute-start | bytes 1966088 | tf_op jit(solution)/shard_map/ppermute | solution.py:34
  0.5 20.4 %collective-permute-start.1 = (bf16[256,1280]{1,0:T(8,128)(2,1)}, bf16[256,1280]{1,0:T(8,128)(2,1)S(1)}, u32[]{:S(2)}, u32[]{:S(2)}) collective-permute-start(bf16[256,1280]{1,0:T(8,128)(2,1)} %k_ref.1), channel_id=1, source_target_pairs={{8,16},{12,20},{16,8},{20,12},{9,17},{13,21},{17,9},{21,13},{10,18... | collective-permute-start | bytes 1966088 | tf_op jit(solution)/shard_map/ppermute | solution.py:34
  5.1 25.7 %collective-permute-start.3 = (bf16[256,1280]{1,0:T(8,128)(2,1)}, bf16[256,1280]{1,0:T(8,128)(2,1)S(1)}, u32[]{:S(2)}, u32[]{:S(2)}) collective-permute-start(bf16[256,1280]{1,0:T(8,128)(2,1)} %v_ref.1), channel_id=1, source_target_pairs={{0,8},{4,12},{8,0},{12,4},{16,24},{20,28},{24,16},{28,20},{1,9},{5... | collective-permute-start | bytes 1966088 | tf_op jit(solution)/shard_map/ppermute | solution.py:34
  5.1 29.1 %collective-permute-start.4 = (bf16[256,1280]{1,0:T(8,128)(2,1)}, bf16[256,1280]{1,0:T(8,128)(2,1)S(1)}, u32[]{:S(2)}, u32[]{:S(2)}) collective-permute-start(bf16[256,1280]{1,0:T(8,128)(2,1)} %v_ref.1), channel_id=1, source_target_pairs={{8,16},{12,20},{16,8},{20,12},{9,17},{13,21},{17,9},{21,13},{10,18... | collective-permute-start | bytes 1966088 | tf_op jit(solution)/shard_map/ppermute | solution.py:34
  7.1 30.2 %collective-permute-start.2 = (bf16[256,1280]{1,0:T(8,128)(2,1)}, bf16[256,1280]{1,0:T(8,128)(2,1)}, u32[]{:S(2)}, u32[]{:S(2)}) collective-permute-start(bf16[256,1280]{1,0:T(8,128)(2,1)} %k_ref.1), channel_id=1, source_target_pairs={{0,4},{4,0},{8,12},{12,8},{16,20},{20,16},{24,28},{28,24},{1,5},{5... | collective-permute-start | bytes 1966088 | tf_op jit(solution)/shard_map/ppermute | solution.py:34
  17.8 19.5 %copy-start.3 = (bf16[256,1280]{1,0:T(8,128)(2,1)}, bf16[256,1280]{1,0:T(8,128)(2,1)S(1)}, u32[]{:S(2)}) copy-start(bf16[256,1280]{1,0:T(8,128)(2,1)S(1)} %collective-permute-done.rest_0_) | copy-start | bytes 1966084
  17.8 21.9 %collective-permute-start.5 = (bf16[256,1280]{1,0:T(8,128)(2,1)}, bf16[256,1280]{1,0:T(8,128)(2,1)S(1)}, u32[]{:S(2)}, u32[]{:S(2)}) collective-permute-start(bf16[256,1280]{1,0:T(8,128)(2,1)} %v_ref.1), channel_id=1, source_target_pairs={{0,4},{4,0},{8,12},{12,8},{16,20},{20,16},{24,28},{28,24},{1,5},{5... | collective-permute-start | bytes 1966088 | tf_op jit(solution)/shard_map/ppermute | solution.py:34
  20.9 16.4 %copy-start.4 = (bf16[256,1280]{1,0:T(8,128)(2,1)}, bf16[256,1280]{1,0:T(8,128)(2,1)S(1)}, u32[]{:S(2)}) copy-start(bf16[256,1280]{1,0:T(8,128)(2,1)S(1)} %collective-permute-done.1.rest_1_) | copy-start | bytes 1966084
  20.9 37.0 %copy-start.9 = (s32[4,32]{1,0:T(4,128)S(1)}, s32[4,32]{1,0:T(4,128)}, u32[]{:S(2)}) copy-start(s32[4,32]{1,0:T(4,128)} %param.8) | copy-start | bytes 1540
  20.9 32.2 %collective-permute-start.8 = (bf16[256,1280]{1,0:T(8,128)(2,1)S(1)}, bf16[256,1280]{1,0:T(8,128)(2,1)S(1)}, u32[]{:S(2)}, u32[]{:S(2)}) collective-permute-start(bf16[256,1280]{1,0:T(8,128)(2,1)S(1)} %broadcast_select_fusion.1), channel_id=1, source_target_pairs={{0,4},{8,12},{12,8},{16,20},{20,16},{28,24},{1,5},{9,13},{13,9},{1... | collective-permute-start | bytes 1966088 | tf_op jit(solution)/shard_map/ppermute | solution.py:34
  30.7 29.6 %copy-start.1 = (bf16[256,1280]{1,0:T(8,128)(2,1)}, bf16[256,1280]{1,0:T(8,128)(2,1)S(1)}, u32[]{:S(2)}) copy-start(bf16[256,1280]{1,0:T(8,128)(2,1)S(1)} %collective-permute-done.3.rest_3_) | copy-start | bytes 1966084
  30.7 40.1 %collective-permute-start.6 = (bf16[256,1280]{1,0:T(8,128)(2,1)S(1)}, bf16[256,1280]{1,0:T(8,128)(2,1)}, u32[]{:S(2)}, u32[]{:S(2)}) collective-permute-start(bf16[256,1280]{1,0:T(8,128)(2,1)S(1)} %collective-permute-done.rest_0_), channel_id=1, source_target_pairs={{8,16},{12,20},{16,8},{20,12},{9,17},{13,21},{17,9},{21,13},{10,18... | collective-permute-start | bytes 1966088 | tf_op jit(solution)/shard_map/ppermute | solution.py:34
  34.2 26.1 %copy-start.2 = (bf16[256,1280]{1,0:T(8,128)(2,1)}, bf16[256,1280]{1,0:T(8,128)(2,1)S(1)}, u32[]{:S(2)}) copy-start(bf16[256,1280]{1,0:T(8,128)(2,1)S(1)} %collective-permute-done.4.rest_4_) | copy-start | bytes 1966084
  34.2 36.6 %collective-permute-start.7 = (bf16[256,1280]{1,0:T(8,128)(2,1)S(1)}, bf16[256,1280]{1,0:T(8,128)(2,1)}, u32[]{:S(2)}, u32[]{:S(2)}) collective-permute-start(bf16[256,1280]{1,0:T(8,128)(2,1)S(1)} %collective-permute-done.1.rest_1_), channel_id=1, source_target_pairs={{8,0},{12,4},{16,24},{20,28},{9,1},{13,5},{17,25},{21,29},{10,2},{... | collective-permute-start | bytes 1966088 | tf_op jit(solution)/shard_map/ppermute | solution.py:34
  37.3 43.9 %collective-permute-start.11 = (bf16[256,1280]{1,0:T(8,128)(2,1)}, bf16[256,1280]{1,0:T(8,128)(2,1)S(1)}, u32[]{:S(2)}, u32[]{:S(2)}) collective-permute-start(bf16[256,1280]{1,0:T(8,128)(2,1)} %broadcast_select_fusion), channel_id=1, source_target_pairs={{0,4},{8,12},{12,8},{16,20},{20,16},{28,24},{1,5},{9,13},{13,9},{1... | collective-permute-start | bytes 1966088 | tf_op jit(solution)/shard_map/ppermute | solution.py:34
  39.8 2.9 %copy-start.7 = (bf16[256,1280]{1,0:T(8,128)(2,1)}, bf16[256,1280]{1,0:T(8,128)(2,1)S(1)}, u32[]{:S(2)}) copy-start(bf16[256,1280]{1,0:T(8,128)(2,1)S(1)} %collective-permute-done.5.rest_5_) | copy-start | bytes 1966084
  39.8 41.5 %collective-permute-start.10 = (bf16[256,1280]{1,0:T(8,128)(2,1)S(1)}, bf16[256,1280]{1,0:T(8,128)(2,1)}, u32[]{:S(2)}, u32[]{:S(2)}) collective-permute-start(bf16[256,1280]{1,0:T(8,128)(2,1)S(1)} %collective-permute-done.4.rest_4_), channel_id=1, source_target_pairs={{8,0},{12,4},{16,24},{20,28},{9,1},{13,5},{17,25},{21,29},{10,2},{... | collective-permute-start | bytes 1966088 | tf_op jit(solution)/shard_map/ppermute | solution.py:34
  53.9 27.3 %collective-permute-start.9 = (bf16[256,1280]{1,0:T(8,128)(2,1)S(1)}, bf16[256,1280]{1,0:T(8,128)(2,1)}, u32[]{:S(2)}, u32[]{:S(2)}) collective-permute-start(bf16[256,1280]{1,0:T(8,128)(2,1)S(1)} %collective-permute-done.3.rest_3_), channel_id=1, source_target_pairs={{8,16},{12,20},{16,8},{20,12},{9,17},{13,21},{17,9},{21,13},{10,18... | collective-permute-start | bytes 1966088 | tf_op jit(solution)/shard_map/ppermute | solution.py:34
  81.2 0.8 copy-start.6
  92.4 9.3 %collective-permute-start.13 = (bf16[256,1280]{1,0:T(8,128)(2,1)S(1)}, bf16[256,1280]{1,0:T(8,128)(2,1)S(1)}, u32[]{:S(2)}, u32[]{:S(2)}) collective-permute-start(bf16[256,1280]{1,0:T(8,128)(2,1)S(1)} %slice.15), channel_id=1, source_target_pairs={{0,1},{1,0},{2,3},{3,2},{4,5},{5,4},{6,7},{7,6},{8,9},{9,8},{10,11... | collective-permute-start | bytes 1966088 | tf_op jit(solution)/shard_map/ppermute | solution.py:34
  100.0 1.8 %copy-start.5 = (bf16[512,1280]{1,0:T(8,128)(2,1)S(1)}, bf16[512,1280]{1,0:T(8,128)(2,1)}, u32[]{:S(2)}) copy-start(bf16[512,1280]{1,0:T(8,128)(2,1)} %get-tuple-element.18) | copy-start | bytes 3932164
  101.2 17.6 %copy-start = (bf16[512,1280]{1,0:T(8,128)(2,1)S(1)}, bf16[512,1280]{1,0:T(8,128)(2,1)}, u32[]{:S(2)}) copy-start(bf16[512,1280]{1,0:T(8,128)(2,1)} %project.1) | copy-start | bytes 3932164
  101.2 2.3 %collective-permute-start.12 = (bf16[256,1280]{1,0:T(8,128)(2,1)S(1)}, bf16[256,1280]{1,0:T(8,128)(2,1)S(1)}, u32[]{:S(2)}, u32[]{:S(2)}) collective-permute-start(bf16[256,1280]{1,0:T(8,128)(2,1)S(1)} %slice.17), channel_id=1, source_target_pairs={{0,1},{1,0},{2,3},{3,2},{4,5},{5,4},{6,7},{7,6},{8,9},{9,8},{10,11... | collective-permute-start | bytes 1966088 | tf_op jit(solution)/shard_map/ppermute | solution.py:34
  101.9 16.9 %collective-permute-start.14 = (bf16[256,1280]{1,0:T(8,128)(2,1)S(1)}, bf16[256,1280]{1,0:T(8,128)(2,1)S(1)}, u32[]{:S(2)}, u32[]{:S(2)}) collective-permute-start(bf16[256,1280]{1,0:T(8,128)(2,1)S(1)} %add_convert_fusion.1), channel_id=1, source_target_pairs={{0,2},{1,3},{2,0},{3,1},{4,6},{5,7},{6,4},{7,5},{8,10},{9,11},{10,... | collective-permute-start | bytes 1966088 | tf_op jit(solution)/shard_map/ppermute | solution.py:34
  (1 other events, 0.8 us)

commit v3 on v0

v3 whole, which is shorter than its diff:
```python
import functools
import math

import jax
import jax.numpy as jnp
from jax import lax
from jax.experimental import pallas as pl
from jax.experimental.pallas import tpu as pltpu
from jax.sharding import PartitionSpec as P

HDIM = 128
BLK = 64
EXP_SCALE = math.log2(math.e) / math.sqrt(HDIM)
DEAD = -1e30
F32 = jnp.float32
BF16 = jnp.bfloat16


def offsets_for(frames):
    result = [0]
    step = 1
    while step <= frames // 2:
        result.append(step)
        result.append(-step)
        step = step * 2
    return result


def send(x, axis, pairs):
    return lax.ppermute(x, axis, pairs)


def from_offset(x, frames, offset):
    return send(
        x, "frame", [(i + offset, i) for i in range(frames) if 0 <= i + offset < frames]
    )


def early_hops(x, frames):
    if frames != 8:
        return [from_offset(x, frames, o) for o in offsets_for(frames)[1:-2]]
    return [
        send(x, "frame", [(i, i ^ 2) for i in range(frames)]),
        send(x, "frame", [(i, i ^ 6) for i in (2, 3, 4, 5)]),
        send(x, "frame", [(i, i ^ 1) for i in range(frames)]),
    ]


def late_hops(x, hops, own, frames, hold):
    if frames != 8:
        return [from_offset(x, frames, o) for o in offsets_for(frames)[-2:]]
    outer, inner, _ = hops
    across = jnp.where((own == 2) | (own == 5), inner, outer)
    return [
        send(outer, "frame", [(i, i ^ 6) for i in (2, 3, 4, 5)]),
        send(inner, "frame", [(i, i ^ 2) for i in (2, 3, 4, 5)]),
        send(hold(across), "frame", [(i, i ^ 1) for i in (0, 2, 3, 4, 5, 7)]),
    ]


def plan(own, frames):
    if frames != 8:
        held = [own + o for o in offsets_for(frames)]
        return held[:-2], held[-2:], ((0,), (1,)), own >= 0
    middle = (own >= 2) & (own <= 5)
    odd = lax.rem(own, 2)
    flip = 1 - 2 * odd
    low = lax.rem(lax.div(own, 2), 2)
    outer = own + 2 - 4 * low
    early = [own, outer, jnp.where(middle, own - 2 + 4 * low, -1), own + flip]
    late = [jnp.where(own >= 4, own - 4, own + 4), own - flip]
    return early, late, ((0, 1), (2,)), middle


def params():
    return pltpu.CompilerParams(vmem_limit_bytes=20 << 20)


VMEM = pl.BlockSpec(memory_space=pltpu.VMEM)
SMEM = pl.BlockSpec(memory_space=pltpu.SMEM)


def fill_bias(bias_ref, live_ref, held, frames):
    blocks = live_ref.shape[0]
    left = lax.broadcasted_iota(jnp.int32, (8, 2 * BLK), 1) < BLK
    for n, frame in enumerate(held):
        inside = (frame >= 0) & (frame < frames)
        base = jnp.where(inside, frame, 0) * blocks
        for b in range(blocks):
            for c in range(0, blocks, 2):
                one, two = (
                    jnp.where(inside & (live_ref[b, base + c + d] > 0), 0.0, DEAD).astype(F32)
                    for d in (0, 1)
                )
                at = n * blocks * BLK + c * BLK
                bias_ref[8 * b : 8 * b + 8, at : at + 2 * BLK] = jnp.where(left, one, two)


def scores_of(q, key, bias_ref, n):
    rows = q.shape[0]
    s = lax.dot_general(q, key, (((1,), (1,)), ((), ())), preferred_element_type=F32)
    if bias_ref is None:
        return s
    parts = []
    for b in range(rows // BLK):
        bias = bias_ref[8 * b : 8 * b + 8, n * rows : (n + 1) * rows]
        part = s[b * BLK : (b + 1) * BLK].reshape(BLK // 8, 8, rows) + bias[None]
        parts.append(part.reshape(BLK, rows))
    return jnp.concatenate(parts, 0)


def each_head(heads, body, unroll):
    def some(step, _):
        for n in range(unroll):
            h = step * unroll + n
            body(h, pl.ds(pl.multiple_of(h * HDIM, HDIM), HDIM))
        return 0

    lax.fori_loop(0, heads // unroll, some, 0)


def early_kernel(count, live_ref, q_ref, k_ref, v_ref, *rest):
    keys, values = (k_ref, *rest[:count]), (v_ref, *rest[count : 2 * count])
    sum_ref, peak_ref, total_ref, bias_ref = rest[2 * count :]
    frames = lax.axis_size("frame")
    held = plan(lax.axis_index("frame"), frames)[0]
    fill_bias(bias_ref, live_ref, held[1:], frames)

    def head(h, columns):
        q = q_ref[:, columns]
        scores = []
        for n, ref in enumerate(keys):
            scores.append(scores_of(q, ref[:, columns], bias_ref if n else None, n - 1))
        peak = jnp.max(functools.reduce(jnp.maximum, scores), axis=1, keepdims=True)
        acc = None
        total = None
        for s, ref in zip(scores, values):
            e = jnp.exp2((s - peak) * EXP_SCALE)
            total = e if total is None else total + e
            part = jnp.dot(e.astype(BF16), ref[:, columns], preferred_element_type=F32)
            acc = part if acc is None else acc + part
        sum_ref[:, columns] = acc
        peak_ref[:, columns] = jnp.broadcast_to(peak, acc.shape)
        total_ref[:, columns] = jnp.broadcast_to(
            jnp.sum(total, axis=1, keepdims=True), acc.shape
        )

    each_head(q_ref.shape[1] // HDIM, head, 2)


def early_attention(live_blocks, queries, keys, values, early_keys, early_values):
    rows, width = queries.shape
    count = len(early_keys)
    seen = rows * (count + 1)
    heads = width // HDIM
    return pl.pallas_call(
        functools.partial(early_kernel, count),
        out_shape=[jax.ShapeDtypeStruct((rows, width), F32)] * 3,
        in_specs=[SMEM] + [VMEM] * (3 + 2 * count),
        out_specs=[VMEM] * 3,
        scratch_shapes=[pltpu.VMEM((8 * rows // BLK, count * rows), F32)],
        compiler_params=params(),
        cost_estimate=pl.CostEstimate(
            flops=4 * heads * rows * seen * HDIM,
            bytes_accessed=4 * heads * seen * HDIM,
            transcendentals=heads * rows * seen,
        ),
        name="early_attention",
    )(live_blocks, queries, keys, values, *early_keys, *early_values)


def pick(refs, group, columns, first):
    if len(group) == 1:
        return refs[group[0]][:, columns]
    one, two = (refs[g][:, columns] for g in group)
    return jnp.where(first, one, two)


def late_kernel(live_ref, q_ref, sum_ref, peak_ref, total_ref, *rest):
    keys, (weight_ref, scaled_ref, bias_ref) = rest[:-3], rest[-3:]
    frames = lax.axis_size("frame")
    _, held, groups, first = plan(lax.axis_index("frame"), frames)
    rows = q_ref.shape[0]
    seen = rows * len(groups)
    fill_bias(bias_ref, live_ref, held, frames)

    def head(h, columns):
        q = q_ref[:, columns]
        scores = [
            scores_of(q, pick(keys, group, columns, first), bias_ref, n)
            for n, group in enumerate(groups)
        ]
        before = peak_ref[:, columns]
        peak = jnp.max(functools.reduce(jnp.maximum, scores), axis=1, keepdims=True)
        peak = jnp.maximum(before, jnp.broadcast_to(peak, before.shape))
        expos = []
        for s in scores:
            for c in range(0, rows, HDIM):
                expos.append(jnp.exp2((s[:, c : c + HDIM] - peak) * EXP_SCALE))
        total = jnp.sum(functools.reduce(jnp.add, expos), axis=1, keepdims=True)
        shrink = jnp.exp2((before - peak) * EXP_SCALE)
        over = 1.0 / (total_ref[:, columns] * shrink + jnp.broadcast_to(total, before.shape))
        for n, e in enumerate(expos):
            at = pl.multiple_of(h * seen + n * HDIM, HDIM)
            weight_ref[:, pl.ds(at, HDIM)] = (e * over).astype(BF16)
        scaled_ref[:, columns] = sum_ref[:, columns] * (shrink * over)

    each_head(q_ref.shape[1] // HDIM, head, 2)


def late_weights(live_blocks, queries, sums, peaks, totals, late_keys, places):
    rows, width = queries.shape
    heads = width // HDIM
    seen = rows * places
    return pl.pallas_call(
        late_kernel,
        out_shape=[
            jax.ShapeDtypeStruct((rows, heads * seen), BF16),
            jax.ShapeDtypeStruct((rows, width), F32),
        ],
        in_specs=[SMEM] + [VMEM] * (4 + len(late_keys)),
        out_specs=[VMEM] * 2,
        scratch_shapes=[pltpu.VMEM((8 * rows // BLK, seen), F32)],
        compiler_params=params(),
        cost_estimate=pl.CostEstimate(
            flops=2 * heads * rows * seen * HDIM,
            bytes_accessed=4 * heads * seen * HDIM,
            transcendentals=heads * rows * seen,
        ),
        name="late_weights",
    )(live_blocks, queries, sums, peaks, totals, *late_keys)


def multiply(a_ref, w_ref, out_ref, group):
    width = out_ref.shape[1]
    step = width // 5 if width % (5 * HDIM) == 0 else width
    for n in range(0, width, step):
        columns = pl.ds(pl.multiple_of(group * width + n, HDIM), step)
        out_ref[:, n : n + step] = jnp.dot(
            a_ref[...], w_ref[:, columns], preferred_element_type=F32
        ).astype(BF16)


def first_project_kernel(count, scaled_ref, weights_ref, *rest):
    values = rest[:count]
    w_ref, out_ref, att_ref = rest[count:]
    rows, width = scaled_ref.shape
    _, _, groups, first = plan(lax.axis_index("frame"), lax.axis_size("frame"))
    seen = rows * len(groups)
    for h in range(width // HDIM):
        columns = slice(h * HDIM, (h + 1) * HDIM)
        acc = scaled_ref[:, columns]
        for n, group in enumerate(groups):
            value = pick(values, group, columns, first)
            weight = weights_ref[:, h * seen + n * rows : h * seen + (n + 1) * rows]
            acc += jnp.dot(weight, value, preferred_element_type=F32)
        att_ref[:, columns] = acc.astype(BF16)
    multiply(att_ref, w_ref, out_ref, lax.axis_index("head") ^ 3)


def project_cost(rows, width, columns, count):
    return pl.CostEstimate(
        flops=2 * rows * width * columns * count,
        bytes_accessed=2 * width * columns * count,
        transcendentals=0,
    )


def first_project(scaled, weights, late_values, weight):
    rows, width = scaled.shape
    columns = weight.shape[1] // lax.axis_size("head")
    return pl.pallas_call(
        functools.partial(first_project_kernel, len(late_values)),
        out_shape=[
            jax.ShapeDtypeStruct((rows, columns), BF16),
            jax.ShapeDtypeStruct((rows, width), BF16),
        ],
        in_specs=[VMEM] * (3 + len(late_values)),
        out_specs=[VMEM] * 2,
        compiler_params=params(),
        cost_estimate=project_cost(rows, width, columns, 1),
        name="first_project",
    )(scaled, weights, *late_values, weight)


def project_kernel(bits, a_ref, w_ref, *outs):
    for bit, out_ref in zip(bits, outs):
        multiply(a_ref, w_ref, out_ref, lax.axis_index("head") ^ bit)


def project(attended, weight, bits):
    rows, width = attended.shape
    columns = weight.shape[1] // lax.axis_size("head")
    return pl.pallas_call(
        functools.partial(project_kernel, bits),
        out_shape=[jax.ShapeDtypeStruct((rows, columns), BF16)] * len(bits),
        in_specs=[VMEM] * 2,
        out_specs=[VMEM] * len(bits),
        compiler_params=params(),
        cost_estimate=project_cost(rows, width, columns, len(bits)),
        name="project",
    )(attended, weight)


def after(x, *others):
    return lax.optimization_barrier((x, *others))[0]


def on_device(queries, key_vectors, value_vectors, live_blocks, out_weight):
    frames = lax.axis_size("frame")
    own = lax.axis_index("frame")

    early_keys = early_hops(key_vectors, frames)
    early_values = early_hops(value_vectors, frames)
    late_keys = late_hops(key_vectors, early_keys, own, frames, lambda x: after(x, early_values[0]))

    sums, peaks, totals = early_attention(
        live_blocks, queries, key_vectors, value_vectors, early_keys, early_values
    )
    late_values = late_hops(value_vectors, early_values, own, frames, lambda x: after(x, sums))
    places = 2
    weights, scaled = late_weights(
        live_blocks, queries, sums, peaks, totals, late_keys, places
    )

    swap = lambda x, bit: send(x, "head", [(g, g ^ bit) for g in range(4)])
    for_sibling, attended = first_project(scaled, weights, late_values, out_weight)
    (mine,) = project(attended, out_weight, (2,))
    crossed = (mine.astype(F32) + swap(for_sibling, 1).astype(F32)).astype(BF16)
    from_far = swap(crossed, 2)
    near, total = project(after(attended, crossed), out_weight, (1, 0))
    from_near = swap(near, 1)
    total = total.astype(F32) + from_near.astype(F32) + from_far.astype(F32)
    return total.astype(BF16)


def solution(mesh):
    placed = (
        P("frame", "head"),
        P("frame", "head"),
        P("frame", "head"),
        P("frame", None),
        P("head", None),
    )
    return jax.shard_map(
        on_device, mesh=mesh, in_specs=placed, out_specs=P("frame", "head"), check_vma=False
    )
```

time: 271 us -> 94.1 us (0.35)
  the two profiles are of different devices: /device:TPU:10 before, /device:TPU:0 now
where the time goes in v3:
time: 94.1 us; the launch traced here: 93.8 us
  waiting for transfers between devices  50.9 us (54%)
  starting transfers between devices  26.1 us (28%)
  Pallas kernels  15.2 us (16%)
  other arithmetic  1.4 us (1%)
    ppermute x15, waiting for transfers between devices, send(): return lax.ppermute(x, axis, pairs)  50.9 us
    ppermute x15, starting transfers between devices, send(): return lax.ppermute(x, axis, pairs)  26.1 us
    pallas_call x1, Pallas kernels, early_attention(): pl.pallas_call(functools.partial(early_kernel, count), out_shape=[jax.Sha...  6.33 us
    pallas_call x1, Pallas kernels, late_weights(): pl.pallas_call(late_kernel, out_shape=[jax.ShapeDtypeStruct((rows, heads...  3.95 us
    pallas_call x2, Pallas kernels, project(): pl.pallas_call(functools.partial(project_kernel, bits), out_shape=[jax.Sh...  3 us
    pallas_call x1, Pallas kernels, first_project(): pl.pallas_call(functools.partial(first_project_kernel, len(late_values)),...  1.93 us
  transfers between devices with their start and end apart: 15, of which 10 were waited for; matrix products, arithmetic and copies ran while one was open for 0% of the time, Pallas kernels for 12%

profile of v3, /device:TPU:0, one launch (start us, length us, event | category | flops | bytes accessed | tf_op | source)
XLA Modules:
  0.0 93.8 jit_solution(417438615268064949)
XLA Ops:
  0.0 3.0 %collective-permute-start = (bf16[256,1280]{1,0:T(8,128)(2,1)}, bf16[256,1280]{1,0:T(8,128)(2,1)S(1)}, u32[]{:S(2)}, u32[]{:S(2)}) collective-permute-start(bf16[256,1280]{1,0:T(8,128)(2,1)} %k_ref.1), channel_id=1, source_target_pairs={{0,8},{4,12},{8,0},{12,4},{16,24},{20,28},{24,16},{28,20},{1,9},{5... | collective-permute-start | bytes 1966088 | tf_op jit(solution)/shard_map/ppermute | solution.py:30
  3.7 4.4 %collective-permute-start.3 = (bf16[256,1280]{1,0:T(8,128)(2,1)}, bf16[256,1280]{1,0:T(8,128)(2,1)S(1)}, u32[]{:S(2)}, u32[]{:S(2)}) collective-permute-start(bf16[256,1280]{1,0:T(8,128)(2,1)} %v_ref.1), channel_id=1, source_target_pairs={{0,8},{4,12},{8,0},{12,4},{16,24},{20,28},{24,16},{28,20},{1,9},{5... | collective-permute-start | bytes 1966088 | tf_op jit(solution)/shard_map/ppermute | solution.py:30
  8.8 1.6 %collective-permute-start.2 = (bf16[256,1280]{1,0:T(8,128)(2,1)}, bf16[256,1280]{1,0:T(8,128)(2,1)S(1)}, u32[]{:S(2)}, u32[]{:S(2)}) collective-permute-start(bf16[256,1280]{1,0:T(8,128)(2,1)} %k_ref.1), channel_id=1, source_target_pairs={{0,4},{4,0},{8,12},{12,8},{16,20},{20,16},{24,28},{28,24},{1,5},{5... | collective-permute-start | bytes 1966088 | tf_op jit(solution)/shard_map/ppermute | solution.py:30
  10.4 8.4 %collective-permute-done.rest_0_ = bf16[256,1280]{1,0:T(8,128)(2,1)S(1)} collective-permute-done((bf16[256,1280]{1,0:T(8,128)(2,1)}, bf16[256,1280]{1,0:T(8,128)(2,1)S(1)}, u32[]{:S(2)}, u32[]{:S(2)}) %collective-permute-start) | collective-permute-done | bytes 655392 | tf_op jit(solution)/shard_map/ppermute | solution.py:30
  18.8 2.0 %collective-permute-start.5 = (bf16[256,1280]{1,0:T(8,128)(2,1)}, bf16[256,1280]{1,0:T(8,128)(2,1)S(1)}, u32[]{:S(2)}, u32[]{:S(2)}) collective-permute-start(bf16[256,1280]{1,0:T(8,128)(2,1)} %v_ref.1), channel_id=1, source_target_pairs={{0,4},{4,0},{8,12},{12,8},{16,20},{20,16},{24,28},{28,24},{1,5},{5... | collective-permute-start | bytes 1966088 | tf_op jit(solution)/shard_map/ppermute | solution.py:30
  20.9 11.1 %collective-permute-done.3.rest_3_ = bf16[256,1280]{1,0:T(8,128)(2,1)S(1)} collective-permute-done((bf16[256,1280]{1,0:T(8,128)(2,1)}, bf16[256,1280]{1,0:T(8,128)(2,1)S(1)}, u32[]{:S(2)}, u32[]{:S(2)}) %collective-permute-start.3) | collective-permute-done | bytes 655392 | tf_op jit(solution)/shard_map/ppermute | solution.py:30
  32.0 3.6 %collective-permute-start.8 = (bf16[256,1280]{1,0:T(8,128)(2,1)S(1)}, bf16[256,1280]{1,0:T(8,128)(2,1)S(1)}, u32[]{:S(2)}, u32[]{:S(2)}) collective-permute-start(bf16[256,1280]{1,0:T(8,128)(2,1)S(1)} %broadcast_select_fusion.1), channel_id=1, source_target_pairs={{0,4},{8,12},{12,8},{16,20},{20,16},{28,24},{1,5},{9,13},{13,9},{1... | collective-permute-start | bytes 1966088 | tf_op jit(solution)/shard_map/ppermute | solution.py:30
  35.6 0.7 collective-permute-start.6
  36.3 1.3 %collective-permute-start.7 = (bf16[256,1280]{1,0:T(8,128)(2,1)S(1)}, bf16[256,1280]{1,0:T(8,128)(2,1)S(1)}, u32[]{:S(2)}, u32[]{:S(2)}) collective-permute-start(bf16[256,1280]{1,0:T(8,128)(2,1)S(1)} %collective-permute-done.1.rest_1_), channel_id=1, source_target_pairs={{8,0},{12,4},{16,24},{20,28},{9,1},{13,5},{17,25},{21,29},{10,2},{... | collective-permute-start | bytes 1966088 | tf_op jit(solution)/shard_map/ppermute | solution.py:30
  37.7 2.2 %collective-permute-done.5.rest_5_ = bf16[256,1280]{1,0:T(8,128)(2,1)S(1)} collective-permute-done((bf16[256,1280]{1,0:T(8,128)(2,1)}, bf16[256,1280]{1,0:T(8,128)(2,1)S(1)}, u32[]{:S(2)}, u32[]{:S(2)}) %collective-permute-start.5) | collective-permute-done | bytes 655392 | tf_op jit(solution)/shard_map/ppermute | solution.py:30
  40.0 6.3 %early_attention.1 = (f32[256,1280]{1,0:T(8,128)S(1)}, f32[256,1280]{1,0:T(8,128)S(1)}, f32[256,1280]{1,0:T(8,128)S(1)}) custom-call(s32[4,32]{1,0:T(4,128)S(1)} %copy-done.4, bf16[256,1280]{1,0:T(8,128)(2,1)S(1)} %copy-done.1, bf16[256,1280]{1,0:T(8,128)(2,1)S(1)} %copy-done.2, bf16[256,1280]{1,0:T(8,128)(2,1)S(1)} %copy-done.3, ...), custom_call_target="tpu_custom_call" | custom-call | flops 1342177280 | bytes 5242880 | tf_op jit(solution)/shard_map/early_attention/pallas_call | solution.py:156
  46.3 4.3 %collective-permute-start.11 = (bf16[256,1280]{1,0:T(8,128)(2,1)S(1)}, bf16[256,1280]{1,0:T(8,128)(2,1)S(1)}, u32[]{:S(2)}, u32[]{:S(2)}) collective-permute-start(bf16[256,1280]{1,0:T(8,128)(2,1)S(1)} %broadcast_select_fusion), channel_id=1, source_target_pairs={{0,4},{8,12},{12,8},{16,20},{20,16},{28,24},{1,5},{9,13},{13,9},{1... | collective-permute-start | bytes 1966088 | tf_op jit(solution)/shard_map/ppermute | solution.py:30
  51.3 2.5 %collective-permute-done.8.rest_2_ = bf16[256,1280]{1,0:T(8,128)(2,1)S(1)} collective-permute-done((bf16[256,1280]{1,0:T(8,128)(2,1)S(1)}, bf16[256,1280]{1,0:T(8,128)(2,1)S(1)}, u32[]{:S(2)}, u32[]{:S(2)}) %collective-permute-start.8) | collective-permute-done | bytes 655392 | tf_op jit(solution)/shard_map/ppermute | solution.py:30
  53.9 1.3 %collective-permute-start.10 = (bf16[256,1280]{1,0:T(8,128)(2,1)S(1)}, bf16[256,1280]{1,0:T(8,128)(2,1)S(1)}, u32[]{:S(2)}, u32[]{:S(2)}) collective-permute-start(bf16[256,1280]{1,0:T(8,128)(2,1)S(1)} %collective-permute-done.4.rest_4_), channel_id=1, source_target_pairs={{8,0},{12,4},{16,24},{20,28},{9,1},{13,5},{17,25},{21,29},{10,2},{... | collective-permute-start | bytes 1966088 | tf_op jit(solution)/shard_map/ppermute | solution.py:30
  55.5 3.9 %late_weights.1 = (bf16[256,5120]{1,0:T(8,128)(2,1)S(1)}, f32[256,1280]{1,0:T(8,128)S(1)}) custom-call(s32[4,32]{1,0:T(4,128)S(1)} %copy-done.4, bf16[256,1280]{1,0:T(8,128)(2,1)S(1)} %copy-done.1, f32[256,1280]{1,0:T(8,128)S(1)} %get-tuple-element.17.sum_ref, f32[256,1280]{1,0:T(8,128)S(1)} %get-tuple-element.18.peak_ref, ...), custom_call_target="tpu_custom_call" | custom-call | flops 335544320 | bytes 2621440 | tf_op jit(solution)/shard_map/late_weights/pallas_call | solution.py:215
  59.5 6.4 %collective-permute-done.11.rest_2_ = bf16[256,1280]{1,0:T(8,128)(2,1)S(1)} collective-permute-done((bf16[256,1280]{1,0:T(8,128)(2,1)S(1)}, bf16[256,1280]{1,0:T(8,128)(2,1)S(1)}, u32[]{:S(2)}, u32[]{:S(2)}) %collective-permute-start.11) | collective-permute-done | bytes 655392 | tf_op jit(solution)/shard_map/ppermute | solution.py:30
  65.9 3.4 %collective-permute-done.10.rest_1_ = bf16[256,1280]{1,0:T(8,128)(2,1)S(1)} collective-permute-done((bf16[256,1280]{1,0:T(8,128)(2,1)S(1)}, bf16[256,1280]{1,0:T(8,128)(2,1)S(1)}, u32[]{:S(2)}, u32[]{:S(2)}) %collective-permute-start.10) | collective-permute-done | bytes 655392 | tf_op jit(solution)/shard_map/ppermute | solution.py:30
  69.3 1.9 %first_project.1 = (bf16[256,1280]{1,0:T(8,128)(2,1)S(1)}, bf16[256,1280]{1,0:T(8,128)(2,1)S(1)}) custom-call(f32[256,1280]{1,0:T(8,128)S(1)} %get-tuple-element.21.scaled_ref, bf16[256,5120]{1,0:T(8,128)(2,1)S(1)} %get-tuple-element.22.weights_ref, bf16[256,1280]{1,0:T(8,128)(2,1)S(1)} %collective-permute-done.9.rest_0_, ...), custom_call_target="tpu_custom_call" | custom-call | flops 838860800 | bytes 3276800 | tf_op jit(solution)/shard_map/first_project/pallas_call | solution.py:272
  71.3 1.1 %project.2 = bf16[256,1280]{1,0:T(8,128)(2,1)S(1)} custom-call(bf16[256,1280]{1,0:T(8,128)(2,1)S(1)} %get-tuple-element.26.a_ref, bf16[1280,5120]{1,0:T(8,128)(2,1)S(1)} %copy-done), custom_call_target="tpu_custom_call" | custom-call | flops 838860800 | bytes 3276800 | tf_op jit(solution)/shard_map/project/pallas_call | solution.py:294
  72.4 1.0 %collective-permute-done.12 = bf16[256,1280]{1,0:T(8,128)(2,1)S(1)} collective-permute-done((bf16[256,1280]{1,0:T(8,128)(2,1)S(1)}, bf16[256,1280]{1,0:T(8,128)(2,1)S(1)}, u32[]{:S(2)}, u32[]{:S(2)}) %collective-permute-start.12) | collective-permute-done | bytes 655392 | tf_op jit(solution)/shard_map/ppermute | solution.py:30
  73.5 1.9 %project.3 = (bf16[256,1280]{1,0:T(8,128)(2,1)S(1)}, bf16[256,1280]{1,0:T(8,128)(2,1)S(1)}) custom-call(bf16[256,1280]{1,0:T(8,128)(2,1)S(1)} %get-tuple-element.26.a_ref, bf16[1280,5120]{1,0:T(8,128)(2,1)S(1)} %copy-done), custom_call_target="tpu_custom_call" | custom-call | flops 1677721600 | bytes 6553600 | tf_op jit(solution)/shard_map/project/pallas_call | solution.py:294
  75.7 1.5 %collective-permute-start.14 = (bf16[256,1280]{1,0:T(8,128)(2,1)S(1)}, bf16[256,1280]{1,0:T(8,128)(2,1)S(1)}, u32[]{:S(2)}, u32[]{:S(2)}) collective-permute-start(bf16[256,1280]{1,0:T(8,128)(2,1)S(1)} %add_convert_fusion.1), channel_id=1, source_target_pairs={{0,2},{1,3},{2,0},{3,1},{4,6},{5,7},{6,4},{7,5},{8,10},{9,11},{10,... | collective-permute-start | bytes 1966088 | tf_op jit(solution)/shard_map/ppermute | solution.py:30
  77.6 15.1 %collective-permute-done.14 = bf16[256,1280]{1,0:T(8,128)(2,1)S(1)} collective-permute-done((bf16[256,1280]{1,0:T(8,128)(2,1)S(1)}, bf16[256,1280]{1,0:T(8,128)(2,1)S(1)}, u32[]{:S(2)}, u32[]{:S(2)}) %collective-permute-start.14) | collective-permute-done | bytes 655392 | tf_op jit(solution)/shard_map/ppermute | solution.py:30
  92.7 1.1 %add_convert_fusion = bf16[256,1280]{1,0:T(8,128)(2,1)} fusion(bf16[256,1280]{1,0:T(8,128)(2,1)S(1)} %collective-permute-done.14, bf16[256,1280]{1,0:T(8,128)(2,1)S(1)} %collective-permute-done.13, bf16[256,1280]{1,0:T(8,128)(2,1)S(1)} %get-tuple-element.27), kind=kLoop, calls=%fused_computation | loop fusion | flops 1966080 | bytes 2621440 | tf_op jit(solution)/shard_map/convert_element_type | solution.py:334
  (25 shorter events, 3.5 us)
Async XLA Ops:
  0.0 18.8 %collective-permute-start = (bf16[256,1280]{1,0:T(8,128)(2,1)}, bf16[256,1280]{1,0:T(8,128)(2,1)S(1)}, u32[]{:S(2)}, u32[]{:S(2)}) collective-permute-start(bf16[256,1280]{1,0:T(8,128)(2,1)} %k_ref.1), channel_id=1, source_target_pairs={{0,8},{4,12},{8,0},{12,4},{16,24},{20,28},{24,16},{28,20},{1,9},{5... | collective-permute-start | bytes 1966088 | tf_op jit(solution)/shard_map/ppermute | solution.py:30
  3.0 17.7 %collective-permute-start.1 = (bf16[256,1280]{1,0:T(8,128)(2,1)}, bf16[256,1280]{1,0:T(8,128)(2,1)S(1)}, u32[]{:S(2)}, u32[]{:S(2)}) collective-permute-start(bf16[256,1280]{1,0:T(8,128)(2,1)} %k_ref.1), channel_id=1, source_target_pairs={{8,16},{12,20},{16,8},{20,12},{9,17},{13,21},{17,9},{21,13},{10,18... | collective-permute-start | bytes 1966088 | tf_op jit(solution)/shard_map/ppermute | solution.py:30
  3.7 28.3 %collective-permute-start.3 = (bf16[256,1280]{1,0:T(8,128)(2,1)}, bf16[256,1280]{1,0:T(8,128)(2,1)S(1)}, u32[]{:S(2)}, u32[]{:S(2)}) collective-permute-start(bf16[256,1280]{1,0:T(8,128)(2,1)} %v_ref.1), channel_id=1, source_target_pairs={{0,8},{4,12},{8,0},{12,4},{16,24},{20,28},{24,16},{28,20},{1,9},{5... | collective-permute-start | bytes 1966088 | tf_op jit(solution)/shard_map/ppermute | solution.py:30
  8.1 28.2 %collective-permute-start.4 = (bf16[256,1280]{1,0:T(8,128)(2,1)}, bf16[256,1280]{1,0:T(8,128)(2,1)S(1)}, u32[]{:S(2)}, u32[]{:S(2)}) collective-permute-start(bf16[256,1280]{1,0:T(8,128)(2,1)} %v_ref.1), channel_id=1, source_target_pairs={{8,16},{12,20},{16,8},{20,12},{9,17},{13,21},{17,9},{21,13},{10,18... | collective-permute-start | bytes 1966088 | tf_op jit(solution)/shard_map/ppermute | solution.py:30
  8.8 28.9 %collective-permute-start.2 = (bf16[256,1280]{1,0:T(8,128)(2,1)}, bf16[256,1280]{1,0:T(8,128)(2,1)S(1)}, u32[]{:S(2)}, u32[]{:S(2)}) collective-permute-start(bf16[256,1280]{1,0:T(8,128)(2,1)} %k_ref.1), channel_id=1, source_target_pairs={{0,4},{4,0},{8,12},{12,8},{16,20},{20,16},{24,28},{28,24},{1,5},{5... | collective-permute-start | bytes 1966088 | tf_op jit(solution)/shard_map/ppermute | solution.py:30
  18.8 21.2 %collective-permute-start.5 = (bf16[256,1280]{1,0:T(8,128)(2,1)}, bf16[256,1280]{1,0:T(8,128)(2,1)S(1)}, u32[]{:S(2)}, u32[]{:S(2)}) collective-permute-start(bf16[256,1280]{1,0:T(8,128)(2,1)} %v_ref.1), channel_id=1, source_target_pairs={{0,4},{4,0},{8,12},{12,8},{16,20},{20,16},{24,28},{28,24},{1,5},{5... | collective-permute-start | bytes 1966088 | tf_op jit(solution)/shard_map/ppermute | solution.py:30
  20.8 19.2 %copy-start.3 = (bf16[256,1280]{1,0:T(8,128)(2,1)S(1)}, bf16[256,1280]{1,0:T(8,128)(2,1)}, u32[]{:S(2)}) copy-start(bf16[256,1280]{1,0:T(8,128)(2,1)} %v_ref.1) | copy-start | bytes 1966084
  20.8 19.1 %copy-start.1 = (bf16[256,1280]{1,0:T(8,128)(2,1)S(1)}, bf16[256,1280]{1,0:T(8,128)(2,1)}, u32[]{:S(2)}) copy-start(bf16[256,1280]{1,0:T(8,128)(2,1)} %q_ref.3) | copy-start | bytes 1966084
  20.9 19.1 %copy-start.2 = (bf16[256,1280]{1,0:T(8,128)(2,1)S(1)}, bf16[256,1280]{1,0:T(8,128)(2,1)}, u32[]{:S(2)}) copy-start(bf16[256,1280]{1,0:T(8,128)(2,1)} %k_ref.1) | copy-start | bytes 1966084
  20.9 19.1 %copy-start.4 = (s32[4,32]{1,0:T(4,128)S(1)}, s32[4,32]{1,0:T(4,128)}, u32[]{:S(2)}) copy-start(s32[4,32]{1,0:T(4,128)} %live_ref.3) | copy-start | bytes 1540
  32.0 21.9 %collective-permute-start.8 = (bf16[256,1280]{1,0:T(8,128)(2,1)S(1)}, bf16[256,1280]{1,0:T(8,128)(2,1)S(1)}, u32[]{:S(2)}, u32[]{:S(2)}) collective-permute-start(bf16[256,1280]{1,0:T(8,128)(2,1)S(1)} %broadcast_select_fusion.1), channel_id=1, source_target_pairs={{0,4},{8,12},{12,8},{16,20},{20,16},{28,24},{1,5},{9,13},{13,9},{1... | collective-permute-start | bytes 1966088 | tf_op jit(solution)/shard_map/ppermute | solution.py:30
  35.6 19.6 %collective-permute-start.6 = (bf16[256,1280]{1,0:T(8,128)(2,1)S(1)}, bf16[256,1280]{1,0:T(8,128)(2,1)S(1)}, u32[]{:S(2)}, u32[]{:S(2)}) collective-permute-start(bf16[256,1280]{1,0:T(8,128)(2,1)S(1)} %collective-permute-done.rest_0_), channel_id=1, source_target_pairs={{8,16},{12,20},{16,8},{20,12},{9,17},{13,21},{17,9},{21,13},{10,18... | collective-permute-start | bytes 1966088 | tf_op jit(solution)/shard_map/ppermute | solution.py:30
  36.3 19.2 %collective-permute-start.7 = (bf16[256,1280]{1,0:T(8,128)(2,1)S(1)}, bf16[256,1280]{1,0:T(8,128)(2,1)S(1)}, u32[]{:S(2)}, u32[]{:S(2)}) collective-permute-start(bf16[256,1280]{1,0:T(8,128)(2,1)S(1)} %collective-permute-done.1.rest_1_), channel_id=1, source_target_pairs={{8,0},{12,4},{16,24},{20,28},{9,1},{13,5},{17,25},{21,29},{10,2},{... | collective-permute-start | bytes 1966088 | tf_op jit(solution)/shard_map/ppermute | solution.py:30
  37.6 31.6 %copy-start = (bf16[1280,5120]{1,0:T(8,128)(2,1)S(1)}, bf16[1280,5120]{1,0:T(8,128)(2,1)}, u32[]{:S(2)}) copy-start(bf16[1280,5120]{1,0:T(8,128)(2,1)} %w_ref.3) | copy-start | bytes 39321604
  46.3 19.6 %collective-permute-start.11 = (bf16[256,1280]{1,0:T(8,128)(2,1)S(1)}, bf16[256,1280]{1,0:T(8,128)(2,1)S(1)}, u32[]{:S(2)}, u32[]{:S(2)}) collective-permute-start(bf16[256,1280]{1,0:T(8,128)(2,1)S(1)} %broadcast_select_fusion), channel_id=1, source_target_pairs={{0,4},{8,12},{12,8},{16,20},{20,16},{28,24},{1,5},{9,13},{13,9},{1... | collective-permute-start | bytes 1966088 | tf_op jit(solution)/shard_map/ppermute | solution.py:30
  50.6 15.3 %collective-permute-start.9 = (bf16[256,1280]{1,0:T(8,128)(2,1)S(1)}, bf16[256,1280]{1,0:T(8,128)(2,1)S(1)}, u32[]{:S(2)}, u32[]{:S(2)}) collective-permute-start(bf16[256,1280]{1,0:T(8,128)(2,1)S(1)} %collective-permute-done.3.rest_3_), channel_id=1, source_target_pairs={{8,16},{12,20},{16,8},{20,12},{9,17},{13,21},{17,9},{21,13},{10,18... | collective-permute-start | bytes 1966088 | tf_op jit(solution)/shard_map/ppermute | solution.py:30
  53.9 15.4 %collective-permute-start.10 = (bf16[256,1280]{1,0:T(8,128)(2,1)S(1)}, bf16[256,1280]{1,0:T(8,128)(2,1)S(1)}, u32[]{:S(2)}, u32[]{:S(2)}) collective-permute-start(bf16[256,1280]{1,0:T(8,128)(2,1)S(1)} %collective-permute-done.4.rest_4_), channel_id=1, source_target_pairs={{8,0},{12,4},{16,24},{20,28},{9,1},{13,5},{17,25},{21,29},{10,2},{... | collective-permute-start | bytes 1966088 | tf_op jit(solution)/shard_map/ppermute | solution.py:30
  71.2 2.2 %collective-permute-start.12 = (bf16[256,1280]{1,0:T(8,128)(2,1)S(1)}, bf16[256,1280]{1,0:T(8,128)(2,1)S(1)}, u32[]{:S(2)}, u32[]{:S(2)}) collective-permute-start(bf16[256,1280]{1,0:T(8,128)(2,1)S(1)} %get-tuple-element.25), channel_id=1, source_target_pairs={{0,1},{1,0},{2,3},{3,2},{4,5},{5,4},{6,7},{7,6},{8,9},{9,8},{10,11... | collective-permute-start | bytes 1966088 | tf_op jit(solution)/shard_map/ppermute | solution.py:30
  75.5 2.2 %collective-permute-start.13 = (bf16[256,1280]{1,0:T(8,128)(2,1)S(1)}, bf16[256,1280]{1,0:T(8,128)(2,1)S(1)}, u32[]{:S(2)}, u32[]{:S(2)}) collective-permute-start(bf16[256,1280]{1,0:T(8,128)(2,1)S(1)} %get-tuple-element.28), channel_id=1, source_target_pairs={{0,1},{1,0},{2,3},{3,2},{4,5},{5,4},{6,7},{7,6},{8,9},{9,8},{10,11... | collective-permute-start | bytes 1966088 | tf_op jit(solution)/shard_map/ppermute | solution.py:30
  75.7 17.0 %collective-permute-start.14 = (bf16[256,1280]{1,0:T(8,128)(2,1)S(1)}, bf16[256,1280]{1,0:T(8,128)(2,1)S(1)}, u32[]{:S(2)}, u32[]{:S(2)}) collective-permute-start(bf16[256,1280]{1,0:T(8,128)(2,1)S(1)} %add_convert_fusion.1), channel_id=1, source_target_pairs={{0,2},{1,3},{2,0},{3,1},{4,6},{5,7},{6,4},{7,5},{8,10},{9,11},{10,... | collective-permute-start | bytes 1966088 | tf_op jit(solution)/shard_map/ppermute | solution.py:30

commit v4 on v3

--- a/solution.py
+++ b/solution.py
@@ -12,8 +12,10 @@
 BLK = 64
 EXP_SCALE = math.log2(math.e) / math.sqrt(HDIM)
 DEAD = -1e30
+BARS = {'XV': ('E2K',), 'F1K': ('E1K',), 'DK': ('XK', 'E1K'), 'F1V': ('S', 'F2K'), 'F2V': ('XV',)}
 F32 = jnp.float32
 BF16 = jnp.bfloat16
+LIGHT = pl.CostEstimate(flops=0, bytes_accessed=0, transcendentals=0)
 
 
 def offsets_for(frames):
@@ -36,26 +38,38 @@
     )
 
 
-def early_hops(x, frames):
+def wait(x, name, done):
+    return after(x, *(done[n] for n in BARS.get(name, ())))
+
+
+def early_hops(x, frames, kind, done):
     if frames != 8:
         return [from_offset(x, frames, o) for o in offsets_for(frames)[1:-2]]
-    return [
-        send(x, "frame", [(i, i ^ 2) for i in range(frames)]),
-        send(x, "frame", [(i, i ^ 6) for i in (2, 3, 4, 5)]),
-        send(x, "frame", [(i, i ^ 1) for i in range(frames)]),
-    ]
-
-
-def late_hops(x, hops, own, frames, hold):
+    hops = []
+    for name, pairs in (
+        ("E1", [(i, i ^ 2) for i in range(frames)]),
+        ("E2", [(i, i ^ 6) for i in (2, 3, 4, 5)]),
+        ("X", [(i, i ^ 1) for i in range(frames)]),
+    ):
+        hops.append(send(wait(x, name + kind, done), "frame", pairs))
+        done[name + kind] = hops[-1]
+    return hops
+
+
+def late_hops(x, hops, own, frames, kind, done):
     if frames != 8:
         return [from_offset(x, frames, o) for o in offsets_for(frames)[-2:]]
     outer, inner, _ = hops
     across = jnp.where((own == 2) | (own == 5), inner, outer)
-    return [
-        send(outer, "frame", [(i, i ^ 6) for i in (2, 3, 4, 5)]),
-        send(inner, "frame", [(i, i ^ 2) for i in (2, 3, 4, 5)]),
-        send(hold(across), "frame", [(i, i ^ 1) for i in (0, 2, 3, 4, 5, 7)]),
-    ]
+    results = []
+    for name, x, pairs in (
+        ("F1", outer, [(i, i ^ 6) for i in (2, 3, 4, 5)]),
+        ("F2", inner, [(i, i ^ 2) for i in (2, 3, 4, 5)]),
+        ("D", across, [(i, i ^ 1) for i in (0, 2, 3, 4, 5, 7)]),
+    ):
+        results.append(send(wait(x, name + kind, done), "frame", pairs))
+        done[name + kind] = results[-1]
+    return results
 
 
 def plan(own, frames):
@@ -160,11 +174,7 @@
         out_specs=[VMEM] * 3,
         scratch_shapes=[pltpu.VMEM((8 * rows // BLK, count * rows), F32)],
         compiler_params=params(),
-        cost_estimate=pl.CostEstimate(
-            flops=4 * heads * rows * seen * HDIM,
-            bytes_accessed=4 * heads * seen * HDIM,
-            transcendentals=heads * rows * seen,
-        ),
+        cost_estimate=LIGHT,
         name="early_attention",
     )(live_blocks, queries, keys, values, *early_keys, *early_values)
 
@@ -222,23 +232,23 @@
         out_specs=[VMEM] * 2,
         scratch_shapes=[pltpu.VMEM((8 * rows // BLK, seen), F32)],
         compiler_params=params(),
-        cost_estimate=pl.CostEstimate(
-            flops=2 * heads * rows * seen * HDIM,
-            bytes_accessed=4 * heads * seen * HDIM,
-            transcendentals=heads * rows * seen,
-        ),
+        cost_estimate=LIGHT,
         name="late_weights",
     )(live_blocks, queries, sums, peaks, totals, *late_keys)
 
 
-def multiply(a_ref, w_ref, out_ref, group):
-    width = out_ref.shape[1]
-    step = width // 5 if width % (5 * HDIM) == 0 else width
-    for n in range(0, width, step):
-        columns = pl.ds(pl.multiple_of(group * width + n, HDIM), step)
-        out_ref[:, n : n + step] = jnp.dot(
-            a_ref[...], w_ref[:, columns], preferred_element_type=F32
-        ).astype(BF16)
+def multiply(a_ref, w_ref, out_ref, *parts):
+    columns = w_ref.shape[1] // lax.axis_size("head")
+    step = 2 * HDIM
+    base = 0
+    for bit, start, width in parts:
+        group = lax.axis_index("head") ^ bit
+        for n in range(0, width, step):
+            at = pl.ds(pl.multiple_of(group * columns + (start + n), HDIM), step)
+            out_ref[:, base + n : base + n + step] = jnp.dot(
+                a_ref[...], w_ref[:, at], preferred_element_type=F32
+            ).astype(BF16)
+        base += width
 
 
 def first_project_kernel(count, scaled_ref, weights_ref, *rest):
@@ -255,20 +265,11 @@
             weight = weights_ref[:, h * seen + n * rows : h * seen + (n + 1) * rows]
             acc += jnp.dot(weight, value, preferred_element_type=F32)
         att_ref[:, columns] = acc.astype(BF16)
-    multiply(att_ref, w_ref, out_ref, lax.axis_index("head") ^ 3)
-
-
-def project_cost(rows, width, columns, count):
-    return pl.CostEstimate(
-        flops=2 * rows * width * columns * count,
-        bytes_accessed=2 * width * columns * count,
-        transcendentals=0,
-    )
-
-
-def first_project(scaled, weights, late_values, weight):
+    multiply(att_ref, w_ref, out_ref, (3, 0, out_ref.shape[1]))
+
+
+def first_project(scaled, weights, late_values, weight, columns):
     rows, width = scaled.shape
-    columns = weight.shape[1] // lax.axis_size("head")
     return pl.pallas_call(
         functools.partial(first_project_kernel, len(late_values)),
         out_shape=[
@@ -278,58 +279,64 @@
         in_specs=[VMEM] * (3 + len(late_values)),
         out_specs=[VMEM] * 2,
         compiler_params=params(),
-        cost_estimate=project_cost(rows, width, columns, 1),
+        cost_estimate=LIGHT,
         name="first_project",
     )(scaled, weights, *late_values, weight)
 
 
-def project_kernel(bits, a_ref, w_ref, *outs):
-    for bit, out_ref in zip(bits, outs):
-        multiply(a_ref, w_ref, out_ref, lax.axis_index("head") ^ bit)
-
-
-def project(attended, weight, bits):
-    rows, width = attended.shape
-    columns = weight.shape[1] // lax.axis_size("head")
+def project_kernel(outputs, a_ref, w_ref, *outs):
+    for parts, out_ref in zip(outputs, outs):
+        multiply(a_ref, w_ref, out_ref, *parts)
+
+
+def project(attended, weight, *outputs):
+    rows = attended.shape[0]
     return pl.pallas_call(
-        functools.partial(project_kernel, bits),
-        out_shape=[jax.ShapeDtypeStruct((rows, columns), BF16)] * len(bits),
+        functools.partial(project_kernel, outputs),
+        out_shape=[
+            jax.ShapeDtypeStruct((rows, sum(width for _, _, width in parts)), BF16)
+            for parts in outputs
+        ],
         in_specs=[VMEM] * 2,
-        out_specs=[VMEM] * len(bits),
+        out_specs=[VMEM] * len(outputs),
         compiler_params=params(),
-        cost_estimate=project_cost(rows, width, columns, len(bits)),
+        cost_estimate=LIGHT,
         name="project",
     )(attended, weight)
 
 
 def after(x, *others):
-    return lax.optimization_barrier((x, *others))[0]
+    return lax.optimization_barrier((x, *others))[0] if others else x
 
 
 def on_device(queries, key_vectors, value_vectors, live_blocks, out_weight):
     frames = lax.axis_size("frame")
     own = lax.axis_index("frame")
 
-    early_keys = early_hops(key_vectors, frames)
-    early_values = early_hops(value_vectors, frames)
-    late_keys = late_hops(key_vectors, early_keys, own, frames, lambda x: after(x, early_values[0]))
-
+    done = {}
+    early_keys = early_hops(key_vectors, frames, "K", done)
+    early_values = early_hops(value_vectors, frames, "V", done)
+    late_keys = late_hops(key_vectors, early_keys, own, frames, "K", done)
+    held_queries = wait(queries, "S", done) if frames == 8 else queries
     sums, peaks, totals = early_attention(
-        live_blocks, queries, key_vectors, value_vectors, early_keys, early_values
-    )
-    late_values = late_hops(value_vectors, early_values, own, frames, lambda x: after(x, sums))
+        live_blocks, held_queries, key_vectors, value_vectors, early_keys, early_values
+    )
+    done["S"] = sums
+    late_values = late_hops(value_vectors, early_values, own, frames, "V", done)
     places = 2
     weights, scaled = late_weights(
         live_blocks, queries, sums, peaks, totals, late_keys, places
     )
 
     swap = lambda x, bit: send(x, "head", [(g, g ^ bit) for g in range(4)])
-    for_sibling, attended = first_project(scaled, weights, late_values, out_weight)
-    (mine,) = project(attended, out_weight, (2,))
-    crossed = (mine.astype(F32) + swap(for_sibling, 1).astype(F32)).astype(BF16)
+    add = lambda a, b: (a.astype(F32) + b.astype(F32)).astype(BF16)
+    columns = out_weight.shape[1] // lax.axis_size("head")
+    for_sibling, attended = first_project(scaled, weights, late_values, out_weight, columns)
+    (mine,) = project(attended, out_weight, ((2, 0, columns),))
+    crossed = add(mine, swap(for_sibling, 1))
+    near_a, near_b, total = project(after(attended, crossed), out_weight, ((1, 0, columns // 5 * 2),), ((1, columns // 5 * 2, columns // 5 * 3),), ((0, 0, columns),))
+    from_near = jnp.concatenate([swap(near_a, 1), swap(near_b, 1)], 1)
     from_far = swap(crossed, 2)
-    near, total = project(after(attended, crossed), out_weight, (1, 0))
-    from_near = swap(near, 1)
     total = total.astype(F32) + from_near.astype(F32) + from_far.astype(F32)
     return total.astype(BF16)
 

time: 94.1 us -> 86.6 us (0.920)
  the two profiles are of different devices: /device:TPU:0 before, /device:TPU:10 now
where the time goes in v4:
time: 86.6 us; the launch traced here: 86.4 us
  waiting for transfers between devices  44.4 us (51%)
  starting transfers between devices  25 us (29%)
  Pallas kernels  15.3 us (18%)
  other arithmetic  1.37 us (2%)
    ppermute x16, waiting for transfers between devices, send(): return lax.ppermute(x, axis, pairs)  44.4 us
    ppermute x16, starting transfers between devices, send(): return lax.ppermute(x, axis, pairs)  25 us
    pallas_call x1, Pallas kernels, early_attention(): pl.pallas_call(functools.partial(early_kernel, count), out_shape=[jax.Sha...  6.33 us
    pallas_call x1, Pallas kernels, late_weights(): pl.pallas_call(late_kernel, out_shape=[jax.ShapeDtypeStruct((rows, heads...  4.03 us
    pallas_call x2, Pallas kernels, project(): pl.pallas_call(functools.partial(project_kernel, outputs), out_shape=[jax...  2.99 us
    pallas_call x1, Pallas kernels, first_project(): pl.pallas_call(functools.partial(first_project_kernel, len(late_values)),...  1.97 us
  transfers between devices with their start and end apart: 16, of which 8 were waited for; matrix products, arithmetic and copies ran while one was open for 0% of the time, Pallas kernels for 15%

profile of v4, /device:TPU:10, one launch (start us, length us, event | category | flops | bytes accessed | tf_op | source)
XLA Modules:
  0.0 86.4 jit_solution(4474975578943390938)
XLA Ops:
  0.0 3.5 %collective-permute-start.1 = (bf16[256,1280]{1,0:T(8,128)(2,1)}, bf16[256,1280]{1,0:T(8,128)(2,1)S(1)}, u32[]{:S(2)}, u32[]{:S(2)}) collective-permute-start(bf16[256,1280]{1,0:T(8,128)(2,1)} %k_ref.1), channel_id=1, source_target_pairs={{8,16},{12,20},{16,8},{20,12},{9,17},{13,21},{17,9},{21,13},{10,18... | collective-permute-start | bytes 1966088 | tf_op jit(solution)/shard_map/ppermute | solution.py:32
  3.6 0.6 collective-permute-start.2
  4.2 2.3 %collective-permute-start.4 = (bf16[256,1280]{1,0:T(8,128)(2,1)}, bf16[256,1280]{1,0:T(8,128)(2,1)S(1)}, u32[]{:S(2)}, u32[]{:S(2)}) collective-permute-start(bf16[256,1280]{1,0:T(8,128)(2,1)} %v_ref.1), channel_id=1, source_target_pairs={{8,16},{12,20},{16,8},{20,12},{9,17},{13,21},{17,9},{21,13},{10,18... | collective-permute-start | bytes 1966088 | tf_op jit(solution)/shard_map/ppermute | solution.py:32
  6.9 12.8 %collective-permute-done.1.rest_1_ = bf16[256,1280]{1,0:T(8,128)(2,1)S(1)} collective-permute-done((bf16[256,1280]{1,0:T(8,128)(2,1)}, bf16[256,1280]{1,0:T(8,128)(2,1)S(1)}, u32[]{:S(2)}, u32[]{:S(2)}) %collective-permute-start.1) | collective-permute-done | bytes 655392 | tf_op jit(solution)/shard_map/ppermute | solution.py:32
  20.2 1.2 %collective-permute-done.rest_0_ = bf16[256,1280]{1,0:T(8,128)(2,1)S(1)} collective-permute-done((bf16[256,1280]{1,0:T(8,128)(2,1)}, bf16[256,1280]{1,0:T(8,128)(2,1)S(1)}, u32[]{:S(2)}, u32[]{:S(2)}) %collective-permute-start) | collective-permute-done | bytes 655392 | tf_op jit(solution)/shard_map/ppermute | solution.py:32
  21.4 1.9 %collective-permute-start.7 = (bf16[256,1280]{1,0:T(8,128)(2,1)S(1)}, bf16[256,1280]{1,0:T(8,128)(2,1)S(1)}, u32[]{:S(2)}, u32[]{:S(2)}) collective-permute-start(bf16[256,1280]{1,0:T(8,128)(2,1)S(1)} %collective-permute-done.1.rest_1_), channel_id=1, source_target_pairs={{8,0},{12,4},{16,24},{20,28},{9,1},{13,5},{17,25},{21,29},{10,2},{... | collective-permute-start | bytes 1966088 | tf_op jit(solution)/shard_map/ppermute | solution.py:32
  23.5 2.5 %collective-permute-start.6 = (bf16[256,1280]{1,0:T(8,128)(2,1)S(1)}, bf16[256,1280]{1,0:T(8,128)(2,1)S(1)}, u32[]{:S(2)}, u32[]{:S(2)}) collective-permute-start(bf16[256,1280]{1,0:T(8,128)(2,1)S(1)} %collective-permute-done.rest_0_), channel_id=1, source_target_pairs={{8,16},{12,20},{16,8},{20,12},{9,17},{13,21},{17,9},{21,13},{10,18... | collective-permute-start | bytes 1966088 | tf_op jit(solution)/shard_map/ppermute | solution.py:32
  26.0 7.8 %collective-permute-done.4.rest_4_ = bf16[256,1280]{1,0:T(8,128)(2,1)S(1)} collective-permute-done((bf16[256,1280]{1,0:T(8,128)(2,1)}, bf16[256,1280]{1,0:T(8,128)(2,1)S(1)}, u32[]{:S(2)}, u32[]{:S(2)}) %collective-permute-start.4) | collective-permute-done | bytes 655392 | tf_op jit(solution)/shard_map/ppermute | solution.py:32
  33.8 2.4 %collective-permute-start.8 = (bf16[256,1280]{1,0:T(8,128)(2,1)S(1)}, bf16[256,1280]{1,0:T(8,128)(2,1)S(1)}, u32[]{:S(2)}, u32[]{:S(2)}) collective-permute-start(bf16[256,1280]{1,0:T(8,128)(2,1)S(1)} %broadcast_select_fusion.1), channel_id=1, source_target_pairs={{0,4},{8,12},{12,8},{16,20},{20,16},{28,24},{1,5},{9,13},{13,9},{1... | collective-permute-start | bytes 1966088 | tf_op jit(solution)/shard_map/ppermute | solution.py:32
  36.3 3.8 %collective-permute-start.11 = (bf16[256,1280]{1,0:T(8,128)(2,1)S(1)}, bf16[256,1280]{1,0:T(8,128)(2,1)S(1)}, u32[]{:S(2)}, u32[]{:S(2)}) collective-permute-start(bf16[256,1280]{1,0:T(8,128)(2,1)S(1)} %broadcast_select_fusion), channel_id=1, source_target_pairs={{0,4},{8,12},{12,8},{16,20},{20,16},{28,24},{1,5},{9,13},{13,9},{1... | collective-permute-start | bytes 1966088 | tf_op jit(solution)/shard_map/ppermute | solution.py:32
  40.1 1.3 %collective-permute-start.10 = (bf16[256,1280]{1,0:T(8,128)(2,1)S(1)}, bf16[256,1280]{1,0:T(8,128)(2,1)S(1)}, u32[]{:S(2)}, u32[]{:S(2)}) collective-permute-start(bf16[256,1280]{1,0:T(8,128)(2,1)S(1)} %collective-permute-done.4.rest_4_), channel_id=1, source_target_pairs={{8,0},{12,4},{16,24},{20,28},{9,1},{13,5},{17,25},{21,29},{10,2},{... | collective-permute-start | bytes 1966088 | tf_op jit(solution)/shard_map/ppermute | solution.py:32
  41.5 6.3 %early_attention.1 = (f32[256,1280]{1,0:T(8,128)S(1)}, f32[256,1280]{1,0:T(8,128)S(1)}, f32[256,1280]{1,0:T(8,128)S(1)}) custom-call(s32[4,32]{1,0:T(4,128)S(1)} %copy-done.4, bf16[256,1280]{1,0:T(8,128)(2,1)S(1)} %copy-done.1, bf16[256,1280]{1,0:T(8,128)(2,1)S(1)} %copy-done.2, bf16[256,1280]{1,0:T(8,128)(2,1)S(1)} %copy-done.3, ...), custom_call_target="tpu_custom_call" | custom-call | tf_op jit(solution)/shard_map/early_attention/pallas_call | solution.py:170
  47.8 3.5 %collective-permute-start.9 = (bf16[256,1280]{1,0:T(8,128)(2,1)S(1)}, bf16[256,1280]{1,0:T(8,128)(2,1)S(1)}, u32[]{:S(2)}, u32[]{:S(2)}) collective-permute-start(bf16[256,1280]{1,0:T(8,128)(2,1)S(1)} %collective-permute-done.3.rest_3_), channel_id=1, source_target_pairs={{8,16},{12,20},{16,8},{20,12},{9,17},{13,21},{17,9},{21,13},{10,18... | collective-permute-start | bytes 1966088 | tf_op jit(solution)/shard_map/ppermute | solution.py:32
  51.3 2.0 %collective-permute-done.8.rest_2_ = bf16[256,1280]{1,0:T(8,128)(2,1)S(1)} collective-permute-done((bf16[256,1280]{1,0:T(8,128)(2,1)S(1)}, bf16[256,1280]{1,0:T(8,128)(2,1)S(1)}, u32[]{:S(2)}, u32[]{:S(2)}) %collective-permute-start.8) | collective-permute-done | bytes 655392 | tf_op jit(solution)/shard_map/ppermute | solution.py:32
  53.3 4.0 %late_weights.1 = (bf16[256,5120]{1,0:T(8,128)(2,1)S(1)}, f32[256,1280]{1,0:T(8,128)S(1)}) custom-call(s32[4,32]{1,0:T(4,128)S(1)} %copy-done.4, bf16[256,1280]{1,0:T(8,128)(2,1)S(1)} %copy-done.1, f32[256,1280]{1,0:T(8,128)S(1)} %get-tuple-element.22.sum_ref, f32[256,1280]{1,0:T(8,128)S(1)} %get-tuple-element.23.peak_ref, ...), custom_call_target="tpu_custom_call" | custom-call | tf_op jit(solution)/shard_map/late_weights/pallas_call | solution.py:225
  57.3 6.8 %collective-permute-done.11.rest_2_ = bf16[256,1280]{1,0:T(8,128)(2,1)S(1)} collective-permute-done((bf16[256,1280]{1,0:T(8,128)(2,1)S(1)}, bf16[256,1280]{1,0:T(8,128)(2,1)S(1)}, u32[]{:S(2)}, u32[]{:S(2)}) %collective-permute-start.11) | collective-permute-done | bytes 655392 | tf_op jit(solution)/shard_map/ppermute | solution.py:32
  64.2 2.0 %first_project.1 = (bf16[256,1280]{1,0:T(8,128)(2,1)S(1)}, bf16[256,1280]{1,0:T(8,128)(2,1)S(1)}) custom-call(f32[256,1280]{1,0:T(8,128)S(1)} %get-tuple-element.27.scaled_ref, bf16[256,5120]{1,0:T(8,128)(2,1)S(1)} %get-tuple-element.28.weights_ref, bf16[256,1280]{1,0:T(8,128)(2,1)S(1)} %collective-permute-done.9.rest_0_, ...), custom_call_target="tpu_custom_call" | custom-call | tf_op jit(solution)/shard_map/first_project/pallas_call | solution.py:273
  66.2 1.1 %project.2 = bf16[256,1280]{1,0:T(8,128)(2,1)S(1)} custom-call(bf16[256,1280]{1,0:T(8,128)(2,1)S(1)} %get-tuple-element.33.a_ref, bf16[1280,5120]{1,0:T(8,128)(2,1)S(1)} %copy-done), custom_call_target="tpu_custom_call" | custom-call | tf_op jit(solution)/shard_map/project/pallas_call | solution.py:294
  67.3 1.0 %collective-permute-done.12 = bf16[256,1280]{1,0:T(8,128)(2,1)S(1)} collective-permute-done((bf16[256,1280]{1,0:T(8,128)(2,1)S(1)}, bf16[256,1280]{1,0:T(8,128)(2,1)S(1)}, u32[]{:S(2)}, u32[]{:S(2)}) %collective-permute-start.12) | collective-permute-done | bytes 655392 | tf_op jit(solution)/shard_map/ppermute | solution.py:32
  68.4 1.6 %collective-permute-start.15 = (bf16[256,1280]{1,0:T(8,128)(2,1)S(1)}, bf16[256,1280]{1,0:T(8,128)(2,1)S(1)}, u32[]{:S(2)}, u32[]{:S(2)}) collective-permute-start(bf16[256,1280]{1,0:T(8,128)(2,1)S(1)} %add_convert_fusion.1), channel_id=1, source_target_pairs={{0,2},{1,3},{2,0},{3,1},{4,6},{5,7},{6,4},{7,5},{8,10},{9,11},{10,... | collective-permute-start | bytes 1966088 | tf_op jit(solution)/shard_map/ppermute | solution.py:32
  70.0 1.9 %project.3 = (bf16[256,512]{1,0:T(8,128)(2,1)S(1)}, bf16[256,768]{1,0:T(8,128)(2,1)S(1)}, bf16[256,1280]{1,0:T(8,128)(2,1)S(1)}) custom-call(bf16[256,1280]{1,0:T(8,128)(2,1)S(1)} %get-tuple-element.33.a_ref, bf16[1280,5120]{1,0:T(8,128)(2,1)S(1)} %copy-done), custom_call_target="tpu_custom_call" | custom-call | tf_op jit(solution)/shard_map/project/pallas_call | solution.py:294
  72.5 1.6 %collective-permute-done.13 = bf16[256,512]{1,0:T(8,128)(2,1)S(1)} collective-permute-done((bf16[256,512]{1,0:T(8,128)(2,1)S(1)}, bf16[256,512]{1,0:T(8,128)(2,1)S(1)}, u32[]{:S(2)}, u32[]{:S(2)}) %collective-permute-start.13) | collective-permute-done | bytes 262176 | tf_op jit(solution)/shard_map/ppermute | solution.py:32
  74.1 11.2 %collective-permute-done.15 = bf16[256,1280]{1,0:T(8,128)(2,1)S(1)} collective-permute-done((bf16[256,1280]{1,0:T(8,128)(2,1)S(1)}, bf16[256,1280]{1,0:T(8,128)(2,1)S(1)}, u32[]{:S(2)}, u32[]{:S(2)}) %collective-permute-start.15) | collective-permute-done | bytes 655392 | tf_op jit(solution)/shard_map/ppermute | solution.py:32
  85.3 1.1 %add_convert_fusion = bf16[256,1280]{1,0:T(8,128)(2,1)} fusion(bf16[256,1280]{1,0:T(8,128)(2,1)S(1)} %collective-permute-done.15, bf16[256,1280]{1,0:T(8,128)(2,1)S(1)} %get-tuple-element.34, bf16[256,768]{1,0:T(8,128)(2,1)S(1)} %collective-permute-done.14, bf16[256,512]{1,0:T(8,128)(2,1)S(1)} %collective-permute-done.13), kind=kLoop, calls=%fused_computation | loop fusion | flops 2949120 | bytes 2621440 | tf_op jit(solution)/shard_map/convert_element_type | solution.py:341
  (27 shorter events, 1.9 us)
Async XLA Ops:
  0.0 19.7 %collective-permute-start.1 = (bf16[256,1280]{1,0:T(8,128)(2,1)}, bf16[256,1280]{1,0:T(8,128)(2,1)S(1)}, u32[]{:S(2)}, u32[]{:S(2)}) collective-permute-start(bf16[256,1280]{1,0:T(8,128)(2,1)} %k_ref.1), channel_id=1, source_target_pairs={{8,16},{12,20},{16,8},{20,12},{9,17},{13,21},{17,9},{21,13},{10,18... | collective-permute-start | bytes 1966088 | tf_op jit(solution)/shard_map/ppermute | solution.py:32
  3.5 17.9 %collective-permute-start = (bf16[256,1280]{1,0:T(8,128)(2,1)}, bf16[256,1280]{1,0:T(8,128)(2,1)S(1)}, u32[]{:S(2)}, u32[]{:S(2)}) collective-permute-start(bf16[256,1280]{1,0:T(8,128)(2,1)} %k_ref.1), channel_id=1, source_target_pairs={{0,8},{4,12},{8,0},{12,4},{16,24},{20,28},{24,16},{28,20},{1,9},{5... | collective-permute-start | bytes 1966088 | tf_op jit(solution)/shard_map/ppermute | solution.py:32
  3.6 19.9 %collective-permute-start.2 = (bf16[256,1280]{1,0:T(8,128)(2,1)}, bf16[256,1280]{1,0:T(8,128)(2,1)S(1)}, u32[]{:S(2)}, u32[]{:S(2)}) collective-permute-start(bf16[256,1280]{1,0:T(8,128)(2,1)} %k_ref.1), channel_id=1, source_target_pairs={{0,4},{4,0},{8,12},{12,8},{16,20},{20,16},{24,28},{28,24},{1,5},{5... | collective-permute-start | bytes 1966088 | tf_op jit(solution)/shard_map/ppermute | solution.py:32
  4.2 29.6 %collective-permute-start.4 = (bf16[256,1280]{1,0:T(8,128)(2,1)}, bf16[256,1280]{1,0:T(8,128)(2,1)S(1)}, u32[]{:S(2)}, u32[]{:S(2)}) collective-permute-start(bf16[256,1280]{1,0:T(8,128)(2,1)} %v_ref.1), channel_id=1, source_target_pairs={{8,16},{12,20},{16,8},{20,12},{9,17},{13,21},{17,9},{21,13},{10,18... | collective-permute-start | bytes 1966088 | tf_op jit(solution)/shard_map/ppermute | solution.py:32
  6.5 29.7 %collective-permute-start.3 = (bf16[256,1280]{1,0:T(8,128)(2,1)}, bf16[256,1280]{1,0:T(8,128)(2,1)S(1)}, u32[]{:S(2)}, u32[]{:S(2)}) collective-permute-start(bf16[256,1280]{1,0:T(8,128)(2,1)} %v_ref.1), channel_id=1, source_target_pairs={{0,8},{4,12},{8,0},{12,4},{16,24},{20,28},{24,16},{28,20},{1,9},{5... | collective-permute-start | bytes 1966088 | tf_op jit(solution)/shard_map/ppermute | solution.py:32
  19.7 20.4 %collective-permute-start.5 = (bf16[256,1280]{1,0:T(8,128)(2,1)}, bf16[256,1280]{1,0:T(8,128)(2,1)S(1)}, u32[]{:S(2)}, u32[]{:S(2)}) collective-permute-start(bf16[256,1280]{1,0:T(8,128)(2,1)} %v_ref.1), channel_id=1, source_target_pairs={{0,4},{4,0},{8,12},{12,8},{16,20},{20,16},{24,28},{28,24},{1,5},{5... | collective-permute-start | bytes 1966088 | tf_op jit(solution)/shard_map/ppermute | solution.py:32
  21.4 26.4 %collective-permute-start.7 = (bf16[256,1280]{1,0:T(8,128)(2,1)S(1)}, bf16[256,1280]{1,0:T(8,128)(2,1)S(1)}, u32[]{:S(2)}, u32[]{:S(2)}) collective-permute-start(bf16[256,1280]{1,0:T(8,128)(2,1)S(1)} %collective-permute-done.1.rest_1_), channel_id=1, source_target_pairs={{8,0},{12,4},{16,24},{20,28},{9,1},{13,5},{17,25},{21,29},{10,2},{... | collective-permute-start | bytes 1966088 | tf_op jit(solution)/shard_map/ppermute | solution.py:32
  23.3 18.1 %copy-start.3 = (bf16[256,1280]{1,0:T(8,128)(2,1)S(1)}, bf16[256,1280]{1,0:T(8,128)(2,1)}, u32[]{:S(2)}) copy-start(bf16[256,1280]{1,0:T(8,128)(2,1)} %v_ref.1) | copy-start | bytes 1966084
  23.4 18.0 %copy-start.1 = (bf16[256,1280]{1,0:T(8,128)(2,1)S(1)}, bf16[256,1280]{1,0:T(8,128)(2,1)}, u32[]{:S(2)}) copy-start(bf16[256,1280]{1,0:T(8,128)(2,1)} %q_ref.3) | copy-start | bytes 1966084
  23.4 18.0 %copy-start.2 = (bf16[256,1280]{1,0:T(8,128)(2,1)S(1)}, bf16[256,1280]{1,0:T(8,128)(2,1)}, u32[]{:S(2)}) copy-start(bf16[256,1280]{1,0:T(8,128)(2,1)} %k_ref.1) | copy-start | bytes 1966084
  23.4 18.0 %copy-start.4 = (s32[4,32]{1,0:T(4,128)S(1)}, s32[4,32]{1,0:T(4,128)}, u32[]{:S(2)}) copy-start(s32[4,32]{1,0:T(4,128)} %live_ref.3) | copy-start | bytes 1540
  23.5 27.9 %collective-permute-start.6 = (bf16[256,1280]{1,0:T(8,128)(2,1)S(1)}, bf16[256,1280]{1,0:T(8,128)(2,1)S(1)}, u32[]{:S(2)}, u32[]{:S(2)}) collective-permute-start(bf16[256,1280]{1,0:T(8,128)(2,1)S(1)} %collective-permute-done.rest_0_), channel_id=1, source_target_pairs={{8,16},{12,20},{16,8},{20,12},{9,17},{13,21},{17,9},{21,13},{10,18... | collective-permute-start | bytes 1966088 | tf_op jit(solution)/shard_map/ppermute | solution.py:32
  33.8 19.6 %collective-permute-start.8 = (bf16[256,1280]{1,0:T(8,128)(2,1)S(1)}, bf16[256,1280]{1,0:T(8,128)(2,1)S(1)}, u32[]{:S(2)}, u32[]{:S(2)}) collective-permute-start(bf16[256,1280]{1,0:T(8,128)(2,1)S(1)} %broadcast_select_fusion.1), channel_id=1, source_target_pairs={{0,4},{8,12},{12,8},{16,20},{20,16},{28,24},{1,5},{9,13},{13,9},{1... | collective-permute-start | bytes 1966088 | tf_op jit(solution)/shard_map/ppermute | solution.py:32
  36.2 27.9 %copy-start = (bf16[1280,5120]{1,0:T(8,128)(2,1)S(1)}, bf16[1280,5120]{1,0:T(8,128)(2,1)}, u32[]{:S(2)}) copy-start(bf16[1280,5120]{1,0:T(8,128)(2,1)} %w_ref.3) | copy-start | bytes 39321604
  36.3 27.8 %collective-permute-start.11 = (bf16[256,1280]{1,0:T(8,128)(2,1)S(1)}, bf16[256,1280]{1,0:T(8,128)(2,1)S(1)}, u32[]{:S(2)}, u32[]{:S(2)}) collective-permute-start(bf16[256,1280]{1,0:T(8,128)(2,1)S(1)} %broadcast_select_fusion), channel_id=1, source_target_pairs={{0,4},{8,12},{12,8},{16,20},{20,16},{28,24},{1,5},{9,13},{13,9},{1... | collective-permute-start | bytes 1966088 | tf_op jit(solution)/shard_map/ppermute | solution.py:32
  40.1 24.0 %collective-permute-start.10 = (bf16[256,1280]{1,0:T(8,128)(2,1)S(1)}, bf16[256,1280]{1,0:T(8,128)(2,1)S(1)}, u32[]{:S(2)}, u32[]{:S(2)}) collective-permute-start(bf16[256,1280]{1,0:T(8,128)(2,1)S(1)} %collective-permute-done.4.rest_4_), channel_id=1, source_target_pairs={{8,0},{12,4},{16,24},{20,28},{9,1},{13,5},{17,25},{21,29},{10,2},{... | collective-permute-start | bytes 1966088 | tf_op jit(solution)/shard_map/ppermute | solution.py:32
  47.8 16.3 %collective-permute-start.9 = (bf16[256,1280]{1,0:T(8,128)(2,1)S(1)}, bf16[256,1280]{1,0:T(8,128)(2,1)S(1)}, u32[]{:S(2)}, u32[]{:S(2)}) collective-permute-start(bf16[256,1280]{1,0:T(8,128)(2,1)S(1)} %collective-permute-done.3.rest_3_), channel_id=1, source_target_pairs={{8,16},{12,20},{16,8},{20,12},{9,17},{13,21},{17,9},{21,13},{10,18... | collective-permute-start | bytes 1966088 | tf_op jit(solution)/shard_map/ppermute | solution.py:32
  66.1 2.2 %collective-permute-start.12 = (bf16[256,1280]{1,0:T(8,128)(2,1)S(1)}, bf16[256,1280]{1,0:T(8,128)(2,1)S(1)}, u32[]{:S(2)}, u32[]{:S(2)}) collective-permute-start(bf16[256,1280]{1,0:T(8,128)(2,1)S(1)} %get-tuple-element.32), channel_id=1, source_target_pairs={{0,1},{1,0},{2,3},{3,2},{4,5},{5,4},{6,7},{7,6},{8,9},{9,8},{10,11... | collective-permute-start | bytes 1966088 | tf_op jit(solution)/shard_map/ppermute | solution.py:32
  68.4 16.8 %collective-permute-start.15 = (bf16[256,1280]{1,0:T(8,128)(2,1)S(1)}, bf16[256,1280]{1,0:T(8,128)(2,1)S(1)}, u32[]{:S(2)}, u32[]{:S(2)}) collective-permute-start(bf16[256,1280]{1,0:T(8,128)(2,1)S(1)} %add_convert_fusion.1), channel_id=1, source_target_pairs={{0,2},{1,3},{2,0},{3,1},{4,6},{5,7},{6,4},{7,5},{8,10},{9,11},{10,... | collective-permute-start | bytes 1966088 | tf_op jit(solution)/shard_map/ppermute | solution.py:32
  71.9 2.2 %collective-permute-start.14 = (bf16[256,768]{1,0:T(8,128)(2,1)S(1)}, bf16[256,768]{1,0:T(8,128)(2,1)S(1)}, u32[]{:S(2)}, u32[]{:S(2)}) collective-permute-start(bf16[256,768]{1,0:T(8,128)(2,1)S(1)} %get-tuple-element.36), channel_id=1, source_target_pairs={{0,1},{1,0},{2,3},{3,2},{4,5},{5,4},{6,7},{7,6},{8,9},{9,8},{10,11... | collective-permute-start | bytes 1179656 | tf_op jit(solution)/shard_map/ppermute | solution.py:32
  72.0 2.1 %collective-permute-start.13 = (bf16[256,512]{1,0:T(8,128)(2,1)S(1)}, bf16[256,512]{1,0:T(8,128)(2,1)S(1)}, u32[]{:S(2)}, u32[]{:S(2)}) collective-permute-start(bf16[256,512]{1,0:T(8,128)(2,1)S(1)} %get-tuple-element.35), channel_id=1, source_target_pairs={{0,1},{1,0},{2,3},{3,2},{4,5},{5,4},{6,7},{7,6},{8,9},{9,8},{10,11... | collective-permute-start | bytes 786440 | tf_op jit(solution)/shard_map/ppermute | solution.py:32

commit v5 on v4

--- a/solution.py
+++ b/solution.py
@@ -12,7 +12,7 @@
 BLK = 64
 EXP_SCALE = math.log2(math.e) / math.sqrt(HDIM)
 DEAD = -1e30
-BARS = {'XV': ('E2K',), 'F1K': ('E1K',), 'DK': ('XK', 'E1K'), 'F1V': ('S', 'F2K'), 'F2V': ('XV',)}
+BARS = {'XV': ('E1K', 'XK'), 'F1K': ('E2K', 'E1V'), 'F1V': ('S',), 'DV': ('XV',)}
 F32 = jnp.float32
 BF16 = jnp.bfloat16
 LIGHT = pl.CostEstimate(flops=0, bytes_accessed=0, transcendentals=0)
@@ -239,11 +239,11 @@
 
 def multiply(a_ref, w_ref, out_ref, *parts):
     columns = w_ref.shape[1] // lax.axis_size("head")
-    step = 2 * HDIM
     base = 0
     for bit, start, width in parts:
         group = lax.axis_index("head") ^ bit
-        for n in range(0, width, step):
+        for n in range(0, width, 2 * HDIM):
+            step = min(2 * HDIM, width - n)
             at = pl.ds(pl.multiple_of(group * columns + (start + n), HDIM), step)
             out_ref[:, base + n : base + n + step] = jnp.dot(
                 a_ref[...], w_ref[:, at], preferred_element_type=F32
@@ -331,14 +331,25 @@
     swap = lambda x, bit: send(x, "head", [(g, g ^ bit) for g in range(4)])
     add = lambda a, b: (a.astype(F32) + b.astype(F32)).astype(BF16)
     columns = out_weight.shape[1] // lax.axis_size("head")
-    for_sibling, attended = first_project(scaled, weights, late_values, out_weight, columns)
-    (mine,) = project(attended, out_weight, ((2, 0, columns),))
-    crossed = add(mine, swap(for_sibling, 1))
-    near_a, near_b, total = project(after(attended, crossed), out_weight, ((1, 0, columns // 5 * 2),), ((1, columns // 5 * 2, columns // 5 * 3),), ((0, 0, columns),))
-    from_near = jnp.concatenate([swap(near_a, 1), swap(near_b, 1)], 1)
-    from_far = swap(crossed, 2)
-    total = total.astype(F32) + from_near.astype(F32) + from_far.astype(F32)
-    return total.astype(BF16)
+    cut = columns // 2
+    rest = columns - cut
+    sibling_a, attended = first_project(scaled, weights, late_values, out_weight, cut)
+    sibling_b, mine_a = project(attended, out_weight, ((3, cut, rest),), ((2, 0, cut),))
+    crossed_a = add(mine_a, swap(sibling_a, 1))
+    far_a = swap(crossed_a, 2)
+    sibling_b = swap(after(sibling_b, crossed_a), 1)
+    (mine_b,) = project(after(attended, crossed_a), out_weight, ((2, cut, rest),))
+    crossed_b = add(mine_b, sibling_b)
+    far_b = swap(crossed_b, 2)
+    bounds = [0, 4 * HDIM, 8 * HDIM, columns]
+    *near, total = project(
+        after(attended, crossed_b), out_weight,
+        *(((1, p, q - p),) for p, q in zip(bounds[:-1], bounds[1:])), ((0, 0, columns),),
+    )
+    near = jnp.concatenate([swap(part, 1) for part in near], 1)
+    total = total.astype(F32) + near.astype(F32)
+    far = jnp.concatenate([far_a, far_b], 1)
+    return (total + far.astype(F32)).astype(BF16)
 
 
 def solution(mesh):

time: 86.6 us -> 85 us (0.982)
  waiting for transfers between devices: 44.4 us -> 37.6 us
  starting transfers between devices: 25 us -> 29.1 us
    ppermute x16 -> x19, waiting for transfers between devices: 44.4 us -> 37.6 us  [send(): return lax.ppermute(x, axis, pairs)]
    ppermute x16 -> x19, starting transfers between devices: 25 us -> 29.1 us  [send(): return lax.ppermute(x, axis, pairs)]
    pallas_call x2 -> x3, Pallas kernels: 2.99 us -> 3.88 us  [project(): pl.pallas_call(functools.partial(project_kernel, outputs), out_shape=[jax...]
  transfers between devices with their start and end apart: 16 -> 19, of which waited for: 8 -> 9; matrix products, arithmetic and copies ran while one was open for 0% -> 0% of each run, Pallas kernels for 15% -> 17%
where the time goes in v5:
time: 85 us; the launch traced here: 84 us
  waiting for transfers between devices  37.6 us (44%)
  starting transfers between devices  29.1 us (34%)
  Pallas kernels  15.6 us (18%)
  other arithmetic  1.4 us (2%)
    ppermute x19, waiting for transfers between devices, send(): return lax.ppermute(x, axis, pairs)  37.6 us
    ppermute x19, starting transfers between devices, send(): return lax.ppermute(x, axis, pairs)  29.1 us
    pallas_call x1, Pallas kernels, early_attention(): pl.pallas_call(functools.partial(early_kernel, count), out_shape=[jax.Sha...  6.33 us
    pallas_call x1, Pallas kernels, late_weights(): pl.pallas_call(late_kernel, out_shape=[jax.ShapeDtypeStruct((rows, heads...  3.97 us
    pallas_call x3, Pallas kernels, project(): pl.pallas_call(functools.partial(project_kernel, outputs), out_shape=[jax...  3.88 us
  transfers between devices with their start and end apart: 19, of which 9 were waited for; matrix products, arithmetic and copies ran while one was open for 0% of the time, Pallas kernels for 17%

profile of v5, /device:TPU:10, one launch (start us, length us, event | category | flops | bytes accessed | tf_op | source)
XLA Modules:
  0.0 84.0 jit_solution(8042341575885703616)
XLA Ops:
  0.5 5.0 %collective-permute-start.1 = (bf16[256,1280]{1,0:T(8,128)(2,1)}, bf16[256,1280]{1,0:T(8,128)(2,1)S(1)}, u32[]{:S(2)}, u32[]{:S(2)}) collective-permute-start(bf16[256,1280]{1,0:T(8,128)(2,1)} %k_ref.1), channel_id=1, source_target_pairs={{8,16},{12,20},{16,8},{20,12},{9,17},{13,21},{17,9},{21,13},{10,18... | collective-permute-start | bytes 1966088 | tf_op jit(solution)/shard_map/ppermute | solution.py:32
  5.7 1.9 %collective-permute-start.4 = (bf16[256,1280]{1,0:T(8,128)(2,1)}, bf16[256,1280]{1,0:T(8,128)(2,1)S(1)}, u32[]{:S(2)}, u32[]{:S(2)}) collective-permute-start(bf16[256,1280]{1,0:T(8,128)(2,1)} %v_ref.1), channel_id=1, source_target_pairs={{8,16},{12,20},{16,8},{20,12},{9,17},{13,21},{17,9},{21,13},{10,18... | collective-permute-start | bytes 1966088 | tf_op jit(solution)/shard_map/ppermute | solution.py:32
  7.6 10.2 %collective-permute-done.rest_0_ = bf16[256,1280]{1,0:T(8,128)(2,1)S(1)} collective-permute-done((bf16[256,1280]{1,0:T(8,128)(2,1)}, bf16[256,1280]{1,0:T(8,128)(2,1)S(1)}, u32[]{:S(2)}, u32[]{:S(2)}) %collective-permute-start) | collective-permute-done | bytes 655392 | tf_op jit(solution)/shard_map/ppermute | solution.py:32
  18.4 3.1 %collective-permute-done.1.rest_1_ = bf16[256,1280]{1,0:T(8,128)(2,1)S(1)} collective-permute-done((bf16[256,1280]{1,0:T(8,128)(2,1)}, bf16[256,1280]{1,0:T(8,128)(2,1)S(1)}, u32[]{:S(2)}, u32[]{:S(2)}) %collective-permute-start.1) | collective-permute-done | bytes 655392 | tf_op jit(solution)/shard_map/ppermute | solution.py:32
  21.4 1.3 %collective-permute-start.7 = (bf16[256,1280]{1,0:T(8,128)(2,1)S(1)}, bf16[256,1280]{1,0:T(8,128)(2,1)S(1)}, u32[]{:S(2)}, u32[]{:S(2)}) collective-permute-start(bf16[256,1280]{1,0:T(8,128)(2,1)S(1)} %collective-permute-done.1.rest_1_), channel_id=1, source_target_pairs={{8,0},{12,4},{16,24},{20,28},{9,1},{13,5},{17,25},{21,29},{10,2},{... | collective-permute-start | bytes 1966088 | tf_op jit(solution)/shard_map/ppermute | solution.py:32
  22.9 3.5 %collective-permute-start.8 = (bf16[256,1280]{1,0:T(8,128)(2,1)S(1)}, bf16[256,1280]{1,0:T(8,128)(2,1)S(1)}, u32[]{:S(2)}, u32[]{:S(2)}) collective-permute-start(bf16[256,1280]{1,0:T(8,128)(2,1)S(1)} %broadcast_select_fusion.1), channel_id=1, source_target_pairs={{0,4},{8,12},{12,8},{16,20},{20,16},{28,24},{1,5},{9,13},{13,9},{1... | collective-permute-start | bytes 1966088 | tf_op jit(solution)/shard_map/ppermute | solution.py:32
  26.4 4.3 %collective-permute-done.3.rest_3_ = bf16[256,1280]{1,0:T(8,128)(2,1)S(1)} collective-permute-done((bf16[256,1280]{1,0:T(8,128)(2,1)}, bf16[256,1280]{1,0:T(8,128)(2,1)S(1)}, u32[]{:S(2)}, u32[]{:S(2)}) %collective-permute-start.3) | collective-permute-done | bytes 655392 | tf_op jit(solution)/shard_map/ppermute | solution.py:32
  30.7 3.8 %collective-permute-start.6 = (bf16[256,1280]{1,0:T(8,128)(2,1)S(1)}, bf16[256,1280]{1,0:T(8,128)(2,1)S(1)}, u32[]{:S(2)}, u32[]{:S(2)}) collective-permute-start(bf16[256,1280]{1,0:T(8,128)(2,1)S(1)} %collective-permute-done.rest_0_), channel_id=1, source_target_pairs={{8,16},{12,20},{16,8},{20,12},{9,17},{13,21},{17,9},{21,13},{10,18... | collective-permute-start | bytes 1966088 | tf_op jit(solution)/shard_map/ppermute | solution.py:32
  34.6 1.3 %collective-permute-start.10 = (bf16[256,1280]{1,0:T(8,128)(2,1)S(1)}, bf16[256,1280]{1,0:T(8,128)(2,1)S(1)}, u32[]{:S(2)}, u32[]{:S(2)}) collective-permute-start(bf16[256,1280]{1,0:T(8,128)(2,1)S(1)} %collective-permute-done.4.rest_4_), channel_id=1, source_target_pairs={{8,0},{12,4},{16,24},{20,28},{9,1},{13,5},{17,25},{21,29},{10,2},{... | collective-permute-start | bytes 1966088 | tf_op jit(solution)/shard_map/ppermute | solution.py:32
  36.0 3.9 %collective-permute-start.11 = (bf16[256,1280]{1,0:T(8,128)(2,1)S(1)}, bf16[256,1280]{1,0:T(8,128)(2,1)S(1)}, u32[]{:S(2)}, u32[]{:S(2)}) collective-permute-start(bf16[256,1280]{1,0:T(8,128)(2,1)S(1)} %broadcast_select_fusion), channel_id=1, source_target_pairs={{0,4},{8,12},{12,8},{16,20},{20,16},{28,24},{1,5},{9,13},{13,9},{1... | collective-permute-start | bytes 1966088 | tf_op jit(solution)/shard_map/ppermute | solution.py:32
  40.0 6.3 %early_attention.1 = (f32[256,1280]{1,0:T(8,128)S(1)}, f32[256,1280]{1,0:T(8,128)S(1)}, f32[256,1280]{1,0:T(8,128)S(1)}) custom-call(s32[4,32]{1,0:T(4,128)S(1)} %copy-done.4, bf16[256,1280]{1,0:T(8,128)(2,1)S(1)} %copy-done.1, bf16[256,1280]{1,0:T(8,128)(2,1)S(1)} %copy-done.2, bf16[256,1280]{1,0:T(8,128)(2,1)S(1)} %copy-done.3, ...), custom_call_target="tpu_custom_call" | custom-call | tf_op jit(solution)/shard_map/early_attention/pallas_call | solution.py:170
  46.3 3.8 %collective-permute-start.9 = (bf16[256,1280]{1,0:T(8,128)(2,1)S(1)}, bf16[256,1280]{1,0:T(8,128)(2,1)S(1)}, u32[]{:S(2)}, u32[]{:S(2)}) collective-permute-start(bf16[256,1280]{1,0:T(8,128)(2,1)S(1)} %collective-permute-done.3.rest_3_), channel_id=1, source_target_pairs={{8,16},{12,20},{16,8},{20,12},{9,17},{13,21},{17,9},{21,13},{10,18... | collective-permute-start | bytes 1966088 | tf_op jit(solution)/shard_map/ppermute | solution.py:32
  50.2 4.0 %late_weights.1 = (bf16[256,5120]{1,0:T(8,128)(2,1)S(1)}, f32[256,1280]{1,0:T(8,128)S(1)}) custom-call(s32[4,32]{1,0:T(4,128)S(1)} %copy-done.4, bf16[256,1280]{1,0:T(8,128)(2,1)S(1)} %copy-done.1, f32[256,1280]{1,0:T(8,128)S(1)} %get-tuple-element.26.sum_ref, f32[256,1280]{1,0:T(8,128)S(1)} %get-tuple-element.27.peak_ref, ...), custom_call_target="tpu_custom_call" | custom-call | tf_op jit(solution)/shard_map/late_weights/pallas_call | solution.py:225
  54.2 2.6 %collective-permute-done.10.rest_1_ = bf16[256,1280]{1,0:T(8,128)(2,1)S(1)} collective-permute-done((bf16[256,1280]{1,0:T(8,128)(2,1)S(1)}, bf16[256,1280]{1,0:T(8,128)(2,1)S(1)}, u32[]{:S(2)}, u32[]{:S(2)}) %collective-permute-start.10) | collective-permute-done | bytes 655392 | tf_op jit(solution)/shard_map/ppermute | solution.py:32
  56.8 3.8 %collective-permute-done.11.rest_2_ = bf16[256,1280]{1,0:T(8,128)(2,1)S(1)} collective-permute-done((bf16[256,1280]{1,0:T(8,128)(2,1)S(1)}, bf16[256,1280]{1,0:T(8,128)(2,1)S(1)}, u32[]{:S(2)}, u32[]{:S(2)}) %collective-permute-start.11) | collective-permute-done | bytes 655392 | tf_op jit(solution)/shard_map/ppermute | solution.py:32
  60.6 1.9 %collective-permute-done.9.rest_0_ = bf16[256,1280]{1,0:T(8,128)(2,1)S(1)} collective-permute-done((bf16[256,1280]{1,0:T(8,128)(2,1)S(1)}, bf16[256,1280]{1,0:T(8,128)(2,1)S(1)}, u32[]{:S(2)}, u32[]{:S(2)}) %collective-permute-start.9) | collective-permute-done | bytes 655392 | tf_op jit(solution)/shard_map/ppermute | solution.py:32
  62.5 1.4 %first_project.1 = (bf16[256,640]{1,0:T(8,128)(2,1)S(1)}, bf16[256,1280]{1,0:T(8,128)(2,1)S(1)}) custom-call(f32[256,1280]{1,0:T(8,128)S(1)} %get-tuple-element.30.scaled_ref, bf16[256,5120]{1,0:T(8,128)(2,1)S(1)} %get-tuple-element.31.weights_ref, bf16[256,1280]{1,0:T(8,128)(2,1)S(1)} %collective-permute-done.9.rest_0_, ...), custom_call_target="tpu_custom_call" | custom-call | tf_op jit(solution)/shard_map/first_project/pallas_call | solution.py:273
  64.0 1.3 %project.3 = (bf16[256,640]{1,0:T(8,128)(2,1)S(1)}, bf16[256,640]{1,0:T(8,128)(2,1)S(1)}) custom-call(bf16[256,1280]{1,0:T(8,128)(2,1)S(1)} %get-tuple-element.40.a_ref, bf16[1280,5120]{1,0:T(8,128)(2,1)S(1)} %copy-done), custom_call_target="tpu_custom_call" | custom-call | tf_op jit(solution)/shard_map/project/pallas_call | solution.py:294
  65.9 1.6 %collective-permute-start.17 = (bf16[256,640]{1,0:T(8,128)(2,1)S(1)}, bf16[256,640]{1,0:T(8,128)(2,1)S(1)}, u32[]{:S(2)}, u32[]{:S(2)}) collective-permute-start(bf16[256,640]{1,0:T(8,128)(2,1)S(1)} %add_convert_fusion.2), channel_id=1, source_target_pairs={{0,2},{1,3},{2,0},{3,1},{4,6},{5,7},{6,4},{7,5},{8,10},{9,11},{10,... | collective-permute-start | bytes 983048 | tf_op jit(solution)/shard_map/ppermute | solution.py:32
  68.3 0.8 collective-permute-start.18
  69.1 1.9 %project.5 = (bf16[256,512]{1,0:T(8,128)(2,1)S(1)}, bf16[256,512]{1,0:T(8,128)(2,1)S(1)}, bf16[256,256]{1,0:T(8,128)(2,1)S(1)}, bf16[256,1280]{1,0:T(8,128)(2,1)S(1)}) custom-call(bf16[256,1280]{1,0:T(8,128)(2,1)S(1)} %get-tuple-element.40.a_ref, bf16[1280,5120]{1,0:T(8,128)(2,1)S(1)} %copy-done), custom_call_target="tpu_custom_call" | custom-call | tf_op jit(solution)/shard_map/project/pallas_call | solution.py:294
  71.7 4.8 %collective-permute-done.17 = bf16[256,640]{1,0:T(8,128)(2,1)S(1)} collective-permute-done((bf16[256,640]{1,0:T(8,128)(2,1)S(1)}, bf16[256,640]{1,0:T(8,128)(2,1)S(1)}, u32[]{:S(2)}, u32[]{:S(2)}) %collective-permute-start.17) | collective-permute-done | bytes 327712 | tf_op jit(solution)/shard_map/ppermute | solution.py:32
  76.5 6.5 %collective-permute-done.18 = bf16[256,640]{1,0:T(8,128)(2,1)S(1)} collective-permute-done((bf16[256,640]{1,0:T(8,128)(2,1)S(1)}, bf16[256,640]{1,0:T(8,128)(2,1)S(1)}, u32[]{:S(2)}, u32[]{:S(2)}) %collective-permute-start.18) | collective-permute-done | bytes 327712 | tf_op jit(solution)/shard_map/ppermute | solution.py:32
  82.9 1.1 %add_convert_fusion = bf16[256,1280]{1,0:T(8,128)(2,1)} fusion(bf16[256,1280]{1,0:T(8,128)(2,1)S(1)} %get-tuple-element.41, bf16[256,256]{1,0:T(8,128)(2,1)S(1)} %collective-permute-done.16, bf16[256,512]{1,0:T(8,128)(2,1)S(1)} %collective-permute-done.15, bf16[256,512]{1,0:T(8,128)(2,1)S(1)} %collective-permute-done.14, ...), kind=kLoop, calls=%fused_computation | loop fusion | flops 4587520 | bytes 2621440 | tf_op jit(solution)/shard_map/convert_element_type | solution.py:352
  (35 shorter events, 3.5 us)
Async XLA Ops:
  0.0 17.8 %collective-permute-start = (bf16[256,1280]{1,0:T(8,128)(2,1)}, bf16[256,1280]{1,0:T(8,128)(2,1)S(1)}, u32[]{:S(2)}, u32[]{:S(2)}) collective-permute-start(bf16[256,1280]{1,0:T(8,128)(2,1)} %k_ref.1), channel_id=1, source_target_pairs={{0,8},{4,12},{8,0},{12,4},{16,24},{20,28},{24,16},{28,20},{1,9},{5... | collective-permute-start | bytes 1966088 | tf_op jit(solution)/shard_map/ppermute | solution.py:32
  0.5 17.4 %collective-permute-start.2 = (bf16[256,1280]{1,0:T(8,128)(2,1)}, bf16[256,1280]{1,0:T(8,128)(2,1)S(1)}, u32[]{:S(2)}, u32[]{:S(2)}) collective-permute-start(bf16[256,1280]{1,0:T(8,128)(2,1)} %k_ref.1), channel_id=1, source_target_pairs={{0,4},{4,0},{8,12},{12,8},{16,20},{20,16},{24,28},{28,24},{1,5},{5... | collective-permute-start | bytes 1966088 | tf_op jit(solution)/shard_map/ppermute | solution.py:32
  0.5 20.9 %collective-permute-start.1 = (bf16[256,1280]{1,0:T(8,128)(2,1)}, bf16[256,1280]{1,0:T(8,128)(2,1)S(1)}, u32[]{:S(2)}, u32[]{:S(2)}) collective-permute-start(bf16[256,1280]{1,0:T(8,128)(2,1)} %k_ref.1), channel_id=1, source_target_pairs={{8,16},{12,20},{16,8},{20,12},{9,17},{13,21},{17,9},{21,13},{10,18... | collective-permute-start | bytes 1966088 | tf_op jit(solution)/shard_map/ppermute | solution.py:32
  5.6 25.1 %collective-permute-start.3 = (bf16[256,1280]{1,0:T(8,128)(2,1)}, bf16[256,1280]{1,0:T(8,128)(2,1)S(1)}, u32[]{:S(2)}, u32[]{:S(2)}) collective-permute-start(bf16[256,1280]{1,0:T(8,128)(2,1)} %v_ref.1), channel_id=1, source_target_pairs={{0,8},{4,12},{8,0},{12,4},{16,24},{20,28},{24,16},{28,20},{1,9},{5... | collective-permute-start | bytes 1966088 | tf_op jit(solution)/shard_map/ppermute | solution.py:32
  5.7 28.9 %collective-permute-start.4 = (bf16[256,1280]{1,0:T(8,128)(2,1)}, bf16[256,1280]{1,0:T(8,128)(2,1)S(1)}, u32[]{:S(2)}, u32[]{:S(2)}) collective-permute-start(bf16[256,1280]{1,0:T(8,128)(2,1)} %v_ref.1), channel_id=1, source_target_pairs={{8,16},{12,20},{16,8},{20,12},{9,17},{13,21},{17,9},{21,13},{10,18... | collective-permute-start | bytes 1966088 | tf_op jit(solution)/shard_map/ppermute | solution.py:32
  17.8 18.2 %collective-permute-start.5 = (bf16[256,1280]{1,0:T(8,128)(2,1)}, bf16[256,1280]{1,0:T(8,128)(2,1)S(1)}, u32[]{:S(2)}, u32[]{:S(2)}) collective-permute-start(bf16[256,1280]{1,0:T(8,128)(2,1)} %v_ref.1), channel_id=1, source_target_pairs={{0,4},{4,0},{8,12},{12,8},{16,20},{20,16},{24,28},{28,24},{1,5},{5... | collective-permute-start | bytes 1966088 | tf_op jit(solution)/shard_map/ppermute | solution.py:32
  21.4 24.9 %collective-permute-start.7 = (bf16[256,1280]{1,0:T(8,128)(2,1)S(1)}, bf16[256,1280]{1,0:T(8,128)(2,1)S(1)}, u32[]{:S(2)}, u32[]{:S(2)}) collective-permute-start(bf16[256,1280]{1,0:T(8,128)(2,1)S(1)} %collective-permute-done.1.rest_1_), channel_id=1, source_target_pairs={{8,0},{12,4},{16,24},{20,28},{9,1},{13,5},{17,25},{21,29},{10,2},{... | collective-permute-start | bytes 1966088 | tf_op jit(solution)/shard_map/ppermute | solution.py:32
  22.8 17.2 %copy-start.3 = (bf16[256,1280]{1,0:T(8,128)(2,1)S(1)}, bf16[256,1280]{1,0:T(8,128)(2,1)}, u32[]{:S(2)}) copy-start(bf16[256,1280]{1,0:T(8,128)(2,1)} %v_ref.1) | copy-start | bytes 1966084
  22.8 17.1 %copy-start.1 = (bf16[256,1280]{1,0:T(8,128)(2,1)S(1)}, bf16[256,1280]{1,0:T(8,128)(2,1)}, u32[]{:S(2)}) copy-start(bf16[256,1280]{1,0:T(8,128)(2,1)} %q_ref.3) | copy-start | bytes 1966084
  22.9 17.1 %copy-start.2 = (bf16[256,1280]{1,0:T(8,128)(2,1)S(1)}, bf16[256,1280]{1,0:T(8,128)(2,1)}, u32[]{:S(2)}) copy-start(bf16[256,1280]{1,0:T(8,128)(2,1)} %k_ref.1) | copy-start | bytes 1966084
  22.9 17.1 %copy-start.4 = (s32[4,32]{1,0:T(4,128)S(1)}, s32[4,32]{1,0:T(4,128)}, u32[]{:S(2)}) copy-start(s32[4,32]{1,0:T(4,128)} %live_ref.3) | copy-start | bytes 1540
  22.9 27.3 %collective-permute-start.8 = (bf16[256,1280]{1,0:T(8,128)(2,1)S(1)}, bf16[256,1280]{1,0:T(8,128)(2,1)S(1)}, u32[]{:S(2)}, u32[]{:S(2)}) collective-permute-start(bf16[256,1280]{1,0:T(8,128)(2,1)S(1)} %broadcast_select_fusion.1), channel_id=1, source_target_pairs={{0,4},{8,12},{12,8},{16,20},{20,16},{28,24},{1,5},{9,13},{13,9},{1... | collective-permute-start | bytes 1966088 | tf_op jit(solution)/shard_map/ppermute | solution.py:32
  30.7 19.4 %collective-permute-start.6 = (bf16[256,1280]{1,0:T(8,128)(2,1)S(1)}, bf16[256,1280]{1,0:T(8,128)(2,1)S(1)}, u32[]{:S(2)}, u32[]{:S(2)}) collective-permute-start(bf16[256,1280]{1,0:T(8,128)(2,1)S(1)} %collective-permute-done.rest_0_), channel_id=1, source_target_pairs={{8,16},{12,20},{16,8},{20,12},{9,17},{13,21},{17,9},{21,13},{10,18... | collective-permute-start | bytes 1966088 | tf_op jit(solution)/shard_map/ppermute | solution.py:32
  34.6 22.2 %collective-permute-start.10 = (bf16[256,1280]{1,0:T(8,128)(2,1)S(1)}, bf16[256,1280]{1,0:T(8,128)(2,1)S(1)}, u32[]{:S(2)}, u32[]{:S(2)}) collective-permute-start(bf16[256,1280]{1,0:T(8,128)(2,1)S(1)} %collective-permute-done.4.rest_4_), channel_id=1, source_target_pairs={{8,0},{12,4},{16,24},{20,28},{9,1},{13,5},{17,25},{21,29},{10,2},{... | collective-permute-start | bytes 1966088 | tf_op jit(solution)/shard_map/ppermute | solution.py:32
  35.9 26.6 %copy-start = (bf16[1280,5120]{1,0:T(8,128)(2,1)S(1)}, bf16[1280,5120]{1,0:T(8,128)(2,1)}, u32[]{:S(2)}) copy-start(bf16[1280,5120]{1,0:T(8,128)(2,1)} %w_ref.5) | copy-start | bytes 39321604
  36.0 24.6 %collective-permute-start.11 = (bf16[256,1280]{1,0:T(8,128)(2,1)S(1)}, bf16[256,1280]{1,0:T(8,128)(2,1)S(1)}, u32[]{:S(2)}, u32[]{:S(2)}) collective-permute-start(bf16[256,1280]{1,0:T(8,128)(2,1)S(1)} %broadcast_select_fusion), channel_id=1, source_target_pairs={{0,4},{8,12},{12,8},{16,20},{20,16},{28,24},{1,5},{9,13},{13,9},{1... | collective-permute-start | bytes 1966088 | tf_op jit(solution)/shard_map/ppermute | solution.py:32
  46.3 16.2 %collective-permute-start.9 = (bf16[256,1280]{1,0:T(8,128)(2,1)S(1)}, bf16[256,1280]{1,0:T(8,128)(2,1)S(1)}, u32[]{:S(2)}, u32[]{:S(2)}) collective-permute-start(bf16[256,1280]{1,0:T(8,128)(2,1)S(1)} %collective-permute-done.3.rest_3_), channel_id=1, source_target_pairs={{8,16},{12,20},{16,8},{20,12},{9,17},{13,21},{17,9},{21,13},{10,18... | collective-permute-start | bytes 1966088 | tf_op jit(solution)/shard_map/ppermute | solution.py:32
  63.9 1.7 %collective-permute-start.12 = (bf16[256,640]{1,0:T(8,128)(2,1)S(1)}, bf16[256,640]{1,0:T(8,128)(2,1)S(1)}, u32[]{:S(2)}, u32[]{:S(2)}) collective-permute-start(bf16[256,640]{1,0:T(8,128)(2,1)S(1)} %get-tuple-element.36), channel_id=1, source_target_pairs={{0,1},{1,0},{2,3},{3,2},{4,5},{5,4},{6,7},{7,6},{8,9},{9,8},{10,11... | collective-permute-start | bytes 983048 | tf_op jit(solution)/shard_map/ppermute | solution.py:32
  65.7 2.5 %collective-permute-start.13 = (bf16[256,640]{1,0:T(8,128)(2,1)S(1)}, bf16[256,640]{1,0:T(8,128)(2,1)S(1)}, u32[]{:S(2)}, u32[]{:S(2)}) collective-permute-start(bf16[256,640]{1,0:T(8,128)(2,1)S(1)} %get-tuple-element.39), channel_id=1, source_target_pairs={{0,1},{1,0},{2,3},{3,2},{4,5},{5,4},{6,7},{7,6},{8,9},{9,8},{10,11... | collective-permute-start | bytes 983048 | tf_op jit(solution)/shard_map/ppermute | solution.py:32
  65.9 10.5 %collective-permute-start.17 = (bf16[256,640]{1,0:T(8,128)(2,1)S(1)}, bf16[256,640]{1,0:T(8,128)(2,1)S(1)}, u32[]{:S(2)}, u32[]{:S(2)}) collective-permute-start(bf16[256,640]{1,0:T(8,128)(2,1)S(1)} %add_convert_fusion.2), channel_id=1, source_target_pairs={{0,2},{1,3},{2,0},{3,1},{4,6},{5,7},{6,4},{7,5},{8,10},{9,11},{10,... | collective-permute-start | bytes 983048 | tf_op jit(solution)/shard_map/ppermute | solution.py:32
  68.3 14.7 %collective-permute-start.18 = (bf16[256,640]{1,0:T(8,128)(2,1)S(1)}, bf16[256,640]{1,0:T(8,128)(2,1)S(1)}, u32[]{:S(2)}, u32[]{:S(2)}) collective-permute-start(bf16[256,640]{1,0:T(8,128)(2,1)S(1)} %add_convert_fusion.1), channel_id=1, source_target_pairs={{0,2},{1,3},{2,0},{3,1},{4,6},{5,7},{6,4},{7,5},{8,10},{9,11},{10,... | collective-permute-start | bytes 983048 | tf_op jit(solution)/shard_map/ppermute | solution.py:32
  71.0 5.5 %collective-permute-start.14 = (bf16[256,512]{1,0:T(8,128)(2,1)S(1)}, bf16[256,512]{1,0:T(8,128)(2,1)S(1)}, u32[]{:S(2)}, u32[]{:S(2)}) collective-permute-start(bf16[256,512]{1,0:T(8,128)(2,1)S(1)} %get-tuple-element.42), channel_id=1, source_target_pairs={{0,1},{1,0},{2,3},{3,2},{4,5},{5,4},{6,7},{7,6},{8,9},{9,8},{10,11... | collective-permute-start | bytes 786440 | tf_op jit(solution)/shard_map/ppermute | solution.py:32
  71.1 5.4 %collective-permute-start.15 = (bf16[256,512]{1,0:T(8,128)(2,1)S(1)}, bf16[256,512]{1,0:T(8,128)(2,1)S(1)}, u32[]{:S(2)}, u32[]{:S(2)}) collective-permute-start(bf16[256,512]{1,0:T(8,128)(2,1)S(1)} %get-tuple-element.43), channel_id=1, source_target_pairs={{0,1},{1,0},{2,3},{3,2},{4,5},{5,4},{6,7},{7,6},{8,9},{9,8},{10,11... | collective-permute-start | bytes 786440 | tf_op jit(solution)/shard_map/ppermute | solution.py:32
  71.6 4.9 %collective-permute-start.16 = (bf16[256,256]{1,0:T(8,128)(2,1)S(1)}, bf16[256,256]{1,0:T(8,128)(2,1)S(1)}, u32[]{:S(2)}, u32[]{:S(2)}) collective-permute-start(bf16[256,256]{1,0:T(8,128)(2,1)S(1)} %get-tuple-element.44), channel_id=1, source_target_pairs={{0,1},{1,0},{2,3},{3,2},{4,5},{5,4},{6,7},{7,6},{8,9},{9,8},{10,11... | collective-permute-start | bytes 393224 | tf_op jit(solution)/shard_map/ppermute | solution.py:32

commit v6 on v5

--- a/solution.py
+++ b/solution.py
@@ -251,19 +251,43 @@
         base += width
 
 
+def add_values(acc, weights_ref, values, group, first, h, n, places):
+    rows = weights_ref.shape[0]
+    value = pick(values, group, slice(h * HDIM, (h + 1) * HDIM), first)
+    at = (h * places + n) * rows
+    return acc + jnp.dot(weights_ref[:, at : at + rows], value, preferred_element_type=F32)
+
+
+def second_place_kernel(scaled_ref, weights_ref, value_ref, out_ref):
+    _, _, groups, first = plan(lax.axis_index("frame"), lax.axis_size("frame"))
+    for h in range(scaled_ref.shape[1] // HDIM):
+        columns = slice(h * HDIM, (h + 1) * HDIM)
+        out_ref[:, columns] = add_values(
+            scaled_ref[:, columns], weights_ref, (value_ref,), (0,), first, h, 1, len(groups)
+        )
+
+
+def second_place(scaled, weights, value):
+    return pl.pallas_call(
+        second_place_kernel,
+        out_shape=jax.ShapeDtypeStruct(scaled.shape, F32),
+        in_specs=[VMEM] * 3,
+        out_specs=VMEM,
+        compiler_params=params(),
+        cost_estimate=LIGHT,
+        name="second_place",
+    )(scaled, weights, value)
+
+
 def first_project_kernel(count, scaled_ref, weights_ref, *rest):
     values = rest[:count]
     w_ref, out_ref, att_ref = rest[count:]
-    rows, width = scaled_ref.shape
     _, _, groups, first = plan(lax.axis_index("frame"), lax.axis_size("frame"))
-    seen = rows * len(groups)
-    for h in range(width // HDIM):
+    for h in range(scaled_ref.shape[1] // HDIM):
         columns = slice(h * HDIM, (h + 1) * HDIM)
-        acc = scaled_ref[:, columns]
-        for n, group in enumerate(groups):
-            value = pick(values, group, columns, first)
-            weight = weights_ref[:, h * seen + n * rows : h * seen + (n + 1) * rows]
-            acc += jnp.dot(weight, value, preferred_element_type=F32)
+        acc = add_values(
+            scaled_ref[:, columns], weights_ref, values, groups[0], first, h, 0, len(groups)
+        )
         att_ref[:, columns] = acc.astype(BF16)
     multiply(att_ref, w_ref, out_ref, (3, 0, out_ref.shape[1]))
 
@@ -333,7 +357,8 @@
     columns = out_weight.shape[1] // lax.axis_size("head")
     cut = columns // 2
     rest = columns - cut
-    sibling_a, attended = first_project(scaled, weights, late_values, out_weight, cut)
+    scaled = second_place(scaled, weights, late_values[-1])
+    sibling_a, attended = first_project(scaled, weights, late_values[:-1], out_weight, cut)
     sibling_b, mine_a = project(attended, out_weight, ((3, cut, rest),), ((2, 0, cut),))
     crossed_a = add(mine_a, swap(sibling_a, 1))
     far_a = swap(crossed_a, 2)

time: 85 us -> 84.7 us (level)
  transfers between devices with their start and end apart: 19 -> 19, of which waited for: 9 -> 8; matrix products, arithmetic and copies ran while one was open for 0% -> 0% of each run, Pallas kernels for 17% -> 18%
where the time goes in v6:
time: 84.7 us; the launch traced here: 83.4 us
  waiting for transfers between devices  37.2 us (44%)
  starting transfers between devices  28.8 us (34%)
  Pallas kernels  15.8 us (19%)
  other arithmetic  1.4 us (2%)
    ppermute x19, waiting for transfers between devices, send(): return lax.ppermute(x, axis, pairs)  37.2 us
    ppermute x19, starting transfers between devices, send(): return lax.ppermute(x, axis, pairs)  28.8 us
    pallas_call x1, Pallas kernels, early_attention(): pl.pallas_call(functools.partial(early_kernel, count), out_shape=[jax.Sha...  6.33 us
    pallas_call x1, Pallas kernels, late_weights(): pl.pallas_call(late_kernel, out_shape=[jax.ShapeDtypeStruct((rows, heads...  3.97 us
    pallas_call x3, Pallas kernels, project(): pl.pallas_call(functools.partial(project_kernel, outputs), out_shape=[jax...  3.89 us
  transfers between devices with their start and end apart: 19, of which 8 were waited for; matrix products, arithmetic and copies ran while one was open for 0% of the time, Pallas kernels for 18%

profile of v6, /device:TPU:10, one launch (start us, length us, event | category | flops | bytes accessed | tf_op | source)
XLA Modules:
  0.0 83.4 jit_solution(7661813067658067436)
XLA Ops:
  0.5 5.0 %collective-permute-start.1 = (bf16[256,1280]{1,0:T(8,128)(2,1)}, bf16[256,1280]{1,0:T(8,128)(2,1)S(1)}, u32[]{:S(2)}, u32[]{:S(2)}) collective-permute-start(bf16[256,1280]{1,0:T(8,128)(2,1)} %k_ref.1), channel_id=1, source_target_pairs={{8,16},{12,20},{16,8},{20,12},{9,17},{13,21},{17,9},{21,13},{10,18... | collective-permute-start | bytes 1966088 | tf_op jit(solution)/shard_map/ppermute | solution.py:32
  5.7 1.9 %collective-permute-start.4 = (bf16[256,1280]{1,0:T(8,128)(2,1)}, bf16[256,1280]{1,0:T(8,128)(2,1)S(1)}, u32[]{:S(2)}, u32[]{:S(2)}) collective-permute-start(bf16[256,1280]{1,0:T(8,128)(2,1)} %v_ref.1), channel_id=1, source_target_pairs={{8,16},{12,20},{16,8},{20,12},{9,17},{13,21},{17,9},{21,13},{10,18... | collective-permute-start | bytes 1966088 | tf_op jit(solution)/shard_map/ppermute | solution.py:32
  7.6 10.2 %collective-permute-done.rest_0_ = bf16[256,1280]{1,0:T(8,128)(2,1)S(1)} collective-permute-done((bf16[256,1280]{1,0:T(8,128)(2,1)}, bf16[256,1280]{1,0:T(8,128)(2,1)S(1)}, u32[]{:S(2)}, u32[]{:S(2)}) %collective-permute-start) | collective-permute-done | bytes 655392 | tf_op jit(solution)/shard_map/ppermute | solution.py:32
  18.4 3.1 %collective-permute-done.1.rest_1_ = bf16[256,1280]{1,0:T(8,128)(2,1)S(1)} collective-permute-done((bf16[256,1280]{1,0:T(8,128)(2,1)}, bf16[256,1280]{1,0:T(8,128)(2,1)S(1)}, u32[]{:S(2)}, u32[]{:S(2)}) %collective-permute-start.1) | collective-permute-done | bytes 655392 | tf_op jit(solution)/shard_map/ppermute | solution.py:32
  21.4 1.3 %collective-permute-start.7 = (bf16[256,1280]{1,0:T(8,128)(2,1)S(1)}, bf16[256,1280]{1,0:T(8,128)(2,1)S(1)}, u32[]{:S(2)}, u32[]{:S(2)}) collective-permute-start(bf16[256,1280]{1,0:T(8,128)(2,1)S(1)} %collective-permute-done.1.rest_1_), channel_id=1, source_target_pairs={{8,0},{12,4},{16,24},{20,28},{9,1},{13,5},{17,25},{21,29},{10,2},{... | collective-permute-start | bytes 1966088 | tf_op jit(solution)/shard_map/ppermute | solution.py:32
  22.9 3.5 %collective-permute-start.8 = (bf16[256,1280]{1,0:T(8,128)(2,1)S(1)}, bf16[256,1280]{1,0:T(8,128)(2,1)S(1)}, u32[]{:S(2)}, u32[]{:S(2)}) collective-permute-start(bf16[256,1280]{1,0:T(8,128)(2,1)S(1)} %broadcast_select_fusion.1), channel_id=1, source_target_pairs={{0,4},{8,12},{12,8},{16,20},{20,16},{28,24},{1,5},{9,13},{13,9},{1... | collective-permute-start | bytes 1966088 | tf_op jit(solution)/shard_map/ppermute | solution.py:32
  26.4 4.3 %collective-permute-done.3.rest_3_ = bf16[256,1280]{1,0:T(8,128)(2,1)S(1)} collective-permute-done((bf16[256,1280]{1,0:T(8,128)(2,1)}, bf16[256,1280]{1,0:T(8,128)(2,1)S(1)}, u32[]{:S(2)}, u32[]{:S(2)}) %collective-permute-start.3) | collective-permute-done | bytes 655392 | tf_op jit(solution)/shard_map/ppermute | solution.py:32
  30.7 3.8 %collective-permute-start.6 = (bf16[256,1280]{1,0:T(8,128)(2,1)S(1)}, bf16[256,1280]{1,0:T(8,128)(2,1)S(1)}, u32[]{:S(2)}, u32[]{:S(2)}) collective-permute-start(bf16[256,1280]{1,0:T(8,128)(2,1)S(1)} %collective-permute-done.rest_0_), channel_id=1, source_target_pairs={{8,16},{12,20},{16,8},{20,12},{9,17},{13,21},{17,9},{21,13},{10,18... | collective-permute-start | bytes 1966088 | tf_op jit(solution)/shard_map/ppermute | solution.py:32
  34.6 1.3 %collective-permute-start.11 = (bf16[256,1280]{1,0:T(8,128)(2,1)S(1)}, bf16[256,1280]{1,0:T(8,128)(2,1)S(1)}, u32[]{:S(2)}, u32[]{:S(2)}) collective-permute-start(bf16[256,1280]{1,0:T(8,128)(2,1)S(1)} %collective-permute-done.4.rest_4_), channel_id=1, source_target_pairs={{8,0},{12,4},{16,24},{20,28},{9,1},{13,5},{17,25},{21,29},{10,2},{... | collective-permute-start | bytes 1966088 | tf_op jit(solution)/shard_map/ppermute | solution.py:32
  36.0 3.6 %collective-permute-start.9 = (bf16[256,1280]{1,0:T(8,128)(2,1)S(1)}, bf16[256,1280]{1,0:T(8,128)(2,1)S(1)}, u32[]{:S(2)}, u32[]{:S(2)}) collective-permute-start(bf16[256,1280]{1,0:T(8,128)(2,1)S(1)} %broadcast_select_fusion), channel_id=1, source_target_pairs={{0,4},{8,12},{12,8},{16,20},{20,16},{28,24},{1,5},{9,13},{13,9},{1... | collective-permute-start | bytes 1966088 | tf_op jit(solution)/shard_map/ppermute | solution.py:32
  39.6 6.3 %early_attention.1 = (f32[256,1280]{1,0:T(8,128)S(1)}, f32[256,1280]{1,0:T(8,128)S(1)}, f32[256,1280]{1,0:T(8,128)S(1)}) custom-call(s32[4,32]{1,0:T(4,128)S(1)} %copy-done.4, bf16[256,1280]{1,0:T(8,128)(2,1)S(1)} %copy-done.1, bf16[256,1280]{1,0:T(8,128)(2,1)S(1)} %copy-done.2, bf16[256,1280]{1,0:T(8,128)(2,1)S(1)} %copy-done.3, ...), custom_call_target="tpu_custom_call" | custom-call | tf_op jit(solution)/shard_map/early_attention/pallas_call | solution.py:170
  46.0 3.8 %collective-permute-start.10 = (bf16[256,1280]{1,0:T(8,128)(2,1)S(1)}, bf16[256,1280]{1,0:T(8,128)(2,1)S(1)}, u32[]{:S(2)}, u32[]{:S(2)}) collective-permute-start(bf16[256,1280]{1,0:T(8,128)(2,1)S(1)} %collective-permute-done.3.rest_3_), channel_id=1, source_target_pairs={{8,16},{12,20},{16,8},{20,12},{9,17},{13,21},{17,9},{21,13},{10,18... | collective-permute-start | bytes 1966088 | tf_op jit(solution)/shard_map/ppermute | solution.py:32
  49.8 4.0 %late_weights.1 = (bf16[256,5120]{1,0:T(8,128)(2,1)S(1)}, f32[256,1280]{1,0:T(8,128)S(1)}) custom-call(s32[4,32]{1,0:T(4,128)S(1)} %copy-done.4, bf16[256,1280]{1,0:T(8,128)(2,1)S(1)} %copy-done.1, f32[256,1280]{1,0:T(8,128)S(1)} %get-tuple-element.26.sum_ref, f32[256,1280]{1,0:T(8,128)S(1)} %get-tuple-element.27.peak_ref, ...), custom_call_target="tpu_custom_call" | custom-call | tf_op jit(solution)/shard_map/late_weights/pallas_call | solution.py:225
  53.8 6.8 %collective-permute-done.9.value_ref = bf16[256,1280]{1,0:T(8,128)(2,1)S(1)} collective-permute-done((bf16[256,1280]{1,0:T(8,128)(2,1)S(1)}, bf16[256,1280]{1,0:T(8,128)(2,1)S(1)}, u32[]{:S(2)}, u32[]{:S(2)}) %collective-permute-start.9) | collective-permute-done | bytes 655392 | tf_op jit(solution)/shard_map/ppermute | solution.py:32
  61.1 1.2 %collective-permute-done.10.rest_0_ = bf16[256,1280]{1,0:T(8,128)(2,1)S(1)} collective-permute-done((bf16[256,1280]{1,0:T(8,128)(2,1)S(1)}, bf16[256,1280]{1,0:T(8,128)(2,1)S(1)}, u32[]{:S(2)}, u32[]{:S(2)}) %collective-permute-start.10) | collective-permute-done | bytes 655392 | tf_op jit(solution)/shard_map/ppermute | solution.py:32
  62.3 1.1 %first_project.1 = (bf16[256,640]{1,0:T(8,128)(2,1)S(1)}, bf16[256,1280]{1,0:T(8,128)(2,1)S(1)}) custom-call(f32[256,1280]{1,0:T(8,128)S(1)} %second_place.1.scaled_ref, bf16[256,5120]{1,0:T(8,128)(2,1)S(1)} %get-tuple-element.31.weights_ref, bf16[256,1280]{1,0:T(8,128)(2,1)S(1)} %collective-permute-done.10.rest_0_, ...), custom_call_target="tpu_custom_call" | custom-call | tf_op jit(solution)/shard_map/first_project/pallas_call | solution.py:297
  63.4 1.3 %project.3 = (bf16[256,640]{1,0:T(8,128)(2,1)S(1)}, bf16[256,640]{1,0:T(8,128)(2,1)S(1)}) custom-call(bf16[256,1280]{1,0:T(8,128)(2,1)S(1)} %get-tuple-element.40.a_ref, bf16[1280,5120]{1,0:T(8,128)(2,1)S(1)} %copy-done), custom_call_target="tpu_custom_call" | custom-call | tf_op jit(solution)/shard_map/project/pallas_call | solution.py:318
  65.3 1.6 %collective-permute-start.17 = (bf16[256,640]{1,0:T(8,128)(2,1)S(1)}, bf16[256,640]{1,0:T(8,128)(2,1)S(1)}, u32[]{:S(2)}, u32[]{:S(2)}) collective-permute-start(bf16[256,640]{1,0:T(8,128)(2,1)S(1)} %add_convert_fusion.2), channel_id=1, source_target_pairs={{0,2},{1,3},{2,0},{3,1},{4,6},{5,7},{6,4},{7,5},{8,10},{9,11},{10,... | collective-permute-start | bytes 983048 | tf_op jit(solution)/shard_map/ppermute | solution.py:32
  66.9 0.7 project.4
  67.7 0.8 collective-permute-start.18
  68.5 1.9 %project.5 = (bf16[256,512]{1,0:T(8,128)(2,1)S(1)}, bf16[256,512]{1,0:T(8,128)(2,1)S(1)}, bf16[256,256]{1,0:T(8,128)(2,1)S(1)}, bf16[256,1280]{1,0:T(8,128)(2,1)S(1)}) custom-call(bf16[256,1280]{1,0:T(8,128)(2,1)S(1)} %get-tuple-element.40.a_ref, bf16[1280,5120]{1,0:T(8,128)(2,1)S(1)} %copy-done), custom_call_target="tpu_custom_call" | custom-call | tf_op jit(solution)/shard_map/project/pallas_call | solution.py:318
  71.1 4.8 %collective-permute-done.17 = bf16[256,640]{1,0:T(8,128)(2,1)S(1)} collective-permute-done((bf16[256,640]{1,0:T(8,128)(2,1)S(1)}, bf16[256,640]{1,0:T(8,128)(2,1)S(1)}, u32[]{:S(2)}, u32[]{:S(2)}) %collective-permute-start.17) | collective-permute-done | bytes 327712 | tf_op jit(solution)/shard_map/ppermute | solution.py:32
  75.9 6.5 %collective-permute-done.18 = bf16[256,640]{1,0:T(8,128)(2,1)S(1)} collective-permute-done((bf16[256,640]{1,0:T(8,128)(2,1)S(1)}, bf16[256,640]{1,0:T(8,128)(2,1)S(1)}, u32[]{:S(2)}, u32[]{:S(2)}) %collective-permute-start.18) | collective-permute-done | bytes 327712 | tf_op jit(solution)/shard_map/ppermute | solution.py:32
  82.3 1.1 %add_convert_fusion = bf16[256,1280]{1,0:T(8,128)(2,1)} fusion(bf16[256,1280]{1,0:T(8,128)(2,1)S(1)} %get-tuple-element.41, bf16[256,256]{1,0:T(8,128)(2,1)S(1)} %collective-permute-done.16, bf16[256,512]{1,0:T(8,128)(2,1)S(1)} %collective-permute-done.15, bf16[256,512]{1,0:T(8,128)(2,1)S(1)} %collective-permute-done.14, ...), kind=kLoop, calls=%fused_computation | loop fusion | flops 4587520 | bytes 2621440 | tf_op jit(solution)/shard_map/convert_element_type | solution.py:377
  (36 shorter events, 3.3 us)
Async XLA Ops:
  0.0 17.8 %collective-permute-start = (bf16[256,1280]{1,0:T(8,128)(2,1)}, bf16[256,1280]{1,0:T(8,128)(2,1)S(1)}, u32[]{:S(2)}, u32[]{:S(2)}) collective-permute-start(bf16[256,1280]{1,0:T(8,128)(2,1)} %k_ref.1), channel_id=1, source_target_pairs={{0,8},{4,12},{8,0},{12,4},{16,24},{20,28},{24,16},{28,20},{1,9},{5... | collective-permute-start | bytes 1966088 | tf_op jit(solution)/shard_map/ppermute | solution.py:32
  0.5 17.4 %collective-permute-start.2 = (bf16[256,1280]{1,0:T(8,128)(2,1)}, bf16[256,1280]{1,0:T(8,128)(2,1)S(1)}, u32[]{:S(2)}, u32[]{:S(2)}) collective-permute-start(bf16[256,1280]{1,0:T(8,128)(2,1)} %k_ref.1), channel_id=1, source_target_pairs={{0,4},{4,0},{8,12},{12,8},{16,20},{20,16},{24,28},{28,24},{1,5},{5... | collective-permute-start | bytes 1966088 | tf_op jit(solution)/shard_map/ppermute | solution.py:32
  0.5 20.9 %collective-permute-start.1 = (bf16[256,1280]{1,0:T(8,128)(2,1)}, bf16[256,1280]{1,0:T(8,128)(2,1)S(1)}, u32[]{:S(2)}, u32[]{:S(2)}) collective-permute-start(bf16[256,1280]{1,0:T(8,128)(2,1)} %k_ref.1), channel_id=1, source_target_pairs={{8,16},{12,20},{16,8},{20,12},{9,17},{13,21},{17,9},{21,13},{10,18... | collective-permute-start | bytes 1966088 | tf_op jit(solution)/shard_map/ppermute | solution.py:32
  5.6 25.1 %collective-permute-start.3 = (bf16[256,1280]{1,0:T(8,128)(2,1)}, bf16[256,1280]{1,0:T(8,128)(2,1)S(1)}, u32[]{:S(2)}, u32[]{:S(2)}) collective-permute-start(bf16[256,1280]{1,0:T(8,128)(2,1)} %v_ref.1), channel_id=1, source_target_pairs={{0,8},{4,12},{8,0},{12,4},{16,24},{20,28},{24,16},{28,20},{1,9},{5... | collective-permute-start | bytes 1966088 | tf_op jit(solution)/shard_map/ppermute | solution.py:32
  5.7 28.9 %collective-permute-start.4 = (bf16[256,1280]{1,0:T(8,128)(2,1)}, bf16[256,1280]{1,0:T(8,128)(2,1)S(1)}, u32[]{:S(2)}, u32[]{:S(2)}) collective-permute-start(bf16[256,1280]{1,0:T(8,128)(2,1)} %v_ref.1), channel_id=1, source_target_pairs={{8,16},{12,20},{16,8},{20,12},{9,17},{13,21},{17,9},{21,13},{10,18... | collective-permute-start | bytes 1966088 | tf_op jit(solution)/shard_map/ppermute | solution.py:32
  17.8 18.2 %collective-permute-start.5 = (bf16[256,1280]{1,0:T(8,128)(2,1)}, bf16[256,1280]{1,0:T(8,128)(2,1)S(1)}, u32[]{:S(2)}, u32[]{:S(2)}) collective-permute-start(bf16[256,1280]{1,0:T(8,128)(2,1)} %v_ref.1), channel_id=1, source_target_pairs={{0,4},{4,0},{8,12},{12,8},{16,20},{20,16},{24,28},{28,24},{1,5},{5... | collective-permute-start | bytes 1966088 | tf_op jit(solution)/shard_map/ppermute | solution.py:32
  21.4 24.5 %collective-permute-start.7 = (bf16[256,1280]{1,0:T(8,128)(2,1)S(1)}, bf16[256,1280]{1,0:T(8,128)(2,1)S(1)}, u32[]{:S(2)}, u32[]{:S(2)}) collective-permute-start(bf16[256,1280]{1,0:T(8,128)(2,1)S(1)} %collective-permute-done.1.rest_1_), channel_id=1, source_target_pairs={{8,0},{12,4},{16,24},{20,28},{9,1},{13,5},{17,25},{21,29},{10,2},{... | collective-permute-start | bytes 1966088 | tf_op jit(solution)/shard_map/ppermute | solution.py:32
  22.8 16.8 %copy-start.4 = (s32[4,32]{1,0:T(4,128)S(1)}, s32[4,32]{1,0:T(4,128)}, u32[]{:S(2)}) copy-start(s32[4,32]{1,0:T(4,128)} %live_ref.3) | copy-start | bytes 1540
  22.8 16.7 %copy-start.1 = (bf16[256,1280]{1,0:T(8,128)(2,1)S(1)}, bf16[256,1280]{1,0:T(8,128)(2,1)}, u32[]{:S(2)}) copy-start(bf16[256,1280]{1,0:T(8,128)(2,1)} %q_ref.3) | copy-start | bytes 1966084
  22.9 16.7 %copy-start.2 = (bf16[256,1280]{1,0:T(8,128)(2,1)S(1)}, bf16[256,1280]{1,0:T(8,128)(2,1)}, u32[]{:S(2)}) copy-start(bf16[256,1280]{1,0:T(8,128)(2,1)} %k_ref.1) | copy-start | bytes 1966084
  22.9 16.7 %copy-start.3 = (bf16[256,1280]{1,0:T(8,128)(2,1)S(1)}, bf16[256,1280]{1,0:T(8,128)(2,1)}, u32[]{:S(2)}) copy-start(bf16[256,1280]{1,0:T(8,128)(2,1)} %v_ref.1) | copy-start | bytes 1966084
  22.9 26.9 %collective-permute-start.8 = (bf16[256,1280]{1,0:T(8,128)(2,1)S(1)}, bf16[256,1280]{1,0:T(8,128)(2,1)S(1)}, u32[]{:S(2)}, u32[]{:S(2)}) collective-permute-start(bf16[256,1280]{1,0:T(8,128)(2,1)S(1)} %broadcast_select_fusion.1), channel_id=1, source_target_pairs={{0,4},{8,12},{12,8},{16,20},{20,16},{28,24},{1,5},{9,13},{13,9},{1... | collective-permute-start | bytes 1966088 | tf_op jit(solution)/shard_map/ppermute | solution.py:32
  30.7 19.1 %collective-permute-start.6 = (bf16[256,1280]{1,0:T(8,128)(2,1)S(1)}, bf16[256,1280]{1,0:T(8,128)(2,1)S(1)}, u32[]{:S(2)}, u32[]{:S(2)}) collective-permute-start(bf16[256,1280]{1,0:T(8,128)(2,1)S(1)} %collective-permute-done.rest_0_), channel_id=1, source_target_pairs={{8,16},{12,20},{16,8},{20,12},{9,17},{13,21},{17,9},{21,13},{10,18... | collective-permute-start | bytes 1966088 | tf_op jit(solution)/shard_map/ppermute | solution.py:32
  34.6 26.5 %collective-permute-start.11 = (bf16[256,1280]{1,0:T(8,128)(2,1)S(1)}, bf16[256,1280]{1,0:T(8,128)(2,1)S(1)}, u32[]{:S(2)}, u32[]{:S(2)}) collective-permute-start(bf16[256,1280]{1,0:T(8,128)(2,1)S(1)} %collective-permute-done.4.rest_4_), channel_id=1, source_target_pairs={{8,0},{12,4},{16,24},{20,28},{9,1},{13,5},{17,25},{21,29},{10,2},{... | collective-permute-start | bytes 1966088 | tf_op jit(solution)/shard_map/ppermute | solution.py:32
  36.0 24.6 %collective-permute-start.9 = (bf16[256,1280]{1,0:T(8,128)(2,1)S(1)}, bf16[256,1280]{1,0:T(8,128)(2,1)S(1)}, u32[]{:S(2)}, u32[]{:S(2)}) collective-permute-start(bf16[256,1280]{1,0:T(8,128)(2,1)S(1)} %broadcast_select_fusion), channel_id=1, source_target_pairs={{0,4},{8,12},{12,8},{16,20},{20,16},{28,24},{1,5},{9,13},{13,9},{1... | collective-permute-start | bytes 1966088 | tf_op jit(solution)/shard_map/ppermute | solution.py:32
  39.6 22.7 %copy-start = (bf16[1280,5120]{1,0:T(8,128)(2,1)S(1)}, bf16[1280,5120]{1,0:T(8,128)(2,1)}, u32[]{:S(2)}) copy-start(bf16[1280,5120]{1,0:T(8,128)(2,1)} %w_ref.5) | copy-start | bytes 39321604
  46.0 16.3 %collective-permute-start.10 = (bf16[256,1280]{1,0:T(8,128)(2,1)S(1)}, bf16[256,1280]{1,0:T(8,128)(2,1)S(1)}, u32[]{:S(2)}, u32[]{:S(2)}) collective-permute-start(bf16[256,1280]{1,0:T(8,128)(2,1)S(1)} %collective-permute-done.3.rest_3_), channel_id=1, source_target_pairs={{8,16},{12,20},{16,8},{20,12},{9,17},{13,21},{17,9},{21,13},{10,18... | collective-permute-start | bytes 1966088 | tf_op jit(solution)/shard_map/ppermute | solution.py:32
  63.4 1.7 %collective-permute-start.12 = (bf16[256,640]{1,0:T(8,128)(2,1)S(1)}, bf16[256,640]{1,0:T(8,128)(2,1)S(1)}, u32[]{:S(2)}, u32[]{:S(2)}) collective-permute-start(bf16[256,640]{1,0:T(8,128)(2,1)S(1)} %get-tuple-element.36), channel_id=1, source_target_pairs={{0,1},{1,0},{2,3},{3,2},{4,5},{5,4},{6,7},{7,6},{8,9},{9,8},{10,11... | collective-permute-start | bytes 983048 | tf_op jit(solution)/shard_map/ppermute | solution.py:32
  65.1 2.5 %collective-permute-start.13 = (bf16[256,640]{1,0:T(8,128)(2,1)S(1)}, bf16[256,640]{1,0:T(8,128)(2,1)S(1)}, u32[]{:S(2)}, u32[]{:S(2)}) collective-permute-start(bf16[256,640]{1,0:T(8,128)(2,1)S(1)} %get-tuple-element.39), channel_id=1, source_target_pairs={{0,1},{1,0},{2,3},{3,2},{4,5},{5,4},{6,7},{7,6},{8,9},{9,8},{10,11... | collective-permute-start | bytes 983048 | tf_op jit(solution)/shard_map/ppermute | solution.py:32
  65.3 10.5 %collective-permute-start.17 = (bf16[256,640]{1,0:T(8,128)(2,1)S(1)}, bf16[256,640]{1,0:T(8,128)(2,1)S(1)}, u32[]{:S(2)}, u32[]{:S(2)}) collective-permute-start(bf16[256,640]{1,0:T(8,128)(2,1)S(1)} %add_convert_fusion.2), channel_id=1, source_target_pairs={{0,2},{1,3},{2,0},{3,1},{4,6},{5,7},{6,4},{7,5},{8,10},{9,11},{10,... | collective-permute-start | bytes 983048 | tf_op jit(solution)/shard_map/ppermute | solution.py:32
  67.7 14.6 %collective-permute-start.18 = (bf16[256,640]{1,0:T(8,128)(2,1)S(1)}, bf16[256,640]{1,0:T(8,128)(2,1)S(1)}, u32[]{:S(2)}, u32[]{:S(2)}) collective-permute-start(bf16[256,640]{1,0:T(8,128)(2,1)S(1)} %add_convert_fusion.1), channel_id=1, source_target_pairs={{0,2},{1,3},{2,0},{3,1},{4,6},{5,7},{6,4},{7,5},{8,10},{9,11},{10,... | collective-permute-start | bytes 983048 | tf_op jit(solution)/shard_map/ppermute | solution.py:32
  70.4 5.4 %collective-permute-start.14 = (bf16[256,512]{1,0:T(8,128)(2,1)S(1)}, bf16[256,512]{1,0:T(8,128)(2,1)S(1)}, u32[]{:S(2)}, u32[]{:S(2)}) collective-permute-start(bf16[256,512]{1,0:T(8,128)(2,1)S(1)} %get-tuple-element.42), channel_id=1, source_target_pairs={{0,1},{1,0},{2,3},{3,2},{4,5},{5,4},{6,7},{7,6},{8,9},{9,8},{10,11... | collective-permute-start | bytes 786440 | tf_op jit(solution)/shard_map/ppermute | solution.py:32
  70.5 5.4 %collective-permute-start.15 = (bf16[256,512]{1,0:T(8,128)(2,1)S(1)}, bf16[256,512]{1,0:T(8,128)(2,1)S(1)}, u32[]{:S(2)}, u32[]{:S(2)}) collective-permute-start(bf16[256,512]{1,0:T(8,128)(2,1)S(1)} %get-tuple-element.43), channel_id=1, source_target_pairs={{0,1},{1,0},{2,3},{3,2},{4,5},{5,4},{6,7},{7,6},{8,9},{9,8},{10,11... | collective-permute-start | bytes 786440 | tf_op jit(solution)/shard_map/ppermute | solution.py:32
  71.0 4.9 %collective-permute-start.16 = (bf16[256,256]{1,0:T(8,128)(2,1)S(1)}, bf16[256,256]{1,0:T(8,128)(2,1)S(1)}, u32[]{:S(2)}, u32[]{:S(2)}) collective-permute-start(bf16[256,256]{1,0:T(8,128)(2,1)S(1)} %get-tuple-element.44), channel_id=1, source_target_pairs={{0,1},{1,0},{2,3},{3,2},{4,5},{5,4},{6,7},{7,6},{8,9},{9,8},{10,11... | collective-permute-start | bytes 393224 | tf_op jit(solution)/shard_map/ppermute | solution.py:32

commit v7 on v6

--- a/solution.py
+++ b/solution.py
@@ -355,26 +355,26 @@
     swap = lambda x, bit: send(x, "head", [(g, g ^ bit) for g in range(4)])
     add = lambda a, b: (a.astype(F32) + b.astype(F32)).astype(BF16)
     columns = out_weight.shape[1] // lax.axis_size("head")
-    cut = columns // 2
+    cut = 4 * HDIM
     rest = columns - cut
     scaled = second_place(scaled, weights, late_values[-1])
     sibling_a, attended = first_project(scaled, weights, late_values[:-1], out_weight, cut)
     sibling_b, mine_a = project(attended, out_weight, ((3, cut, rest),), ((2, 0, cut),))
     crossed_a = add(mine_a, swap(sibling_a, 1))
-    far_a = swap(crossed_a, 2)
+    fars = [swap(crossed_a, 2)]
     sibling_b = swap(after(sibling_b, crossed_a), 1)
     (mine_b,) = project(after(attended, crossed_a), out_weight, ((2, cut, rest),))
     crossed_b = add(mine_b, sibling_b)
-    far_b = swap(crossed_b, 2)
-    bounds = [0, 4 * HDIM, 8 * HDIM, columns]
+    cuts = [0, 3 * HDIM, rest]
+    fars += [swap(crossed_b[:, p:q], 2) for p, q in zip(cuts[:-1], cuts[1:])]
+    bounds = [0, 3 * HDIM, 6 * HDIM, 8 * HDIM, columns]
     *near, total = project(
         after(attended, crossed_b), out_weight,
         *(((1, p, q - p),) for p, q in zip(bounds[:-1], bounds[1:])), ((0, 0, columns),),
     )
     near = jnp.concatenate([swap(part, 1) for part in near], 1)
     total = total.astype(F32) + near.astype(F32)
-    far = jnp.concatenate([far_a, far_b], 1)
-    return (total + far.astype(F32)).astype(BF16)
+    return (total + jnp.concatenate(fars, 1).astype(F32)).astype(BF16)
 
 
 def solution(mesh):

time: 84.7 us -> 84.4 us (level)
  waiting for transfers between devices: 37.2 us -> 35.8 us
  starting transfers between devices: 28.8 us -> 30 us
    ppermute x19 -> x21, waiting for transfers between devices: 37.2 us -> 35.8 us  [send(): return lax.ppermute(x, axis, pairs)]
    ppermute x19 -> x21, starting transfers between devices: 28.8 us -> 30 us  [send(): return lax.ppermute(x, axis, pairs)]
  transfers between devices with their start and end apart: 19 -> 21, of which waited for: 8 -> 10; matrix products, arithmetic and copies ran while one was open for 0% -> 0% of each run, Pallas kernels for 18% -> 18%
where the time goes in v7:
time: 84.4 us; the launch traced here: 83.2 us
  waiting for transfers between devices  35.8 us (42%)
  starting transfers between devices  30 us (36%)
  Pallas kernels  15.6 us (18%)
  other arithmetic  1.4 us (2%)
    ppermute x21, waiting for transfers between devices, send(): return lax.ppermute(x, axis, pairs)  35.8 us
    ppermute x21, starting transfers between devices, send(): return lax.ppermute(x, axis, pairs)  30 us
    pallas_call x1, Pallas kernels, early_attention(): pl.pallas_call(functools.partial(early_kernel, count), out_shape=[jax.Sha...  6.33 us
    pallas_call x1, Pallas kernels, late_weights(): pl.pallas_call(late_kernel, out_shape=[jax.ShapeDtypeStruct((rows, heads...  3.97 us
    pallas_call x3, Pallas kernels, project(): pl.pallas_call(functools.partial(project_kernel, outputs), out_shape=[jax...  3.87 us
  transfers between devices with their start and end apart: 21, of which 10 were waited for; matrix products, arithmetic and copies ran while one was open for 0% of the time, Pallas kernels for 18%

profile of v7, /device:TPU:10, one launch (start us, length us, event | category | flops | bytes accessed | tf_op | source)
XLA Modules:
  0.0 83.2 jit_solution(17078813906846267172)
XLA Ops:
  0.5 5.0 %collective-permute-start.1 = (bf16[256,1280]{1,0:T(8,128)(2,1)}, bf16[256,1280]{1,0:T(8,128)(2,1)S(1)}, u32[]{:S(2)}, u32[]{:S(2)}) collective-permute-start(bf16[256,1280]{1,0:T(8,128)(2,1)} %k_ref.1), channel_id=1, source_target_pairs={{8,16},{12,20},{16,8},{20,12},{9,17},{13,21},{17,9},{21,13},{10,18... | collective-permute-start | bytes 1966088 | tf_op jit(solution)/shard_map/ppermute | solution.py:32
  5.7 1.9 %collective-permute-start.4 = (bf16[256,1280]{1,0:T(8,128)(2,1)}, bf16[256,1280]{1,0:T(8,128)(2,1)S(1)}, u32[]{:S(2)}, u32[]{:S(2)}) collective-permute-start(bf16[256,1280]{1,0:T(8,128)(2,1)} %v_ref.1), channel_id=1, source_target_pairs={{8,16},{12,20},{16,8},{20,12},{9,17},{13,21},{17,9},{21,13},{10,18... | collective-permute-start | bytes 1966088 | tf_op jit(solution)/shard_map/ppermute | solution.py:32
  7.6 10.2 %collective-permute-done.rest_0_ = bf16[256,1280]{1,0:T(8,128)(2,1)S(1)} collective-permute-done((bf16[256,1280]{1,0:T(8,128)(2,1)}, bf16[256,1280]{1,0:T(8,128)(2,1)S(1)}, u32[]{:S(2)}, u32[]{:S(2)}) %collective-permute-start) | collective-permute-done | bytes 655392 | tf_op jit(solution)/shard_map/ppermute | solution.py:32
  18.4 3.1 %collective-permute-done.1.rest_1_ = bf16[256,1280]{1,0:T(8,128)(2,1)S(1)} collective-permute-done((bf16[256,1280]{1,0:T(8,128)(2,1)}, bf16[256,1280]{1,0:T(8,128)(2,1)S(1)}, u32[]{:S(2)}, u32[]{:S(2)}) %collective-permute-start.1) | collective-permute-done | bytes 655392 | tf_op jit(solution)/shard_map/ppermute | solution.py:32
  21.4 1.3 %collective-permute-start.7 = (bf16[256,1280]{1,0:T(8,128)(2,1)S(1)}, bf16[256,1280]{1,0:T(8,128)(2,1)S(1)}, u32[]{:S(2)}, u32[]{:S(2)}) collective-permute-start(bf16[256,1280]{1,0:T(8,128)(2,1)S(1)} %collective-permute-done.1.rest_1_), channel_id=1, source_target_pairs={{8,0},{12,4},{16,24},{20,28},{9,1},{13,5},{17,25},{21,29},{10,2},{... | collective-permute-start | bytes 1966088 | tf_op jit(solution)/shard_map/ppermute | solution.py:32
  22.9 3.5 %collective-permute-start.8 = (bf16[256,1280]{1,0:T(8,128)(2,1)S(1)}, bf16[256,1280]{1,0:T(8,128)(2,1)S(1)}, u32[]{:S(2)}, u32[]{:S(2)}) collective-permute-start(bf16[256,1280]{1,0:T(8,128)(2,1)S(1)} %broadcast_select_fusion.1), channel_id=1, source_target_pairs={{0,4},{8,12},{12,8},{16,20},{20,16},{28,24},{1,5},{9,13},{13,9},{1... | collective-permute-start | bytes 1966088 | tf_op jit(solution)/shard_map/ppermute | solution.py:32
  26.4 4.3 %collective-permute-done.3.rest_3_ = bf16[256,1280]{1,0:T(8,128)(2,1)S(1)} collective-permute-done((bf16[256,1280]{1,0:T(8,128)(2,1)}, bf16[256,1280]{1,0:T(8,128)(2,1)S(1)}, u32[]{:S(2)}, u32[]{:S(2)}) %collective-permute-start.3) | collective-permute-done | bytes 655392 | tf_op jit(solution)/shard_map/ppermute | solution.py:32
  30.7 3.8 %collective-permute-start.6 = (bf16[256,1280]{1,0:T(8,128)(2,1)S(1)}, bf16[256,1280]{1,0:T(8,128)(2,1)S(1)}, u32[]{:S(2)}, u32[]{:S(2)}) collective-permute-start(bf16[256,1280]{1,0:T(8,128)(2,1)S(1)} %collective-permute-done.rest_0_), channel_id=1, source_target_pairs={{8,16},{12,20},{16,8},{20,12},{9,17},{13,21},{17,9},{21,13},{10,18... | collective-permute-start | bytes 1966088 | tf_op jit(solution)/shard_map/ppermute | solution.py:32
  34.6 1.3 %collective-permute-start.11 = (bf16[256,1280]{1,0:T(8,128)(2,1)S(1)}, bf16[256,1280]{1,0:T(8,128)(2,1)S(1)}, u32[]{:S(2)}, u32[]{:S(2)}) collective-permute-start(bf16[256,1280]{1,0:T(8,128)(2,1)S(1)} %collective-permute-done.4.rest_4_), channel_id=1, source_target_pairs={{8,0},{12,4},{16,24},{20,28},{9,1},{13,5},{17,25},{21,29},{10,2},{... | collective-permute-start | bytes 1966088 | tf_op jit(solution)/shard_map/ppermute | solution.py:32
  36.0 3.6 %collective-permute-start.9 = (bf16[256,1280]{1,0:T(8,128)(2,1)S(1)}, bf16[256,1280]{1,0:T(8,128)(2,1)S(1)}, u32[]{:S(2)}, u32[]{:S(2)}) collective-permute-start(bf16[256,1280]{1,0:T(8,128)(2,1)S(1)} %broadcast_select_fusion), channel_id=1, source_target_pairs={{0,4},{8,12},{12,8},{16,20},{20,16},{28,24},{1,5},{9,13},{13,9},{1... | collective-permute-start | bytes 1966088 | tf_op jit(solution)/shard_map/ppermute | solution.py:32
  39.6 6.3 %early_attention.1 = (f32[256,1280]{1,0:T(8,128)S(1)}, f32[256,1280]{1,0:T(8,128)S(1)}, f32[256,1280]{1,0:T(8,128)S(1)}) custom-call(s32[4,32]{1,0:T(4,128)S(1)} %copy-done.4, bf16[256,1280]{1,0:T(8,128)(2,1)S(1)} %copy-done.1, bf16[256,1280]{1,0:T(8,128)(2,1)S(1)} %copy-done.2, bf16[256,1280]{1,0:T(8,128)(2,1)S(1)} %copy-done.3, ...), custom_call_target="tpu_custom_call" | custom-call | tf_op jit(solution)/shard_map/early_attention/pallas_call | solution.py:170
  46.0 3.8 %collective-permute-start.10 = (bf16[256,1280]{1,0:T(8,128)(2,1)S(1)}, bf16[256,1280]{1,0:T(8,128)(2,1)S(1)}, u32[]{:S(2)}, u32[]{:S(2)}) collective-permute-start(bf16[256,1280]{1,0:T(8,128)(2,1)S(1)} %collective-permute-done.3.rest_3_), channel_id=1, source_target_pairs={{8,16},{12,20},{16,8},{20,12},{9,17},{13,21},{17,9},{21,13},{10,18... | collective-permute-start | bytes 1966088 | tf_op jit(solution)/shard_map/ppermute | solution.py:32
  49.8 4.0 %late_weights.1 = (bf16[256,5120]{1,0:T(8,128)(2,1)S(1)}, f32[256,1280]{1,0:T(8,128)S(1)}) custom-call(s32[4,32]{1,0:T(4,128)S(1)} %copy-done.4, bf16[256,1280]{1,0:T(8,128)(2,1)S(1)} %copy-done.1, f32[256,1280]{1,0:T(8,128)S(1)} %get-tuple-element.27.sum_ref, f32[256,1280]{1,0:T(8,128)S(1)} %get-tuple-element.28.peak_ref, ...), custom_call_target="tpu_custom_call" | custom-call | tf_op jit(solution)/shard_map/late_weights/pallas_call | solution.py:225
  53.8 6.8 %collective-permute-done.9.value_ref = bf16[256,1280]{1,0:T(8,128)(2,1)S(1)} collective-permute-done((bf16[256,1280]{1,0:T(8,128)(2,1)S(1)}, bf16[256,1280]{1,0:T(8,128)(2,1)S(1)}, u32[]{:S(2)}, u32[]{:S(2)}) %collective-permute-start.9) | collective-permute-done | bytes 655392 | tf_op jit(solution)/shard_map/ppermute | solution.py:32
  61.1 1.2 %collective-permute-done.10.rest_0_ = bf16[256,1280]{1,0:T(8,128)(2,1)S(1)} collective-permute-done((bf16[256,1280]{1,0:T(8,128)(2,1)S(1)}, bf16[256,1280]{1,0:T(8,128)(2,1)S(1)}, u32[]{:S(2)}, u32[]{:S(2)}) %collective-permute-start.10) | collective-permute-done | bytes 655392 | tf_op jit(solution)/shard_map/ppermute | solution.py:32
  63.2 1.1 %project.3 = (bf16[256,768]{1,0:T(8,128)(2,1)S(1)}, bf16[256,512]{1,0:T(8,128)(2,1)S(1)}) custom-call(bf16[256,1280]{1,0:T(8,128)(2,1)S(1)} %get-tuple-element.41.a_ref, bf16[1280,5120]{1,0:T(8,128)(2,1)S(1)} %copy-done), custom_call_target="tpu_custom_call" | custom-call | tf_op jit(solution)/shard_map/project/pallas_call | solution.py:318
  65.0 1.5 %collective-permute-start.18 = (bf16[256,512]{1,0:T(8,128)(2,1)S(1)}, bf16[256,512]{1,0:T(8,128)(2,1)S(1)}, u32[]{:S(2)}, u32[]{:S(2)}) collective-permute-start(bf16[256,512]{1,0:T(8,128)(2,1)S(1)} %add_convert_fusion.2), channel_id=1, source_target_pairs={{0,2},{1,3},{2,0},{3,1},{4,6},{5,7},{6,4},{7,5},{8,10},{9,11},{10,... | collective-permute-start | bytes 786440 | tf_op jit(solution)/shard_map/ppermute | solution.py:32
  67.4 2.1 %project.5 = (bf16[256,384]{1,0:T(8,128)(2,1)S(1)}, bf16[256,384]{1,0:T(8,128)(2,1)S(1)}, bf16[256,256]{1,0:T(8,128)(2,1)S(1)}, bf16[256,256]{1,0:T(8,128)(2,1)S(1)}, bf16[256,1280]{1,0:T(8,128)(2,1)S(1)}) custom-call(bf16[256,1280]{1,0:T(8,128)(2,1)S(1)} %get-tuple-element.41.a_ref, bf16[1280,5120]{1,0:T(8,128)(2,1)S(1)} %copy-done), custom_call_target="tpu_custom_call" | custom-call | tf_op jit(solution)/shard_map/project/pallas_call | solution.py:318
  70.7 1.1 %collective-permute-start.20 = (bf16[256,384]{1,0:T(8,128)(2,1)S(1)}, bf16[256,384]{1,0:T(8,128)(2,1)S(1)}, u32[]{:S(2)}, u32[]{:S(2)}) collective-permute-start(bf16[256,384]{1,0:T(8,128)(2,1)S(1)} %get-tuple-element.48), channel_id=1, source_target_pairs={{0,2},{1,3},{2,0},{3,1},{4,6},{5,7},{6,4},{7,5},{8,10},{9,11},{10,... | collective-permute-start | bytes 589832 | tf_op jit(solution)/shard_map/ppermute | solution.py:32
  71.8 2.4 %collective-permute-done.18 = bf16[256,512]{1,0:T(8,128)(2,1)S(1)} collective-permute-done((bf16[256,512]{1,0:T(8,128)(2,1)S(1)}, bf16[256,512]{1,0:T(8,128)(2,1)S(1)}, u32[]{:S(2)}, u32[]{:S(2)}) %collective-permute-start.18) | collective-permute-done | bytes 262176 | tf_op jit(solution)/shard_map/ppermute | solution.py:32
  74.7 1.1 %collective-permute-done.17 = bf16[256,256]{1,0:T(8,128)(2,1)S(1)} collective-permute-done((bf16[256,256]{1,0:T(8,128)(2,1)S(1)}, bf16[256,256]{1,0:T(8,128)(2,1)S(1)}, u32[]{:S(2)}, u32[]{:S(2)}) %collective-permute-start.17) | collective-permute-done | bytes 131104 | tf_op jit(solution)/shard_map/ppermute | solution.py:32
  75.8 2.6 %collective-permute-done.19 = bf16[256,384]{1,0:T(8,128)(2,1)S(1)} collective-permute-done((bf16[256,384]{1,0:T(8,128)(2,1)S(1)}, bf16[256,384]{1,0:T(8,128)(2,1)S(1)}, u32[]{:S(2)}, u32[]{:S(2)}) %collective-permute-start.19) | collective-permute-done | bytes 196640 | tf_op jit(solution)/shard_map/ppermute | solution.py:32
  78.4 3.7 %collective-permute-done.20 = bf16[256,384]{1,0:T(8,128)(2,1)S(1)} collective-permute-done((bf16[256,384]{1,0:T(8,128)(2,1)S(1)}, bf16[256,384]{1,0:T(8,128)(2,1)S(1)}, u32[]{:S(2)}, u32[]{:S(2)}) %collective-permute-start.20) | collective-permute-done | bytes 196640 | tf_op jit(solution)/shard_map/ppermute | solution.py:32
  82.1 1.1 %add_convert_fusion = bf16[256,1280]{1,0:T(8,128)(2,1)} fusion(bf16[256,1280]{1,0:T(8,128)(2,1)S(1)} %get-tuple-element.42, bf16[256,256]{1,0:T(8,128)(2,1)S(1)} %collective-permute-done.17, bf16[256,256]{1,0:T(8,128)(2,1)S(1)} %collective-permute-done.16, bf16[256,384]{1,0:T(8,128)(2,1)S(1)} %collective-permute-done.15, ...), kind=kLoop, calls=%fused_computation | loop fusion | flops 5898240 | bytes 2621440 | tf_op jit(solution)/shard_map/convert_element_type | solution.py:377
  (41 shorter events, 6.0 us)
Async XLA Ops:
  0.0 17.8 %collective-permute-start = (bf16[256,1280]{1,0:T(8,128)(2,1)}, bf16[256,1280]{1,0:T(8,128)(2,1)S(1)}, u32[]{:S(2)}, u32[]{:S(2)}) collective-permute-start(bf16[256,1280]{1,0:T(8,128)(2,1)} %k_ref.1), channel_id=1, source_target_pairs={{0,8},{4,12},{8,0},{12,4},{16,24},{20,28},{24,16},{28,20},{1,9},{5... | collective-permute-start | bytes 1966088 | tf_op jit(solution)/shard_map/ppermute | solution.py:32
  0.5 17.4 %collective-permute-start.2 = (bf16[256,1280]{1,0:T(8,128)(2,1)}, bf16[256,1280]{1,0:T(8,128)(2,1)S(1)}, u32[]{:S(2)}, u32[]{:S(2)}) collective-permute-start(bf16[256,1280]{1,0:T(8,128)(2,1)} %k_ref.1), channel_id=1, source_target_pairs={{0,4},{4,0},{8,12},{12,8},{16,20},{20,16},{24,28},{28,24},{1,5},{5... | collective-permute-start | bytes 1966088 | tf_op jit(solution)/shard_map/ppermute | solution.py:32
  0.5 20.9 %collective-permute-start.1 = (bf16[256,1280]{1,0:T(8,128)(2,1)}, bf16[256,1280]{1,0:T(8,128)(2,1)S(1)}, u32[]{:S(2)}, u32[]{:S(2)}) collective-permute-start(bf16[256,1280]{1,0:T(8,128)(2,1)} %k_ref.1), channel_id=1, source_target_pairs={{8,16},{12,20},{16,8},{20,12},{9,17},{13,21},{17,9},{21,13},{10,18... | collective-permute-start | bytes 1966088 | tf_op jit(solution)/shard_map/ppermute | solution.py:32
  5.6 25.1 %collective-permute-start.3 = (bf16[256,1280]{1,0:T(8,128)(2,1)}, bf16[256,1280]{1,0:T(8,128)(2,1)S(1)}, u32[]{:S(2)}, u32[]{:S(2)}) collective-permute-start(bf16[256,1280]{1,0:T(8,128)(2,1)} %v_ref.1), channel_id=1, source_target_pairs={{0,8},{4,12},{8,0},{12,4},{16,24},{20,28},{24,16},{28,20},{1,9},{5... | collective-permute-start | bytes 1966088 | tf_op jit(solution)/shard_map/ppermute | solution.py:32
  5.7 28.9 %collective-permute-start.4 = (bf16[256,1280]{1,0:T(8,128)(2,1)}, bf16[256,1280]{1,0:T(8,128)(2,1)S(1)}, u32[]{:S(2)}, u32[]{:S(2)}) collective-permute-start(bf16[256,1280]{1,0:T(8,128)(2,1)} %v_ref.1), channel_id=1, source_target_pairs={{8,16},{12,20},{16,8},{20,12},{9,17},{13,21},{17,9},{21,13},{10,18... | collective-permute-start | bytes 1966088 | tf_op jit(solution)/shard_map/ppermute | solution.py:32
  17.8 18.2 %collective-permute-start.5 = (bf16[256,1280]{1,0:T(8,128)(2,1)}, bf16[256,1280]{1,0:T(8,128)(2,1)S(1)}, u32[]{:S(2)}, u32[]{:S(2)}) collective-permute-start(bf16[256,1280]{1,0:T(8,128)(2,1)} %v_ref.1), channel_id=1, source_target_pairs={{0,4},{4,0},{8,12},{12,8},{16,20},{20,16},{24,28},{28,24},{1,5},{5... | collective-permute-start | bytes 1966088 | tf_op jit(solution)/shard_map/ppermute | solution.py:32
  21.4 24.5 %collective-permute-start.7 = (bf16[256,1280]{1,0:T(8,128)(2,1)S(1)}, bf16[256,1280]{1,0:T(8,128)(2,1)S(1)}, u32[]{:S(2)}, u32[]{:S(2)}) collective-permute-start(bf16[256,1280]{1,0:T(8,128)(2,1)S(1)} %collective-permute-done.1.rest_1_), channel_id=1, source_target_pairs={{8,0},{12,4},{16,24},{20,28},{9,1},{13,5},{17,25},{21,29},{10,2},{... | collective-permute-start | bytes 1966088 | tf_op jit(solution)/shard_map/ppermute | solution.py:32
  22.8 16.8 %copy-start.4 = (s32[4,32]{1,0:T(4,128)S(1)}, s32[4,32]{1,0:T(4,128)}, u32[]{:S(2)}) copy-start(s32[4,32]{1,0:T(4,128)} %live_ref.3) | copy-start | bytes 1540
  22.8 16.7 %copy-start.1 = (bf16[256,1280]{1,0:T(8,128)(2,1)S(1)}, bf16[256,1280]{1,0:T(8,128)(2,1)}, u32[]{:S(2)}) copy-start(bf16[256,1280]{1,0:T(8,128)(2,1)} %q_ref.3) | copy-start | bytes 1966084
  22.9 26.9 %collective-permute-start.8 = (bf16[256,1280]{1,0:T(8,128)(2,1)S(1)}, bf16[256,1280]{1,0:T(8,128)(2,1)S(1)}, u32[]{:S(2)}, u32[]{:S(2)}) collective-permute-start(bf16[256,1280]{1,0:T(8,128)(2,1)S(1)} %broadcast_select_fusion.1), channel_id=1, source_target_pairs={{0,4},{8,12},{12,8},{16,20},{20,16},{28,24},{1,5},{9,13},{13,9},{1... | collective-permute-start | bytes 1966088 | tf_op jit(solution)/shard_map/ppermute | solution.py:32
  30.7 19.1 %collective-permute-start.6 = (bf16[256,1280]{1,0:T(8,128)(2,1)S(1)}, bf16[256,1280]{1,0:T(8,128)(2,1)S(1)}, u32[]{:S(2)}, u32[]{:S(2)}) collective-permute-start(bf16[256,1280]{1,0:T(8,128)(2,1)S(1)} %collective-permute-done.rest_0_), channel_id=1, source_target_pairs={{8,16},{12,20},{16,8},{20,12},{9,17},{13,21},{17,9},{21,13},{10,18... | collective-permute-start | bytes 1966088 | tf_op jit(solution)/shard_map/ppermute | solution.py:32
  34.6 26.5 %collective-permute-start.11 = (bf16[256,1280]{1,0:T(8,128)(2,1)S(1)}, bf16[256,1280]{1,0:T(8,128)(2,1)S(1)}, u32[]{:S(2)}, u32[]{:S(2)}) collective-permute-start(bf16[256,1280]{1,0:T(8,128)(2,1)S(1)} %collective-permute-done.4.rest_4_), channel_id=1, source_target_pairs={{8,0},{12,4},{16,24},{20,28},{9,1},{13,5},{17,25},{21,29},{10,2},{... | collective-permute-start | bytes 1966088 | tf_op jit(solution)/shard_map/ppermute | solution.py:32
  36.0 24.6 %collective-permute-start.9 = (bf16[256,1280]{1,0:T(8,128)(2,1)S(1)}, bf16[256,1280]{1,0:T(8,128)(2,1)S(1)}, u32[]{:S(2)}, u32[]{:S(2)}) collective-permute-start(bf16[256,1280]{1,0:T(8,128)(2,1)S(1)} %broadcast_select_fusion), channel_id=1, source_target_pairs={{0,4},{8,12},{12,8},{16,20},{20,16},{28,24},{1,5},{9,13},{13,9},{1... | collective-permute-start | bytes 1966088 | tf_op jit(solution)/shard_map/ppermute | solution.py:32
  39.6 22.7 %copy-start = (bf16[1280,5120]{1,0:T(8,128)(2,1)S(1)}, bf16[1280,5120]{1,0:T(8,128)(2,1)}, u32[]{:S(2)}) copy-start(bf16[1280,5120]{1,0:T(8,128)(2,1)} %w_ref.5) | copy-start | bytes 39321604
  46.0 16.3 %collective-permute-start.10 = (bf16[256,1280]{1,0:T(8,128)(2,1)S(1)}, bf16[256,1280]{1,0:T(8,128)(2,1)S(1)}, u32[]{:S(2)}, u32[]{:S(2)}) collective-permute-start(bf16[256,1280]{1,0:T(8,128)(2,1)S(1)} %collective-permute-done.3.rest_3_), channel_id=1, source_target_pairs={{8,16},{12,20},{16,8},{20,12},{9,17},{13,21},{17,9},{21,13},{10,18... | collective-permute-start | bytes 1966088 | tf_op jit(solution)/shard_map/ppermute | solution.py:32
  63.2 1.6 %collective-permute-start.12 = (bf16[256,512]{1,0:T(8,128)(2,1)S(1)}, bf16[256,512]{1,0:T(8,128)(2,1)S(1)}, u32[]{:S(2)}, u32[]{:S(2)}) collective-permute-start(bf16[256,512]{1,0:T(8,128)(2,1)S(1)} %get-tuple-element.37), channel_id=1, source_target_pairs={{0,1},{1,0},{2,3},{3,2},{4,5},{5,4},{6,7},{7,6},{8,9},{9,8},{10,11... | collective-permute-start | bytes 786440 | tf_op jit(solution)/shard_map/ppermute | solution.py:32
  64.8 2.4 %collective-permute-start.13 = (bf16[256,768]{1,0:T(8,128)(2,1)S(1)}, bf16[256,768]{1,0:T(8,128)(2,1)S(1)}, u32[]{:S(2)}, u32[]{:S(2)}) collective-permute-start(bf16[256,768]{1,0:T(8,128)(2,1)S(1)} %get-tuple-element.40), channel_id=1, source_target_pairs={{0,1},{1,0},{2,3},{3,2},{4,5},{5,4},{6,7},{7,6},{8,9},{9,8},{10,11... | collective-permute-start | bytes 1179656 | tf_op jit(solution)/shard_map/ppermute | solution.py:32
  65.0 9.1 %collective-permute-start.18 = (bf16[256,512]{1,0:T(8,128)(2,1)S(1)}, bf16[256,512]{1,0:T(8,128)(2,1)S(1)}, u32[]{:S(2)}, u32[]{:S(2)}) collective-permute-start(bf16[256,512]{1,0:T(8,128)(2,1)S(1)} %add_convert_fusion.2), channel_id=1, source_target_pairs={{0,2},{1,3},{2,0},{3,1},{4,6},{5,7},{6,4},{7,5},{8,10},{9,11},{10,... | collective-permute-start | bytes 786440 | tf_op jit(solution)/shard_map/ppermute | solution.py:32
  69.5 4.7 %collective-permute-start.16 = (bf16[256,256]{1,0:T(8,128)(2,1)S(1)}, bf16[256,256]{1,0:T(8,128)(2,1)S(1)}, u32[]{:S(2)}, u32[]{:S(2)}) collective-permute-start(bf16[256,256]{1,0:T(8,128)(2,1)S(1)} %get-tuple-element.45), channel_id=1, source_target_pairs={{0,1},{1,0},{2,3},{3,2},{4,5},{5,4},{6,7},{7,6},{8,9},{9,8},{10,11... | collective-permute-start | bytes 393224 | tf_op jit(solution)/shard_map/ppermute | solution.py:32
  69.7 8.7 %collective-permute-start.19 = (bf16[256,384]{1,0:T(8,128)(2,1)S(1)}, bf16[256,384]{1,0:T(8,128)(2,1)S(1)}, u32[]{:S(2)}, u32[]{:S(2)}) collective-permute-start(bf16[256,384]{1,0:T(8,128)(2,1)S(1)} %get-tuple-element.47), channel_id=1, source_target_pairs={{0,2},{1,3},{2,0},{3,1},{4,6},{5,7},{6,4},{7,5},{8,10},{9,11},{10,... | collective-permute-start | bytes 589832 | tf_op jit(solution)/shard_map/ppermute | solution.py:32
  70.7 11.3 %collective-permute-start.20 = (bf16[256,384]{1,0:T(8,128)(2,1)S(1)}, bf16[256,384]{1,0:T(8,128)(2,1)S(1)}, u32[]{:S(2)}, u32[]{:S(2)}) collective-permute-start(bf16[256,384]{1,0:T(8,128)(2,1)S(1)} %get-tuple-element.48), channel_id=1, source_target_pairs={{0,2},{1,3},{2,0},{3,1},{4,6},{5,7},{6,4},{7,5},{8,10},{9,11},{10,... | collective-permute-start | bytes 589832 | tf_op jit(solution)/shard_map/ppermute | solution.py:32
  71.8 10.3 %collective-permute-start.14 = (bf16[256,384]{1,0:T(8,128)(2,1)S(1)}, bf16[256,384]{1,0:T(8,128)(2,1)S(1)}, u32[]{:S(2)}, u32[]{:S(2)}) collective-permute-start(bf16[256,384]{1,0:T(8,128)(2,1)S(1)} %get-tuple-element.43), channel_id=1, source_target_pairs={{0,1},{1,0},{2,3},{3,2},{4,5},{5,4},{6,7},{7,6},{8,9},{9,8},{10,11... | collective-permute-start | bytes 589832 | tf_op jit(solution)/shard_map/ppermute | solution.py:32
  74.2 7.9 %collective-permute-start.15 = (bf16[256,384]{1,0:T(8,128)(2,1)S(1)}, bf16[256,384]{1,0:T(8,128)(2,1)S(1)}, u32[]{:S(2)}, u32[]{:S(2)}) collective-permute-start(bf16[256,384]{1,0:T(8,128)(2,1)S(1)} %get-tuple-element.44), channel_id=1, source_target_pairs={{0,1},{1,0},{2,3},{3,2},{4,5},{5,4},{6,7},{7,6},{8,9},{9,8},{10,11... | collective-permute-start | bytes 589832 | tf_op jit(solution)/shard_map/ppermute | solution.py:32
  74.2 1.6 %collective-permute-start.17 = (bf16[256,256]{1,0:T(8,128)(2,1)S(1)}, bf16[256,256]{1,0:T(8,128)(2,1)S(1)}, u32[]{:S(2)}, u32[]{:S(2)}) collective-permute-start(bf16[256,256]{1,0:T(8,128)(2,1)S(1)} %get-tuple-element.46), channel_id=1, source_target_pairs={{0,1},{1,0},{2,3},{3,2},{4,5},{5,4},{6,7},{7,6},{8,9},{9,8},{10,11... | collective-permute-start | bytes 393224 | tf_op jit(solution)/shard_map/ppermute | solution.py:32
  (2 other events, 33.4 us)
